TPU v7x, 512 devices: a whole 4x4x16 slice. The times are simulated.
512 devices in a mesh: wide: 128 (over y, z, core), narrow: 4 (over x).
Axes of the slice: x: 4, y: 4, z: 16, core: 2. Of those that a mesh axis runs over, the one named last changes fastest.
Arguments:
- node_factors: float32 [524288, 512], P(('wide', 'narrow')), may hold values from -0.25 to 0.25
- leaf_q: float32 [262144, 512], P(('wide', 'narrow')), may hold values from -0.25 to 0.25
- modal_basis: float32 [512, 64], replicated, may hold values from -6 to 6
Outputs:
- trunk_modes: float32 [262144, 64], P(('wide', 'narrow'))
All inputs are finite; a program needn't handle non-finite values.
Results may differ from a plain program's by a relative error of at most 0.0002.
Values sent between devices are 32-bit elements; how exact they have to be, the bound alone decides.
No kernel may reach another device: no remote copies, remote signals or barrier semaphores. Data moves between devices by JAX's collectives and lax.ppermute only.
A program may use at most 64 MiB of HBM per device.

v0:
```python
import jax
import jax.numpy as jnp
from jax import lax
from jax.sharding import PartitionSpec as P


def from_behind(block, axis, distance):
    devices = range(lax.axis_size(axis))
    route = [(i - distance, i) for i in devices if i - distance in devices]
    return lax.ppermute(block, axis, route)


def apply_node(factor, coefficient):
    return jnp.dot(
        factor, coefficient, precision=lax.Precision.HIGHEST, preferred_element_type=jnp.float32
    )


def on_device(node_factors, leaf_q, modal_basis):
    narrow_count = lax.axis_size("narrow")
    leaf_count = lax.axis_size("wide") * narrow_count
    levels = leaf_count.bit_length() - 1
    leaf_index = lax.axis_index("wide") * narrow_count + lax.axis_index("narrow")
    snaps = node_factors.shape[1]
    coefficient = modal_basis
    for level in range(levels, 0, -1):
        offset = 2 ** (level - 1)
        position = leaf_index % (2 * offset)
        is_owner = position == offset
        is_holder = position == 0
        arrived = from_behind(coefficient, ("wide", "narrow"), offset)
        operand = jnp.where(is_owner, arrived, coefficient)
        product = apply_node(node_factors, operand)
        returned = from_behind(product[:snaps], ("wide", "narrow"), -offset)
        coefficient = jnp.where(
            is_holder, returned, jnp.where(is_owner, product[snaps:], coefficient)
        )
    return jnp.dot(
        leaf_q, coefficient, precision=lax.Precision.HIGHEST, preferred_element_type=jnp.float32
    )


def solution(mesh):
    return jax.shard_map(
        on_device,
        mesh=mesh,
        in_specs=(P(("wide", "narrow"), None), P(("wide", "narrow"), None), P()),
        out_specs=P(("wide", "narrow"), None),
        check_vma=False,
    )
```

profile of v0, /device:TPU:24, one launch (start us, length us, event | category | flops | bytes accessed | tf_op | source)
XLA Modules:
  0.0 209.0 jit_solution(13712246893108508744)
XLA Ops:
  0.0 1.4 collective-permute-start
  1.4 7.5 %collective-permute-done = f32[512,64]{0,1:T(8,128)S(1)} collective-permute-done((f32[512,64]{0,1:T(8,128)}, f32[512,64]{0,1:T(8,128)S(1)}, u32[]{:S(2)}, u32[]{:S(2)}) %collective-permute-start) | collective-permute-done | bytes 131104 | tf_op jit(solution)/shard_map/ppermute | solution.py:10
  9.0 3.0 %convolution_bitcast_fusion.8 = f32[1024,64]{0,1:T(8,128)S(1)} fusion(f32[1024,512]{1,0:T(8,128)S(1)} %copy-done, f32[512,64]{0,1:T(8,128)S(1)} %collective-permute-done, f32[512,64]{0,1:T(8,128)} %param.5, pred[]{:T(512)S(6)} %eq.81), kind=kOutput, calls=%fused_computation.8 | convolution fusion | flops 402685952 | bytes 2621441 | tf_op jit(solution)/shard_map/dot_general | solution.py:14
  12.0 1.6 collective-permute-start.1
  13.6 2.5 %collective-permute-done.1 = f32[512,64]{0,1:T(8,128)S(1)} collective-permute-done((f32[512,64]{0,1:T(8,128)S(1)}, f32[512,64]{0,1:T(8,128)S(1)}, u32[]{:S(2)}, u32[]{:S(2)}) %collective-permute-start.1) | collective-permute-done | bytes 131104 | tf_op jit(solution)/shard_map/ppermute | solution.py:10
  16.1 1.3 collective-permute-start.2
  17.4 5.6 %collective-permute-done.2 = f32[512,64]{0,1:T(8,128)S(1)} collective-permute-done((f32[512,64]{0,1:T(8,128)S(1)}, f32[512,64]{0,1:T(8,128)S(1)}, u32[]{:S(2)}, u32[]{:S(2)}) %collective-permute-start.2) | collective-permute-done | bytes 131104 | tf_op jit(solution)/shard_map/ppermute | solution.py:10
  23.0 2.1 %convolution_bitcast_fusion.7 = f32[1024,64]{0,1:T(8,128)S(1)} fusion(f32[1024,512]{1,0:T(8,128)S(1)} %copy-done, f32[512,64]{0,1:T(8,128)S(1)} %collective-permute-done.2, f32[512,64]{0,1:T(8,128)S(1)} %fusion.9, pred[]{:T(512)S(6)} %eq.79), kind=kOutput, calls=%fused_computation.7 | convolution fusion | flops 402685952 | bytes 2621441 | tf_op jit(solution)/shard_map/dot_general | solution.py:14
  25.2 3.9 %collective-permute-start.3 = (f32[512,64]{0,1:T(8,128)S(1)}, f32[512,64]{0,1:T(8,128)S(1)}, u32[]{:S(2)}, u32[]{:S(2)}) collective-permute-start(f32[512,64]{0,1:T(8,128)S(1)} %slice.74), channel_id=1, source_target_pairs={{128,0},{129,1},{130,2},{131,3},{132,4},{133,5},{134,6},{135,7},{1... | collective-permute-start | bytes 393224 | tf_op jit(solution)/shard_map/ppermute | solution.py:10
  29.1 2.5 %collective-permute-done.3 = f32[512,64]{0,1:T(8,128)S(1)} collective-permute-done((f32[512,64]{0,1:T(8,128)S(1)}, f32[512,64]{0,1:T(8,128)S(1)}, u32[]{:S(2)}, u32[]{:S(2)}) %collective-permute-start.3) | collective-permute-done | bytes 131104 | tf_op jit(solution)/shard_map/ppermute | solution.py:10
  31.7 15.5 %collective-permute-start.4 = (f32[512,64]{0,1:T(8,128)S(1)}, f32[512,64]{0,1:T(8,128)S(1)}, u32[]{:S(2)}, u32[]{:S(2)}) collective-permute-start(f32[512,64]{0,1:T(8,128)S(1)} %fusion.8), channel_id=1, source_target_pairs={{0,64},{1,65},{2,66},{3,67},{4,68},{5,69},{6,70},{7,71},{8,72},{9,... | collective-permute-start | bytes 393224 | tf_op jit(solution)/shard_map/ppermute | solution.py:10
  47.2 8.6 %collective-permute-done.4 = f32[512,64]{0,1:T(8,128)S(1)} collective-permute-done((f32[512,64]{0,1:T(8,128)S(1)}, f32[512,64]{0,1:T(8,128)S(1)}, u32[]{:S(2)}, u32[]{:S(2)}) %collective-permute-start.4) | collective-permute-done | bytes 131104 | tf_op jit(solution)/shard_map/ppermute | solution.py:10
  55.8 2.1 %convolution_bitcast_fusion.6 = f32[1024,64]{0,1:T(8,128)S(1)} fusion(f32[1024,512]{1,0:T(8,128)S(1)} %copy-done, f32[512,64]{0,1:T(8,128)S(1)} %collective-permute-done.4, f32[512,64]{0,1:T(8,128)S(1)} %fusion.8, pred[]{:T(512)S(6)} %eq.77), kind=kOutput, calls=%fused_computation.6 | convolution fusion | flops 402685952 | bytes 2621441 | tf_op jit(solution)/shard_map/dot_general | solution.py:14
  58.0 11.0 %collective-permute-start.5 = (f32[512,64]{0,1:T(8,128)S(1)}, f32[512,64]{0,1:T(8,128)S(1)}, u32[]{:S(2)}, u32[]{:S(2)}) collective-permute-start(f32[512,64]{0,1:T(8,128)S(1)} %slice.76), channel_id=1, source_target_pairs={{64,0},{65,1},{66,2},{67,3},{68,4},{69,5},{70,6},{71,7},{72,8},{73... | collective-permute-start | bytes 393224 | tf_op jit(solution)/shard_map/ppermute | solution.py:10
  69.0 7.8 %collective-permute-done.5 = f32[512,64]{0,1:T(8,128)S(1)} collective-permute-done((f32[512,64]{0,1:T(8,128)S(1)}, f32[512,64]{0,1:T(8,128)S(1)}, u32[]{:S(2)}, u32[]{:S(2)}) %collective-permute-start.5) | collective-permute-done | bytes 131104 | tf_op jit(solution)/shard_map/ppermute | solution.py:10
  76.8 1.9 collective-permute-start.6
  78.7 10.6 %collective-permute-done.6 = f32[512,64]{0,1:T(8,128)S(1)} collective-permute-done((f32[512,64]{0,1:T(8,128)S(1)}, f32[512,64]{0,1:T(8,128)S(1)}, u32[]{:S(2)}, u32[]{:S(2)}) %collective-permute-start.6) | collective-permute-done | bytes 131104 | tf_op jit(solution)/shard_map/ppermute | solution.py:10
  89.3 2.1 %convolution_bitcast_fusion.5 = f32[1024,64]{0,1:T(8,128)S(1)} fusion(f32[1024,512]{1,0:T(8,128)S(1)} %copy-done, f32[512,64]{0,1:T(8,128)S(1)} %collective-permute-done.6, f32[512,64]{0,1:T(8,128)S(1)} %fusion.7, pred[]{:T(512)S(6)} %eq.75), kind=kOutput, calls=%fused_computation.5 | convolution fusion | flops 402685952 | bytes 2621441 | tf_op jit(solution)/shard_map/dot_general | solution.py:14
  91.5 9.3 %collective-permute-start.7 = (f32[512,64]{0,1:T(8,128)S(1)}, f32[512,64]{0,1:T(8,128)S(1)}, u32[]{:S(2)}, u32[]{:S(2)}) collective-permute-start(f32[512,64]{0,1:T(8,128)S(1)} %slice.78), channel_id=1, source_target_pairs={{32,0},{33,1},{34,2},{35,3},{36,4},{37,5},{38,6},{39,7},{40,8},{41... | collective-permute-start | bytes 393224 | tf_op jit(solution)/shard_map/ppermute | solution.py:10
  100.8 6.6 %collective-permute-done.7 = f32[512,64]{0,1:T(8,128)S(1)} collective-permute-done((f32[512,64]{0,1:T(8,128)S(1)}, f32[512,64]{0,1:T(8,128)S(1)}, u32[]{:S(2)}, u32[]{:S(2)}) %collective-permute-start.7) | collective-permute-done | bytes 131104 | tf_op jit(solution)/shard_map/ppermute | solution.py:10
  107.5 1.9 collective-permute-start.8
  109.4 8.7 %collective-permute-done.8 = f32[512,64]{0,1:T(8,128)S(1)} collective-permute-done((f32[512,64]{0,1:T(8,128)S(1)}, f32[512,64]{0,1:T(8,128)S(1)}, u32[]{:S(2)}, u32[]{:S(2)}) %collective-permute-start.8) | collective-permute-done | bytes 131104 | tf_op jit(solution)/shard_map/ppermute | solution.py:10
  118.1 2.1 %convolution_bitcast_fusion.4 = f32[1024,64]{0,1:T(8,128)S(1)} fusion(f32[1024,512]{1,0:T(8,128)S(1)} %copy-done, f32[512,64]{0,1:T(8,128)S(1)} %collective-permute-done.8, f32[512,64]{0,1:T(8,128)S(1)} %fusion.6, pred[]{:T(512)S(6)} %eq.73), kind=kOutput, calls=%fused_computation.4 | convolution fusion | flops 402685952 | bytes 2621441 | tf_op jit(solution)/shard_map/dot_general | solution.py:14
  120.3 5.3 %collective-permute-start.9 = (f32[512,64]{0,1:T(8,128)S(1)}, f32[512,64]{0,1:T(8,128)S(1)}, u32[]{:S(2)}, u32[]{:S(2)}) collective-permute-start(f32[512,64]{0,1:T(8,128)S(1)} %slice.80), channel_id=1, source_target_pairs={{16,0},{17,1},{18,2},{19,3},{20,4},{21,5},{22,6},{23,7},{24,8},{25... | collective-permute-start | bytes 393224 | tf_op jit(solution)/shard_map/ppermute | solution.py:10
  125.6 2.5 %collective-permute-done.9 = f32[512,64]{0,1:T(8,128)S(1)} collective-permute-done((f32[512,64]{0,1:T(8,128)S(1)}, f32[512,64]{0,1:T(8,128)S(1)}, u32[]{:S(2)}, u32[]{:S(2)}) %collective-permute-start.9) | collective-permute-done | bytes 131104 | tf_op jit(solution)/shard_map/ppermute | solution.py:10
  128.1 1.9 collective-permute-start.10
  130.1 7.0 %collective-permute-done.10 = f32[512,64]{0,1:T(8,128)S(1)} collective-permute-done((f32[512,64]{0,1:T(8,128)S(1)}, f32[512,64]{0,1:T(8,128)S(1)}, u32[]{:S(2)}, u32[]{:S(2)}) %collective-permute-start.10) | collective-permute-done | bytes 131104 | tf_op jit(solution)/shard_map/ppermute | solution.py:10
  137.1 2.1 %convolution_bitcast_fusion.3 = f32[1024,64]{0,1:T(8,128)S(1)} fusion(f32[1024,512]{1,0:T(8,128)S(1)} %copy-done, f32[512,64]{0,1:T(8,128)S(1)} %collective-permute-done.10, f32[512,64]{0,1:T(8,128)S(1)} %fusion.5, pred[]{:T(512)S(6)} %eq.71), kind=kOutput, calls=%fused_computation.3 | convolution fusion | flops 402685952 | bytes 2621441 | tf_op jit(solution)/shard_map/dot_general | solution.py:14
  139.3 3.8 %collective-permute-start.11 = (f32[512,64]{0,1:T(8,128)S(1)}, f32[512,64]{0,1:T(8,128)S(1)}, u32[]{:S(2)}, u32[]{:S(2)}) collective-permute-start(f32[512,64]{0,1:T(8,128)S(1)} %slice.82), channel_id=1, source_target_pairs={{8,0},{9,1},{10,2},{11,3},{12,4},{13,5},{14,6},{15,7},{16,8},{17,9... | collective-permute-start | bytes 393224 | tf_op jit(solution)/shard_map/ppermute | solution.py:10
  143.1 3.0 %collective-permute-done.11 = f32[512,64]{0,1:T(8,128)S(1)} collective-permute-done((f32[512,64]{0,1:T(8,128)S(1)}, f32[512,64]{0,1:T(8,128)S(1)}, u32[]{:S(2)}, u32[]{:S(2)}) %collective-permute-start.11) | collective-permute-done | bytes 131104 | tf_op jit(solution)/shard_map/ppermute | solution.py:10
  146.1 2.1 %collective-permute-start.12 = (f32[512,64]{0,1:T(8,128)S(1)}, f32[512,64]{0,1:T(8,128)S(1)}, u32[]{:S(2)}, u32[]{:S(2)}) collective-permute-start(f32[512,64]{0,1:T(8,128)S(1)} %fusion.4), channel_id=1, source_target_pairs={{0,4},{1,5},{2,6},{3,7},{4,8},{5,9},{6,10},{7,11},{8,12},{9,13},{1... | collective-permute-start | bytes 393224 | tf_op jit(solution)/shard_map/ppermute | solution.py:10
  148.3 6.3 %collective-permute-done.12 = f32[512,64]{0,1:T(8,128)S(1)} collective-permute-done((f32[512,64]{0,1:T(8,128)S(1)}, f32[512,64]{0,1:T(8,128)S(1)}, u32[]{:S(2)}, u32[]{:S(2)}) %collective-permute-start.12) | collective-permute-done | bytes 131104 | tf_op jit(solution)/shard_map/ppermute | solution.py:10
  154.5 2.1 %convolution_bitcast_fusion.2 = f32[1024,64]{0,1:T(8,128)S(1)} fusion(f32[1024,512]{1,0:T(8,128)S(1)} %copy-done, f32[512,64]{0,1:T(8,128)S(1)} %collective-permute-done.12, f32[512,64]{0,1:T(8,128)S(1)} %fusion.4, pred[]{:T(512)S(6)} %eq.69), kind=kOutput, calls=%fused_computation.2 | convolution fusion | flops 402685952 | bytes 2621441 | tf_op jit(solution)/shard_map/dot_general | solution.py:14
  156.7 1.9 collective-permute-start.13
  158.6 2.5 %collective-permute-done.13 = f32[512,64]{0,1:T(8,128)S(1)} collective-permute-done((f32[512,64]{0,1:T(8,128)S(1)}, f32[512,64]{0,1:T(8,128)S(1)}, u32[]{:S(2)}, u32[]{:S(2)}) %collective-permute-start.13) | collective-permute-done | bytes 131104 | tf_op jit(solution)/shard_map/ppermute | solution.py:10
  161.2 6.6 %collective-permute-start.14 = (f32[512,64]{0,1:T(8,128)S(1)}, f32[512,64]{0,1:T(8,128)S(1)}, u32[]{:S(2)}, u32[]{:S(2)}) collective-permute-start(f32[512,64]{0,1:T(8,128)S(1)} %fusion.3), channel_id=1, source_target_pairs={{0,2},{1,3},{2,4},{3,5},{4,6},{5,7},{6,8},{7,9},{8,10},{9,11},{10,... | collective-permute-start | bytes 393224 | tf_op jit(solution)/shard_map/ppermute | solution.py:10
  167.8 6.0 %collective-permute-done.14 = f32[512,64]{0,1:T(8,128)S(1)} collective-permute-done((f32[512,64]{0,1:T(8,128)S(1)}, f32[512,64]{0,1:T(8,128)S(1)}, u32[]{:S(2)}, u32[]{:S(2)}) %collective-permute-start.14) | collective-permute-done | bytes 131104 | tf_op jit(solution)/shard_map/ppermute | solution.py:10
  173.8 2.1 %convolution_bitcast_fusion.1 = f32[1024,64]{0,1:T(8,128)S(1)} fusion(f32[1024,512]{1,0:T(8,128)S(1)} %copy-done, f32[512,64]{0,1:T(8,128)S(1)} %collective-permute-done.14, f32[512,64]{0,1:T(8,128)S(1)} %fusion.3, pred[]{:T(512)S(6)} %eq.67), kind=kOutput, calls=%fused_computation.1 | convolution fusion | flops 402685952 | bytes 2621441 | tf_op jit(solution)/shard_map/dot_general | solution.py:14
  175.9 0.7 copy-done.2
  176.6 4.7 %collective-permute-start.15 = (f32[512,64]{0,1:T(8,128)S(1)}, f32[512,64]{0,1:T(8,128)S(1)}, u32[]{:S(2)}, u32[]{:S(2)}) collective-permute-start(f32[512,64]{0,1:T(8,128)S(1)} %slice.86), channel_id=1, source_target_pairs={{2,0},{3,1},{4,2},{5,3},{6,4},{7,5},{8,6},{9,7},{10,8},{11,9},{12,... | collective-permute-start | bytes 393224 | tf_op jit(solution)/shard_map/ppermute | solution.py:10
  181.4 3.8 %collective-permute-done.15 = f32[512,64]{0,1:T(8,128)S(1)} collective-permute-done((f32[512,64]{0,1:T(8,128)S(1)}, f32[512,64]{0,1:T(8,128)S(1)}, u32[]{:S(2)}, u32[]{:S(2)}) %collective-permute-start.15) | collective-permute-done | bytes 131104 | tf_op jit(solution)/shard_map/ppermute | solution.py:10
  185.1 0.9 fusion.2
  186.1 3.2 %collective-permute-start.16 = (f32[512,64]{0,1:T(8,128)S(1)}, f32[512,64]{0,1:T(8,128)S(1)}, u32[]{:S(2)}, u32[]{:S(2)}) collective-permute-start(f32[512,64]{0,1:T(8,128)S(1)} %fusion.2), channel_id=1, source_target_pairs={{0,1},{1,2},{2,3},{3,4},{4,5},{5,6},{6,7},{7,8},{8,9},{9,10},{10,1... | collective-permute-start | bytes 393224 | tf_op jit(solution)/shard_map/ppermute | solution.py:10
  189.3 7.3 %collective-permute-done.16 = f32[512,64]{0,1:T(8,128)S(1)} collective-permute-done((f32[512,64]{0,1:T(8,128)S(1)}, f32[512,64]{0,1:T(8,128)S(1)}, u32[]{:S(2)}, u32[]{:S(2)}) %collective-permute-start.16) | collective-permute-done | bytes 131104 | tf_op jit(solution)/shard_map/ppermute | solution.py:10
  196.6 2.1 %convolution_bitcast_fusion = f32[1024,64]{0,1:T(8,128)S(1)} fusion(f32[1024,512]{1,0:T(8,128)S(1)} %copy-done, f32[512,64]{0,1:T(8,128)S(1)} %collective-permute-done.16, f32[512,64]{0,1:T(8,128)S(1)} %fusion.2, pred[]{:T(512)S(6)} %eq.65), kind=kOutput, calls=%fused_computation | convolution fusion | flops 402685952 | bytes 2621441 | tf_op jit(solution)/shard_map/dot_general | solution.py:14
  199.4 1.9 collective-permute-start.17
  201.4 4.9 %collective-permute-done.17 = f32[512,64]{0,1:T(8,128)S(1)} collective-permute-done((f32[512,64]{0,1:T(8,128)S(1)}, f32[512,64]{0,1:T(8,128)S(1)}, u32[]{:S(2)}, u32[]{:S(2)}) %collective-permute-start.17) | collective-permute-done | bytes 131104 | tf_op jit(solution)/shard_map/ppermute | solution.py:10
  206.3 2.7 %convolution_bitcast_fusion.9 = f32[512,64]{0,1:T(8,128)} fusion(f32[512,512]{1,0:T(8,128)S(1)} %copy-done.1, f32[512,64]{0,1:T(8,128)S(1)} %collective-permute-done.17, f32[512,64]{0,1:T(8,128)S(1)} %fusion.2, f32[1024,64]{0,1:T(8,128)} %copy-done.3, pred[]{:T(512)S(6)} %eq.65, pred[]{:T(512)S(6)} %eq.64), kind=kOutput, calls=%fused_computation.9 | convolution fusion | flops 201392128 | bytes 1572866 | tf_op jit(solution)/shard_map/dot_general | solution.py:38
  (25 shorter events, 1.0 us)
Async XLA Ops:
  0.0 9.0 %copy-start = (f32[1024,512]{1,0:T(8,128)S(1)}, f32[1024,512]{1,0:T(8,128)}, u32[]{:S(2)}) copy-start(f32[1024,512]{1,0:T(8,128)} %param.3) | copy-start | bytes 6291460
  0.0 16.1 %copy-start.4 = (f32[512,64]{0,1:T(8,128)S(1)}, f32[512,64]{0,1:T(8,128)}, u32[]{:S(2)}) copy-start(f32[512,64]{0,1:T(8,128)} %param.5) | copy-start | bytes 393220
  0.0 9.0 %collective-permute-start = (f32[512,64]{0,1:T(8,128)}, f32[512,64]{0,1:T(8,128)S(1)}, u32[]{:S(2)}, u32[]{:S(2)}) collective-permute-start(f32[512,64]{0,1:T(8,128)} %param.5), channel_id=1, source_target_pairs={{0,256},{1,257},{2,258},{3,259},{4,260},{5,261},{6,262},{7,263},{8... | collective-permute-start | bytes 393224 | tf_op jit(solution)/shard_map/ppermute | solution.py:10
  12.0 4.1 %collective-permute-start.1 = (f32[512,64]{0,1:T(8,128)S(1)}, f32[512,64]{0,1:T(8,128)S(1)}, u32[]{:S(2)}, u32[]{:S(2)}) collective-permute-start(f32[512,64]{0,1:T(8,128)S(1)} %slice.72), channel_id=1, source_target_pairs={{256,0},{257,1},{258,2},{259,3},{260,4},{261,5},{262,6},{263,7},{2... | collective-permute-start | bytes 393224 | tf_op jit(solution)/shard_map/ppermute | solution.py:10
  16.1 6.9 %collective-permute-start.2 = (f32[512,64]{0,1:T(8,128)S(1)}, f32[512,64]{0,1:T(8,128)S(1)}, u32[]{:S(2)}, u32[]{:S(2)}) collective-permute-start(f32[512,64]{0,1:T(8,128)S(1)} %fusion.9), channel_id=1, source_target_pairs={{0,128},{1,129},{2,130},{3,131},{4,132},{5,133},{6,134},{7,135},{8... | collective-permute-start | bytes 393224 | tf_op jit(solution)/shard_map/ppermute | solution.py:10
  25.2 6.4 %collective-permute-start.3 = (f32[512,64]{0,1:T(8,128)S(1)}, f32[512,64]{0,1:T(8,128)S(1)}, u32[]{:S(2)}, u32[]{:S(2)}) collective-permute-start(f32[512,64]{0,1:T(8,128)S(1)} %slice.74), channel_id=1, source_target_pairs={{128,0},{129,1},{130,2},{131,3},{132,4},{133,5},{134,6},{135,7},{1... | collective-permute-start | bytes 393224 | tf_op jit(solution)/shard_map/ppermute | solution.py:10
  31.7 24.2 %collective-permute-start.4 = (f32[512,64]{0,1:T(8,128)S(1)}, f32[512,64]{0,1:T(8,128)S(1)}, u32[]{:S(2)}, u32[]{:S(2)}) collective-permute-start(f32[512,64]{0,1:T(8,128)S(1)} %fusion.8), channel_id=1, source_target_pairs={{0,64},{1,65},{2,66},{3,67},{4,68},{5,69},{6,70},{7,71},{8,72},{9,... | collective-permute-start | bytes 393224 | tf_op jit(solution)/shard_map/ppermute | solution.py:10
  58.0 18.8 %collective-permute-start.5 = (f32[512,64]{0,1:T(8,128)S(1)}, f32[512,64]{0,1:T(8,128)S(1)}, u32[]{:S(2)}, u32[]{:S(2)}) collective-permute-start(f32[512,64]{0,1:T(8,128)S(1)} %slice.76), channel_id=1, source_target_pairs={{64,0},{65,1},{66,2},{67,3},{68,4},{69,5},{70,6},{71,7},{72,8},{73... | collective-permute-start | bytes 393224 | tf_op jit(solution)/shard_map/ppermute | solution.py:10
  76.8 12.5 %collective-permute-start.6 = (f32[512,64]{0,1:T(8,128)S(1)}, f32[512,64]{0,1:T(8,128)S(1)}, u32[]{:S(2)}, u32[]{:S(2)}) collective-permute-start(f32[512,64]{0,1:T(8,128)S(1)} %fusion.7), channel_id=1, source_target_pairs={{0,32},{1,33},{2,34},{3,35},{4,36},{5,37},{6,38},{7,39},{8,40},{9,... | collective-permute-start | bytes 393224 | tf_op jit(solution)/shard_map/ppermute | solution.py:10
  91.5 16.0 %collective-permute-start.7 = (f32[512,64]{0,1:T(8,128)S(1)}, f32[512,64]{0,1:T(8,128)S(1)}, u32[]{:S(2)}, u32[]{:S(2)}) collective-permute-start(f32[512,64]{0,1:T(8,128)S(1)} %slice.78), channel_id=1, source_target_pairs={{32,0},{33,1},{34,2},{35,3},{36,4},{37,5},{38,6},{39,7},{40,8},{41... | collective-permute-start | bytes 393224 | tf_op jit(solution)/shard_map/ppermute | solution.py:10
  107.5 10.6 %collective-permute-start.8 = (f32[512,64]{0,1:T(8,128)S(1)}, f32[512,64]{0,1:T(8,128)S(1)}, u32[]{:S(2)}, u32[]{:S(2)}) collective-permute-start(f32[512,64]{0,1:T(8,128)S(1)} %fusion.6), channel_id=1, source_target_pairs={{0,16},{1,17},{2,18},{3,19},{4,20},{5,21},{6,22},{7,23},{8,24},{9,... | collective-permute-start | bytes 393224 | tf_op jit(solution)/shard_map/ppermute | solution.py:10
  120.3 7.8 %collective-permute-start.9 = (f32[512,64]{0,1:T(8,128)S(1)}, f32[512,64]{0,1:T(8,128)S(1)}, u32[]{:S(2)}, u32[]{:S(2)}) collective-permute-start(f32[512,64]{0,1:T(8,128)S(1)} %slice.80), channel_id=1, source_target_pairs={{16,0},{17,1},{18,2},{19,3},{20,4},{21,5},{22,6},{23,7},{24,8},{25... | collective-permute-start | bytes 393224 | tf_op jit(solution)/shard_map/ppermute | solution.py:10
  128.1 9.0 %collective-permute-start.10 = (f32[512,64]{0,1:T(8,128)S(1)}, f32[512,64]{0,1:T(8,128)S(1)}, u32[]{:S(2)}, u32[]{:S(2)}) collective-permute-start(f32[512,64]{0,1:T(8,128)S(1)} %fusion.5), channel_id=1, source_target_pairs={{0,8},{1,9},{2,10},{3,11},{4,12},{5,13},{6,14},{7,15},{8,16},{9,17... | collective-permute-start | bytes 393224 | tf_op jit(solution)/shard_map/ppermute | solution.py:10
  139.3 6.9 %collective-permute-start.11 = (f32[512,64]{0,1:T(8,128)S(1)}, f32[512,64]{0,1:T(8,128)S(1)}, u32[]{:S(2)}, u32[]{:S(2)}) collective-permute-start(f32[512,64]{0,1:T(8,128)S(1)} %slice.82), channel_id=1, source_target_pairs={{8,0},{9,1},{10,2},{11,3},{12,4},{13,5},{14,6},{15,7},{16,8},{17,9... | collective-permute-start | bytes 393224 | tf_op jit(solution)/shard_map/ppermute | solution.py:10
  146.1 8.4 %collective-permute-start.12 = (f32[512,64]{0,1:T(8,128)S(1)}, f32[512,64]{0,1:T(8,128)S(1)}, u32[]{:S(2)}, u32[]{:S(2)}) collective-permute-start(f32[512,64]{0,1:T(8,128)S(1)} %fusion.4), channel_id=1, source_target_pairs={{0,4},{1,5},{2,6},{3,7},{4,8},{5,9},{6,10},{7,11},{8,12},{9,13},{1... | collective-permute-start | bytes 393224 | tf_op jit(solution)/shard_map/ppermute | solution.py:10
  156.7 4.4 %collective-permute-start.13 = (f32[512,64]{0,1:T(8,128)S(1)}, f32[512,64]{0,1:T(8,128)S(1)}, u32[]{:S(2)}, u32[]{:S(2)}) collective-permute-start(f32[512,64]{0,1:T(8,128)S(1)} %slice.84), channel_id=1, source_target_pairs={{4,0},{5,1},{6,2},{7,3},{8,4},{9,5},{10,6},{11,7},{12,8},{13,9},{1... | collective-permute-start | bytes 393224 | tf_op jit(solution)/shard_map/ppermute | solution.py:10
  161.2 12.6 %collective-permute-start.14 = (f32[512,64]{0,1:T(8,128)S(1)}, f32[512,64]{0,1:T(8,128)S(1)}, u32[]{:S(2)}, u32[]{:S(2)}) collective-permute-start(f32[512,64]{0,1:T(8,128)S(1)} %fusion.3), channel_id=1, source_target_pairs={{0,2},{1,3},{2,4},{3,5},{4,6},{5,7},{6,8},{7,9},{8,10},{9,11},{10,... | collective-permute-start | bytes 393224 | tf_op jit(solution)/shard_map/ppermute | solution.py:10
  175.9 0.7 copy-start.2
  176.6 29.7 %copy-start.1 = (f32[512,512]{1,0:T(8,128)S(1)}, f32[512,512]{1,0:T(8,128)}, u32[]{:S(2)}) copy-start(f32[512,512]{1,0:T(8,128)} %param.4) | copy-start | bytes 3145732
  176.6 8.5 %collective-permute-start.15 = (f32[512,64]{0,1:T(8,128)S(1)}, f32[512,64]{0,1:T(8,128)S(1)}, u32[]{:S(2)}, u32[]{:S(2)}) collective-permute-start(f32[512,64]{0,1:T(8,128)S(1)} %slice.86), channel_id=1, source_target_pairs={{2,0},{3,1},{4,2},{5,3},{6,4},{7,5},{8,6},{9,7},{10,8},{11,9},{12,... | collective-permute-start | bytes 393224 | tf_op jit(solution)/shard_map/ppermute | solution.py:10
  186.1 10.5 %collective-permute-start.16 = (f32[512,64]{0,1:T(8,128)S(1)}, f32[512,64]{0,1:T(8,128)S(1)}, u32[]{:S(2)}, u32[]{:S(2)}) collective-permute-start(f32[512,64]{0,1:T(8,128)S(1)} %fusion.2), channel_id=1, source_target_pairs={{0,1},{1,2},{2,3},{3,4},{4,5},{5,6},{6,7},{7,8},{8,9},{9,10},{10,1... | collective-permute-start | bytes 393224 | tf_op jit(solution)/shard_map/ppermute | solution.py:10
  198.7 0.7 copy-start.3
  199.4 6.9 %collective-permute-start.17 = (f32[512,64]{0,1:T(8,128)S(1)}, f32[512,64]{0,1:T(8,128)S(1)}, u32[]{:S(2)}, u32[]{:S(2)}) collective-permute-start(f32[512,64]{0,1:T(8,128)S(1)} %slice.88), channel_id=1, source_target_pairs={{1,0},{2,1},{3,2},{4,3},{5,4},{6,5},{7,6},{8,7},{9,8},{10,9},{11,1... | collective-permute-start | bytes 393224 | tf_op jit(solution)/shard_map/ppermute | solution.py:10
where the time goes:
time: 210 us; the launch traced here: 209 us
  waiting for transfers between devices  104 us (50%)
  starting transfers between devices  79.3 us (38%)
  matrix products  22.8 us (11%)
    ppermute x18, waiting for transfers between devices, from_behind(): return lax.ppermute(block, axis, route)  104 us
    ppermute x18, starting transfers between devices, from_behind(): return lax.ppermute(block, axis, route)  79.3 us
    dot_general x9, matrix products, apply_node(): jnp.dot(factor, coefficient, precision=lax.Precision.HIGHEST, preferred_e...  20.1 us
  transfers between devices with their start and end apart: 18, of which 18 were waited for; matrix products, arithmetic and copies ran while one was open for 0% of the time, Pallas kernels for 0%

commit v1 on v0

v1 whole, which is shorter than its diff:
```python
import jax
import jax.numpy as jnp
from jax import lax
from jax.sharding import PartitionSpec as P

AXES = ("wide", "narrow")


def times(coefficient, factor):
    return lax.dot_general(
        coefficient, factor, (((1,), (1,)), ((), ())),
        precision=lax.Precision.HIGH, preferred_element_type=jnp.float32,
    )


def on_device(node_factors, leaf_q, modal_basis):
    leaf_count = lax.axis_size("wide") * lax.axis_size("narrow")
    levels = leaf_count.bit_length() - 1
    snaps = node_factors.shape[1]
    leaf = lax.axis_index("wide") * lax.axis_size("narrow") + lax.axis_index("narrow")
    held = modal_basis.T
    upper, lower = node_factors[:snaps], node_factors[snaps:]
    for level in range(levels, 0, -1):
        reach = 2 ** (level - 1)
        owners = range(reach, leaf_count, 2 * reach)
        left = times(held, upper)
        if level > 1:
            step = reach // 2
            from_right = lax.ppermute(left, AXES, [(o, o - step) for o in owners])
            right = times(held, lower)
            from_left = lax.ppermute(right, AXES, [(o, o + step) for o in owners])
            held = jnp.where(leaf % (4 * step) == step, from_right, from_left)
        else:
            from_right = lax.ppermute(left, AXES, [(o, o - 1) for o in owners])
            right = times(held, lower)
            held = jnp.where(leaf % 2 == 0, from_right, right)
    return times(held, leaf_q).T


def solution(mesh):
    return jax.shard_map(
        on_device,
        mesh=mesh,
        in_specs=(P(AXES, None), P(AXES, None), P()),
        out_specs=P(AXES, None),
        check_vma=False,
    )
```

time: 210 us -> 88.6 us (0.42)
  the two profiles are of different devices: /device:TPU:24 before, /device:TPU:93 now
where the time goes in v1:
time: 88.6 us; the launch traced here: 88.3 us
  waiting for transfers between devices  49.2 us (56%)
  matrix products  25 us (28%)
  starting transfers between devices  13.7 us (15%)
    ppermute x8, waiting for transfers between devices, on_device(): from_left = lax.ppermute(right, AXES, [(o, o + step) for o in owners])  44.8 us
    dot_general x19, matrix products, times(): lax.dot_general(coefficient, factor, (((1,), (1,)), ((), ())), precision=...  25 us
    ppermute x8, starting transfers between devices, on_device(): from_left = lax.ppermute(right, AXES, [(o, o + step) for o in owners])  6.51 us
    ppermute x8, starting transfers between devices, on_device(): from_right = lax.ppermute(left, AXES, [(o, o - step) for o in owners])  5.89 us
    ppermute x1, waiting for transfers between devices, on_device(): from_right = lax.ppermute(left, AXES, [(o, o - 1) for o in owners])  4.35 us
  transfers between devices with their start and end apart: 17, of which 3 were waited for; matrix products, arithmetic and copies ran while one was open for 14% of the time, Pallas kernels for 0%

profile of v1, /device:TPU:93, one launch (start us, length us, event | category | flops | bytes accessed | tf_op | source)
XLA Modules:
  0.0 88.3 jit_solution(11586362389276530490)
XLA Ops:
  0.0 2.0 %fusion.34 = f32[64,512]{1,0:T(8,128)S(1)} fusion(f32[512,64]{0,1:T(8,128)} %param.5, f32[1024,512]{1,0:T(8,128)} %param.3), kind=kOutput, calls=%fused_computation.35 | convolution fusion | flops 100663296 | bytes 1310720 | tf_op jit(solution)/shard_map/dot_general | solution.py:10
  2.0 0.7 collective-permute-start
  2.7 2.6 %fusion.16 = f32[64,512]{1,0:T(8,128)} fusion(f32[512,64]{0,1:T(8,128)} %param.5, f32[1024,512]{1,0:T(8,128)} %param.3), kind=kOutput, calls=%fused_computation.17 | convolution fusion | flops 100663296 | bytes 1310720 | tf_op jit(solution)/shard_map/dot_general | solution.py:10
  5.3 0.7 collective-permute-start.1
  6.0 0.0 collective-permute-done
  6.0 1.3 %fusion.32 = f32[64,512]{1,0:T(8,128)} fusion(f32[1024,512]{1,0:T(8,128)S(1)} %copy-done.1, f32[64,512]{1,0:T(8,128)S(1)} %collective-permute-done, f32[64,512]{1,0:T(8,128)S(1)} %collective-permute-done.1, pred[]{:T(512)S(6)} %eq.45), kind=kOutput, calls=%fused_computation.33 | convolution fusion | flops 100696064 | bytes 1441793 | tf_op jit(solution)/shard_map/dot_general | solution.py:10
  7.3 0.7 collective-permute-start.2
  7.9 1.3 %fusion.14 = f32[64,512]{1,0:T(8,128)} fusion(f32[1024,512]{1,0:T(8,128)S(1)} %copy-done.1, f32[64,512]{1,0:T(8,128)S(1)} %collective-permute-done, f32[64,512]{1,0:T(8,128)S(1)} %collective-permute-done.1, pred[]{:T(512)S(6)} %eq.45), kind=kOutput, calls=%fused_computation.15 | convolution fusion | flops 100696064 | bytes 1441793 | tf_op jit(solution)/shard_map/dot_general | solution.py:10
  9.2 0.7 collective-permute-start.3
  9.9 0.0 collective-permute-done.2
  9.9 0.0 collective-permute-done.3
  9.9 1.3 %fusion.30 = f32[64,512]{1,0:T(8,128)} fusion(f32[1024,512]{1,0:T(8,128)S(1)} %copy-done.1, f32[64,512]{1,0:T(8,128)S(1)} %collective-permute-done.2, f32[64,512]{1,0:T(8,128)S(1)} %collective-permute-done.3, pred[]{:T(512)S(6)} %eq.44), kind=kOutput, calls=%fused_computation.31 | convolution fusion | flops 100696064 | bytes 1441793 | tf_op jit(solution)/shard_map/dot_general | solution.py:10
  11.2 0.7 collective-permute-start.4
  11.9 1.3 %fusion.12 = f32[64,512]{1,0:T(8,128)} fusion(f32[1024,512]{1,0:T(8,128)S(1)} %copy-done.1, f32[64,512]{1,0:T(8,128)S(1)} %collective-permute-done.2, f32[64,512]{1,0:T(8,128)S(1)} %collective-permute-done.3, pred[]{:T(512)S(6)} %eq.44), kind=kOutput, calls=%fused_computation.13 | convolution fusion | flops 100696064 | bytes 1441793 | tf_op jit(solution)/shard_map/dot_general | solution.py:10
  13.2 0.7 collective-permute-start.5
  13.8 0.0 collective-permute-done.5
  13.9 1.3 %fusion.28 = f32[64,512]{1,0:T(8,128)} fusion(f32[1024,512]{1,0:T(8,128)S(1)} %copy-done.1, f32[64,512]{1,0:T(8,128)S(1)} %collective-permute-done.4, f32[64,512]{1,0:T(8,128)S(1)} %collective-permute-done.5, pred[]{:T(512)S(6)} %eq.43), kind=kOutput, calls=%fused_computation.29 | convolution fusion | flops 100696064 | bytes 1441793 | tf_op jit(solution)/shard_map/dot_general | solution.py:10
  15.1 0.7 collective-permute-start.6
  15.8 1.3 %fusion.10 = f32[64,512]{1,0:T(8,128)} fusion(f32[1024,512]{1,0:T(8,128)S(1)} %copy-done.1, f32[64,512]{1,0:T(8,128)S(1)} %collective-permute-done.4, f32[64,512]{1,0:T(8,128)S(1)} %collective-permute-done.5, pred[]{:T(512)S(6)} %eq.43), kind=kOutput, calls=%fused_computation.11 | convolution fusion | flops 100696064 | bytes 1441793 | tf_op jit(solution)/shard_map/dot_general | solution.py:10
  17.1 0.7 collective-permute-start.7
  17.8 0.0 collective-permute-done.6
  17.8 1.3 %fusion.26 = f32[64,512]{1,0:T(8,128)} fusion(f32[1024,512]{1,0:T(8,128)S(1)} %copy-done.1, f32[64,512]{1,0:T(8,128)S(1)} %collective-permute-done.6, f32[64,512]{1,0:T(8,128)S(1)} %collective-permute-done.7, pred[]{:T(512)S(6)} %eq.42), kind=kOutput, calls=%fused_computation.27 | convolution fusion | flops 100696064 | bytes 1441793 | tf_op jit(solution)/shard_map/dot_general | solution.py:10
  19.1 0.7 collective-permute-start.8
  19.7 1.3 %fusion.8 = f32[64,512]{1,0:T(8,128)} fusion(f32[1024,512]{1,0:T(8,128)S(1)} %copy-done.1, f32[64,512]{1,0:T(8,128)S(1)} %collective-permute-done.6, f32[64,512]{1,0:T(8,128)S(1)} %collective-permute-done.7, pred[]{:T(512)S(6)} %eq.42), kind=kOutput, calls=%fused_computation.9 | convolution fusion | flops 100696064 | bytes 1441793 | tf_op jit(solution)/shard_map/dot_general | solution.py:10
  21.0 0.7 collective-permute-start.9
  21.7 0.0 collective-permute-done.8
  21.7 0.0 collective-permute-done.9
  21.7 1.3 %fusion.24 = f32[64,512]{1,0:T(8,128)} fusion(f32[1024,512]{1,0:T(8,128)S(1)} %copy-done.1, f32[64,512]{1,0:T(8,128)S(1)} %collective-permute-done.8, f32[64,512]{1,0:T(8,128)S(1)} %collective-permute-done.9, pred[]{:T(512)S(6)} %eq.41), kind=kOutput, calls=%fused_computation.25 | convolution fusion | flops 100696064 | bytes 1441793 | tf_op jit(solution)/shard_map/dot_general | solution.py:10
  23.0 0.7 collective-permute-start.10
  23.6 1.3 %fusion.6 = f32[64,512]{1,0:T(8,128)} fusion(f32[1024,512]{1,0:T(8,128)S(1)} %copy-done.1, f32[64,512]{1,0:T(8,128)S(1)} %collective-permute-done.8, f32[64,512]{1,0:T(8,128)S(1)} %collective-permute-done.9, pred[]{:T(512)S(6)} %eq.41), kind=kOutput, calls=%fused_computation.7 | convolution fusion | flops 100696064 | bytes 1441793 | tf_op jit(solution)/shard_map/dot_general | solution.py:10
  24.9 0.7 collective-permute-start.11
  25.6 0.0 collective-permute-done.10
  25.6 1.3 %fusion.22 = f32[64,512]{1,0:T(8,128)} fusion(f32[1024,512]{1,0:T(8,128)S(1)} %copy-done.1, f32[64,512]{1,0:T(8,128)S(1)} %collective-permute-done.10, f32[64,512]{1,0:T(8,128)S(1)} %collective-permute-done.11, pred[]{:T(512)S(6)} %eq.40), kind=kOutput, calls=%fused_computation.23 | convolution fusion | flops 100696064 | bytes 1441793 | tf_op jit(solution)/shard_map/dot_general | solution.py:10
  26.9 0.7 collective-permute-start.12
  27.6 1.3 %fusion.4 = f32[64,512]{1,0:T(8,128)} fusion(f32[1024,512]{1,0:T(8,128)S(1)} %copy-done.1, f32[64,512]{1,0:T(8,128)S(1)} %collective-permute-done.10, f32[64,512]{1,0:T(8,128)S(1)} %collective-permute-done.11, pred[]{:T(512)S(6)} %eq.40), kind=kOutput, calls=%fused_computation.5 | convolution fusion | flops 100696064 | bytes 1441793 | tf_op jit(solution)/shard_map/dot_general | solution.py:10
  28.9 1.3 %collective-permute-start.13 = (f32[64,512]{1,0:T(8,128)}, f32[64,512]{1,0:T(8,128)S(1)}, u32[]{:S(2)}, u32[]{:S(2)}) collective-permute-start(f32[64,512]{1,0:T(8,128)} %fusion.4), channel_id=1, source_target_pairs={{4,6},{12,14},{20,22},{28,30},{36,38},{44,46},{52,54},{60,62},{68,... | collective-permute-start | bytes 393224 | tf_op jit(solution)/shard_map/ppermute | solution.py:31
  30.2 42.6 %collective-permute-done.13 = f32[64,512]{1,0:T(8,128)S(1)} collective-permute-done((f32[64,512]{1,0:T(8,128)}, f32[64,512]{1,0:T(8,128)S(1)}, u32[]{:S(2)}, u32[]{:S(2)}) %collective-permute-start.13) | collective-permute-done | bytes 131104 | tf_op jit(solution)/shard_map/ppermute | solution.py:31
  72.8 1.3 %fusion.20 = f32[64,512]{1,0:T(8,128)} fusion(f32[1024,512]{1,0:T(8,128)S(1)} %copy-done.1, f32[64,512]{1,0:T(8,128)S(1)} %collective-permute-done.12, f32[64,512]{1,0:T(8,128)S(1)} %collective-permute-done.13, pred[]{:T(512)S(6)} %eq.39), kind=kOutput, calls=%fused_computation.21 | convolution fusion | flops 100696064 | bytes 1441793 | tf_op jit(solution)/shard_map/dot_general | solution.py:10
  74.0 1.3 %collective-permute-start.14 = (f32[64,512]{1,0:T(8,128)}, f32[64,512]{1,0:T(8,128)S(1)}, u32[]{:S(2)}, u32[]{:S(2)}) collective-permute-start(f32[64,512]{1,0:T(8,128)} %fusion.20), channel_id=1, source_target_pairs={{2,1},{6,5},{10,9},{14,13},{18,17},{22,21},{26,25},{30,29},{34,33}... | collective-permute-start | bytes 393224 | tf_op jit(solution)/shard_map/ppermute | solution.py:29
  75.3 1.3 %fusion.2 = f32[64,512]{1,0:T(8,128)} fusion(f32[1024,512]{1,0:T(8,128)S(1)} %copy-done.1, f32[64,512]{1,0:T(8,128)S(1)} %collective-permute-done.12, f32[64,512]{1,0:T(8,128)S(1)} %collective-permute-done.13, pred[]{:T(512)S(6)} %eq.39), kind=kOutput, calls=%fused_computation.3 | convolution fusion | flops 100696064 | bytes 1441793 | tf_op jit(solution)/shard_map/dot_general | solution.py:10
  76.6 1.3 %collective-permute-start.15 = (f32[64,512]{1,0:T(8,128)}, f32[64,512]{1,0:T(8,128)S(1)}, u32[]{:S(2)}, u32[]{:S(2)}) collective-permute-start(f32[64,512]{1,0:T(8,128)} %fusion.2), channel_id=1, source_target_pairs={{2,3},{6,7},{10,11},{14,15},{18,19},{22,23},{26,27},{30,31},{34,35... | collective-permute-start | bytes 393224 | tf_op jit(solution)/shard_map/ppermute | solution.py:31
  77.9 0.0 collective-permute-done.14
  77.9 2.2 %collective-permute-done.15 = f32[64,512]{1,0:T(8,128)S(1)} collective-permute-done((f32[64,512]{1,0:T(8,128)}, f32[64,512]{1,0:T(8,128)S(1)}, u32[]{:S(2)}, u32[]{:S(2)}) %collective-permute-start.15) | collective-permute-done | bytes 131104 | tf_op jit(solution)/shard_map/ppermute | solution.py:31
  80.1 0.6 fusion.18
  80.8 1.3 %collective-permute-start.16 = (f32[64,512]{1,0:T(8,128)S(1)}, f32[64,512]{1,0:T(8,128)S(1)}, u32[]{:S(2)}, u32[]{:S(2)}) collective-permute-start(f32[64,512]{1,0:T(8,128)S(1)} %fusion.18), channel_id=1, source_target_pairs={{1,0},{3,2},{5,4},{7,6},{9,8},{11,10},{13,12},{15,14},{17,16},{19,... | collective-permute-start | bytes 393224 | tf_op jit(solution)/shard_map/ppermute | solution.py:34
  82.0 0.6 fusion
  82.7 4.3 %collective-permute-done.16 = f32[64,512]{1,0:T(8,128)S(1)} collective-permute-done((f32[64,512]{1,0:T(8,128)S(1)}, f32[64,512]{1,0:T(8,128)S(1)}, u32[]{:S(2)}, u32[]{:S(2)}) %collective-permute-start.16) | collective-permute-done | bytes 131104 | tf_op jit(solution)/shard_map/ppermute | solution.py:34
  87.0 1.3 %convolution_bitcast_fusion = f32[512,64]{0,1:T(8,128)} fusion(f32[512,512]{1,0:T(8,128)S(1)} %copy-done, f32[64,512]{1,0:T(8,128)S(1)} %collective-permute-done.16, f32[64,512]{1,0:T(8,128)S(1)} %fusion, pred[]{:T(512)S(6)} %eq.37), kind=kOutput, calls=%fused_computation | convolution fusion | flops 100696064 | bytes 1441793 | tf_op jit(solution)/shard_map/dot_general | solution.py:10
  (9 shorter events, 0.0 us)
Async XLA Ops:
  0.0 87.0 %copy-start = (f32[512,512]{1,0:T(8,128)S(1)}, f32[512,512]{1,0:T(8,128)}, u32[]{:S(2)}) copy-start(f32[512,512]{1,0:T(8,128)} %param.4) | copy-start | bytes 3145732
  0.0 6.0 %copy-start.1 = (f32[1024,512]{1,0:T(8,128)S(1)}, f32[1024,512]{1,0:T(8,128)}, u32[]{:S(2)}) copy-start(f32[1024,512]{1,0:T(8,128)} %param.3) | copy-start | bytes 6291460
  2.0 3.9 %collective-permute-start = (f32[64,512]{1,0:T(8,128)S(1)}, f32[64,512]{1,0:T(8,128)S(1)}, u32[]{:S(2)}, u32[]{:S(2)}) collective-permute-start(f32[64,512]{1,0:T(8,128)S(1)} %fusion.34), channel_id=1, source_target_pairs={{256,128}} | collective-permute-start | bytes 393224 | tf_op jit(solution)/shard_map/ppermute | solution.py:29
  5.3 0.7 collective-permute-start.1
  7.3 2.6 %collective-permute-start.2 = (f32[64,512]{1,0:T(8,128)}, f32[64,512]{1,0:T(8,128)S(1)}, u32[]{:S(2)}, u32[]{:S(2)}) collective-permute-start(f32[64,512]{1,0:T(8,128)} %fusion.32), channel_id=1, source_target_pairs={{128,64},{384,320}} | collective-permute-start | bytes 393224 | tf_op jit(solution)/shard_map/ppermute | solution.py:29
  9.2 0.7 collective-permute-start.3
  11.2 2.6 %collective-permute-start.4 = (f32[64,512]{1,0:T(8,128)}, f32[64,512]{1,0:T(8,128)S(1)}, u32[]{:S(2)}, u32[]{:S(2)}) collective-permute-start(f32[64,512]{1,0:T(8,128)} %fusion.30), channel_id=1, source_target_pairs={{64,32},{192,160},{320,288},{448,416}} | collective-permute-start | bytes 393224 | tf_op jit(solution)/shard_map/ppermute | solution.py:29
  13.2 0.7 collective-permute-start.5
  15.1 2.6 %collective-permute-start.6 = (f32[64,512]{1,0:T(8,128)}, f32[64,512]{1,0:T(8,128)S(1)}, u32[]{:S(2)}, u32[]{:S(2)}) collective-permute-start(f32[64,512]{1,0:T(8,128)} %fusion.28), channel_id=1, source_target_pairs={{32,16},{96,80},{160,144},{224,208},{288,272},{352,336},{416,400},... | collective-permute-start | bytes 393224 | tf_op jit(solution)/shard_map/ppermute | solution.py:29
  17.1 0.7 collective-permute-start.7
  19.1 2.6 %collective-permute-start.8 = (f32[64,512]{1,0:T(8,128)}, f32[64,512]{1,0:T(8,128)S(1)}, u32[]{:S(2)}, u32[]{:S(2)}) collective-permute-start(f32[64,512]{1,0:T(8,128)} %fusion.26), channel_id=1, source_target_pairs={{16,8},{48,40},{80,72},{112,104},{144,136},{176,168},{208,200},{24... | collective-permute-start | bytes 393224 | tf_op jit(solution)/shard_map/ppermute | solution.py:29
  21.0 0.7 collective-permute-start.9
  23.0 2.6 %collective-permute-start.10 = (f32[64,512]{1,0:T(8,128)}, f32[64,512]{1,0:T(8,128)S(1)}, u32[]{:S(2)}, u32[]{:S(2)}) collective-permute-start(f32[64,512]{1,0:T(8,128)} %fusion.24), channel_id=1, source_target_pairs={{8,4},{24,20},{40,36},{56,52},{72,68},{88,84},{104,100},{120,116},... | collective-permute-start | bytes 393224 | tf_op jit(solution)/shard_map/ppermute | solution.py:29
  24.9 0.7 collective-permute-start.11
  26.9 3.3 %collective-permute-start.12 = (f32[64,512]{1,0:T(8,128)}, f32[64,512]{1,0:T(8,128)S(1)}, u32[]{:S(2)}, u32[]{:S(2)}) collective-permute-start(f32[64,512]{1,0:T(8,128)} %fusion.22), channel_id=1, source_target_pairs={{4,2},{12,10},{20,18},{28,26},{36,34},{44,42},{52,50},{60,58},{68,... | collective-permute-start | bytes 393224 | tf_op jit(solution)/shard_map/ppermute | solution.py:29
  28.9 43.9 %collective-permute-start.13 = (f32[64,512]{1,0:T(8,128)}, f32[64,512]{1,0:T(8,128)S(1)}, u32[]{:S(2)}, u32[]{:S(2)}) collective-permute-start(f32[64,512]{1,0:T(8,128)} %fusion.4), channel_id=1, source_target_pairs={{4,6},{12,14},{20,22},{28,30},{36,38},{44,46},{52,54},{60,62},{68,... | collective-permute-start | bytes 393224 | tf_op jit(solution)/shard_map/ppermute | solution.py:31
  74.0 3.9 %collective-permute-start.14 = (f32[64,512]{1,0:T(8,128)}, f32[64,512]{1,0:T(8,128)S(1)}, u32[]{:S(2)}, u32[]{:S(2)}) collective-permute-start(f32[64,512]{1,0:T(8,128)} %fusion.20), channel_id=1, source_target_pairs={{2,1},{6,5},{10,9},{14,13},{18,17},{22,21},{26,25},{30,29},{34,33}... | collective-permute-start | bytes 393224 | tf_op jit(solution)/shard_map/ppermute | solution.py:29
  76.6 3.5 %collective-permute-start.15 = (f32[64,512]{1,0:T(8,128)}, f32[64,512]{1,0:T(8,128)S(1)}, u32[]{:S(2)}, u32[]{:S(2)}) collective-permute-start(f32[64,512]{1,0:T(8,128)} %fusion.2), channel_id=1, source_target_pairs={{2,3},{6,7},{10,11},{14,15},{18,19},{22,23},{26,27},{30,31},{34,35... | collective-permute-start | bytes 393224 | tf_op jit(solution)/shard_map/ppermute | solution.py:31
  80.8 6.3 %collective-permute-start.16 = (f32[64,512]{1,0:T(8,128)S(1)}, f32[64,512]{1,0:T(8,128)S(1)}, u32[]{:S(2)}, u32[]{:S(2)}) collective-permute-start(f32[64,512]{1,0:T(8,128)S(1)} %fusion.18), channel_id=1, source_target_pairs={{1,0},{3,2},{5,4},{7,6},{9,8},{11,10},{13,12},{15,14},{17,16},{19,... | collective-permute-start | bytes 393224 | tf_op jit(solution)/shard_map/ppermute | solution.py:34

commit v2 on v1

v2 whole, which is shorter than its diff:
```python
import functools

import jax
import jax.numpy as jnp
from jax import lax
from jax.experimental import pallas as pl
from jax.experimental.pallas import tpu as pltpu
from jax.sharding import PartitionSpec as P

AXES = ("wide", "narrow")
Y, Z, CORES, X = 4, 16, 2, 4
SNAPS, MODES = 512, 64


def at(y, z, core, x):
    return ((y * Z + z) * CORES + core) * X + x


EVERY = [(y, z, core, x) for y in range(Y) for z in range(Z) for core in range(CORES) for x in range(X)]


def split(value):
    high = value.astype(jnp.bfloat16)
    return high, (value - high.astype(jnp.float32)).astype(jnp.bfloat16)


def times(coefficient, factor):
    dims = (((1,), (1,)), ((), ()))
    c_high, c_low = split(coefficient)
    f_high, f_low = split(factor)
    both = lax.dot_general(
        jnp.concatenate([c_high, c_low], 0), f_high, dims, preferred_element_type=jnp.float32
    )
    cross = lax.dot_general(c_high, f_low, dims, preferred_element_type=jnp.float32)
    return both[:MODES] + (both[MODES:] + cross)


def chain_kernel(plan, pick_ref, *refs):
    n_coefs, steps, ends, n_near, n_far = plan
    coefs, near, far, outs, scratch = (
        refs[sum(plan_sizes[:i]):sum(plan_sizes[:i + 1])]
        for plan_sizes in [(n_coefs, n_near, n_far, len(ends), len(refs) - n_coefs - n_near - n_far - len(ends))]
        for i in range(5)
    )
    held = scratch[0]

    def block(which):
        operand, half = which
        return near[operand][half * SNAPS:(half + 1) * SNAPS, :]

    @pl.when(pick_ref[0] >= 0)
    def _():
        fetches = {}
        for s, choices in enumerate(steps):
            for i, (operand, half) in enumerate(choices):
                if operand >= n_near:
                    fetches[s, i] = pltpu.make_async_copy(
                        far[operand - n_near], scratch[1].at[s], scratch[2].at[s]
                    )
                    pl.when(pick_ref[s + 1] == i)(fetches[s, i].start)
        for i, coef in enumerate(coefs):
            @pl.when(pick_ref[0] == i)
            def _():
                held[...] = coef[...]
        for s, choices in enumerate(steps):
            for i, which in enumerate(choices):
                @pl.when(pick_ref[s + 1] == i)
                def _():
                    if (s, i) in fetches:
                        fetches[s, i].wait()
                        held[...] = times(held[...], scratch[1][s])
                    else:
                        held[...] = times(held[...], block(which))
        for out, which in zip(outs, ends):
            out[...] = held[...] if which is None else times(held[...], block(which))


def chain(picks, coefs, near, far, steps, ends):
    vmem = pl.BlockSpec(memory_space=pltpu.VMEM)
    plan = (len(coefs), tuple(map(tuple, steps)), tuple(ends), len(near), len(far))
    result = jax.ShapeDtypeStruct((MODES, SNAPS), jnp.float32)
    scratch = [pltpu.VMEM((MODES, SNAPS), jnp.float32)]
    if far:
        scratch += [pltpu.VMEM((len(steps), SNAPS, SNAPS), jnp.float32), pltpu.SemaphoreType.DMA((len(steps),))]
    return pl.pallas_call(
        functools.partial(chain_kernel, plan),
        out_shape=[result] * len(ends),
        in_specs=[pl.BlockSpec(memory_space=pltpu.SMEM)] + [vmem] * (len(coefs) + len(near))
        + [pl.BlockSpec(memory_space=pl.ANY)] * len(far),
        out_specs=[vmem] * len(ends),
        scratch_shapes=scratch,
        compiler_params=pltpu.CompilerParams(vmem_limit_bytes=16 << 20),
        cost_estimate=pl.CostEstimate(flops=0, bytes_accessed=0, transcendentals=0),
    )(jnp.stack([jnp.asarray(p, jnp.int32) for p in picks]), *coefs, *near, *far)


def choose(*cases):
    picked = jnp.int32(-1)
    for i in reversed(range(len(cases))):
        picked = jnp.where(cases[i], jnp.int32(i), picked)
    return picked


def send(block, route):
    return lax.ppermute(block, AXES, route)


def on_device(node_factors, leaf_q, modal_basis):
    wide, x = lax.axis_index("wide"), lax.axis_index("narrow")
    core, z, y = wide % CORES, (wide // CORES) % Z, wide // (CORES * Z)
    trunk = (core == 0) & (x == 0)
    U, L = 0, 1

    up, low = chain(
        [choose(trunk & (z == 0) & (y == 2))], [modal_basis.T], [node_factors], [], [], [(0, U), (0, L)]
    )
    to_y1 = send(up, [(at(2, 0, 0, 0), at(1, 0, 0, 0))])
    to_y3 = send(low, [(at(2, 0, 0, 0), at(3, 0, 0, 0))])

    factors, up, low = lax.optimization_barrier((node_factors, up, low))
    upper = factors[:SNAPS]
    other = lax.dynamic_slice_in_dim(factors, jnp.where((core == 1) & (x == 0), 0, SNAPS), SNAPS)
    late = (4, 6, 12)
    early_a = send(
        upper,
        [(at(y, z, c, x), at(y, z, c, x - 1)) for y, z, c, x in EVERY if x >= 2]
        + [(at(y, 8, 0, 0), at(y, 4, 0, 0)) for y in range(Y)]
        + [(at(y, z + 1, 0, 0), at(y, z, 0, 0)) for y in range(Y) for z in range(0, Z, 2) if z not in late]
        + [(at(y, 12, 1, 0), at(y, 12, 0, 0)) for y in range(Y)],
    )
    early_b = send(
        other,
        [(at(y, z, c, 2), at(y, z, c, 3)) for y, z, c, x in EVERY if x == 2]
        + [(at(y, 8, 0, 0), at(y, 12, 0, 0)) for y in range(Y)]
        + [(at(y, z, 1, 0), at(y, z, 0, 0)) for y in range(Y) for z in range(Z) if z != 12],
    )
    early_c = send(upper, [(at(y, z + 1, 0, 0), at(y, z, 0, 0)) for y in range(Y) for z in late])

    up, low = chain(
        [choose(trunk & (z == 0) & (y == 1), trunk & (z == 0) & (y == 3))],
        [to_y1, to_y3], [node_factors], [], [], [(0, U), (0, L)],
    )
    c7 = [
        send(half, [(at(y, 0, 0, 0), at(y - 1 + k, zt, 0, 0)) for y in (1, 3)])
        for k, half in enumerate((up, low)) for zt in (4, 12)
    ]
    *c7, early_a, early_b = lax.optimization_barrier((*c7, early_a, early_b))
    z4, z12, y_low = trunk & (z == 4), trunk & (z == 12), y % 2 == 0
    up, low = chain(
        [choose(z4 & y_low, z12 & y_low, z4 & ~y_low, z12 & ~y_low), choose(z4, z12)],
        c7, [node_factors], [early_a, early_b], [[(1, 0), (2, 0)]], [(0, U), (0, L)],
    )
    c5 = [
        send(half, [(at(y, z, 0, 0), at(y, z + step, 0, 0)) for y in range(Y) for z in (4, 12)])
        for half, step in ((up, -2), (low, 2))
    ]
    up, low = chain(
        [choose(trunk & (z % 8 == 2), trunk & (z % 8 == 6))], c5, [node_factors], [], [], [(0, U), (0, L)]
    )
    c4 = [
        send(half, [(at(y, z, 0, 0), at(y, z + step, 0, 0)) for y in range(Y) for z in range(2, Z, 4)])
        for half, step in ((up, -2), (up, -1), (low, 1))
    ]
    is_late = (z == late[0]) | (z == late[1]) | (z == late[2])
    (c3,) = chain(
        [choose(*[trunk & (z % 4 == k) for k in (0, 1, 3, 2)]), choose(z % 2 == 1, is_late, z % 2 == 0)],
        c4 + [low], [node_factors], [early_a, early_c], [[(0, L), (2, 0), (1, 0)]], [None],
    )
    over = send(c3, [(at(y, z, 0, 0), at(y, z, 1, 0)) for y in range(Y) for z in range(Z)])
    (c2,) = chain(
        [choose((core == 0) & (x == 0), (core == 1) & (x == 0)), choose(core == 1, z == 12, z != 12)],
        [c3, over], [node_factors], [early_a, early_b], [[(0, L), (1, 0), (2, 0)]], [None],
    )
    spread = [
        send(c2, [(at(y, z, c, 0), at(y, z, c, xt)) for y, z, c, x in EVERY if x == 0])
        for xt in (1, 2, 3)
    ]
    c1, first = chain(
        [choose(x == 1), choose(x == 1)], spread[:1], [node_factors], [early_a], [[(1, 0)]], [None, (0, U)]
    )
    first = send(first, [(at(y, z, c, 1), at(y, z, c, 0)) for y, z, c, x in EVERY if x == 0])
    (modes,) = chain(
        [choose(x == 1, x == 2, x == 3), choose(x == 2, x == 3), choose(x % 2 == 1, x == 2)],
        [c1] + spread[1:], [node_factors, leaf_q], [early_a, early_b],
        [[(0, L), (3, 0)], [(0, L), (2, 0)]], [(1, 0)],
    )
    (modes,) = chain(
        [choose(x == 0, x != 0), choose(x == 0)], [first, modes], [leaf_q], [], [[(0, 0)]], [None],
    )
    return modes.T


def solution(mesh):
    return jax.shard_map(
        on_device,
        mesh=mesh,
        in_specs=(P(AXES, None), P(AXES, None), P()),
        out_specs=P(AXES, None),
        check_vma=False,
    )
```

time: 88.6 us -> 79.2 us (0.89)
  the two profiles are of different devices: /device:TPU:93 before, /device:TPU:24 now
where the time goes in v2:
time: 79.2 us; the launch traced here: 78.6 us
  starting transfers between devices  28.1 us (35%)
  waiting for transfers between devices  27.9 us (35%)
  Pallas kernels  12.4 us (16%)
  local copies, waits for them, and re-layouts  9.34 us (12%)
    ppermute x19, starting transfers between devices, send(): return lax.ppermute(block, AXES, route)  28.1 us
    ppermute x19, waiting for transfers between devices, send(): return lax.ppermute(block, AXES, route)  27.9 us
    pallas_call x9, Pallas kernels, chain(): pl.pallas_call(functools.partial(chain_kernel, plan), out_shape=[result]...  12.4 us
    unnamed x16, local copies, waits for them, and re-layouts  7.81 us
  transfers between devices with their start and end apart: 19, of which 7 were waited for; matrix products, arithmetic and copies ran while one was open for 1% of the time, Pallas kernels for 8%

profile of v2, /device:TPU:24, one launch (start us, length us, event | category | flops | bytes accessed | tf_op | source)
XLA Modules:
  0.0 78.6 jit_solution(9432506111078485916)
XLA Ops:
  0.0 1.6 %copy-done = f32[1024,512]{1,0:T(8,128)S(1)} copy-done((f32[1024,512]{1,0:T(8,128)S(1)}, f32[1024,512]{1,0:T(8,128)}, u32[]{:S(2)}) %copy-start) | copy-done | bytes 2097176
  1.6 0.9 %copy-done.3 = f32[512,64]{0,1:T(8,128)S(1)} copy-done((f32[512,64]{0,1:T(8,128)S(1)}, f32[512,64]{0,1:T(8,128)}, u32[]{:S(2)}) %copy-start.3) | copy-done | bytes 131096
  2.5 0.7 shard_map.37
  3.2 1.0 %copy-done.1 = f32[1024,512]{1,0:T(8,128)S(1)} copy-done((f32[1024,512]{1,0:T(8,128)S(1)}, f32[1024,512]{1,0:T(8,128)}, u32[]{:S(2)}) %copy-start.1) | copy-done | bytes 2097176
  4.1 1.5 %constant_dynamic-slice_fusion = (f32[512,512]{1,0:T(8,128)}, f32[512,512]{1,0:T(8,128)}) fusion(f32[1024,512]{1,0:T(8,128)S(1)} %copy-done.1, s32[]{:T(128)S(6)} %select_n.191), kind=kLoop, calls=%fused_computation.6 | loop fusion | bytes 4194308 | tf_op jit(solution)/shard_map/dynamic_slice | solution.py:122
  5.7 1.3 %collective-permute-start.7 = (f32[512,512]{1,0:T(8,128)}, f32[512,512]{1,0:T(8,128)}, u32[]{:S(2)}, u32[]{:S(2)}) collective-permute-start(f32[512,512]{1,0:T(8,128)} %get-tuple-element.39), channel_id=1, source_target_pairs={{2,3},{6,7},{10,11},{14,15},{18,19},{22,23},{26,27},{30,31},{34,35... | collective-permute-start | bytes 3145736 | tf_op jit(solution)/shard_map/ppermute | solution.py:105
  7.0 1.3 %collective-permute-start.6 = (f32[512,512]{1,0:T(8,128)}, f32[512,512]{1,0:T(8,128)S(1)}, u32[]{:S(2)}, u32[]{:S(2)}) collective-permute-start(f32[512,512]{1,0:T(8,128)} %get-tuple-element.40), channel_id=1, source_target_pairs={{2,1},{3,2},{6,5},{7,6},{10,9},{11,10},{14,13},{15,14},{18,17},{19... | collective-permute-start | bytes 3145736 | tf_op jit(solution)/shard_map/ppermute | solution.py:105
  8.3 1.7 %collective-permute-start.13 = (f32[512,512]{1,0:T(8,128)}, f32[512,512]{1,0:T(8,128)}, u32[]{:S(2)}, u32[]{:S(2)}) collective-permute-start(f32[512,512]{1,0:T(8,128)} %get-tuple-element.40), channel_id=1, source_target_pairs={{40,32},{56,48},{104,96},{168,160},{184,176},{232,224},{296,288},{... | collective-permute-start | bytes 3145736 | tf_op jit(solution)/shard_map/ppermute | solution.py:105
  9.9 0.7 collective-permute-start
  10.6 1.3 %collective-permute-start.1 = (f32[64,512]{1,0:T(8,128)S(1)}, f32[64,512]{1,0:T(8,128)S(1)}, u32[]{:S(2)}, u32[]{:S(2)}) collective-permute-start(f32[64,512]{1,0:T(8,128)S(1)} %get-tuple-element.23), channel_id=1, source_target_pairs={{256,384}} | collective-permute-start | bytes 393224 | tf_op jit(solution)/shard_map/ppermute | solution.py:105
  11.9 5.5 %collective-permute-done.1.refs_1_ = f32[64,512]{1,0:T(8,128)S(1)} collective-permute-done((f32[64,512]{1,0:T(8,128)S(1)}, f32[64,512]{1,0:T(8,128)S(1)}, u32[]{:S(2)}, u32[]{:S(2)}) %collective-permute-start.1) | collective-permute-done | bytes 131104 | tf_op jit(solution)/shard_map/ppermute | solution.py:105
  17.4 1.5 %shard_map.38 = (f32[64,512]{1,0:T(8,128)S(1)}, f32[64,512]{1,0:T(8,128)}) custom-call(s32[1]{0:T(128)} %bitcast.10.pick_ref, f32[64,512]{1,0:T(8,128)S(1)} %collective-permute-done.refs_0_, f32[64,512]{1,0:T(8,128)S(1)} %collective-permute-done.1.refs_1_, f32[1024,512]{1,0:T(8,128)S(1)} %copy-done.1), custom_call_target="tpu_custom_call" | custom-call | tf_op jit(solution)/shard_map/pallas_call | solution.py:85
  18.9 5.6 %collective-permute-start.3 = (f32[64,512]{1,0:T(8,128)S(1)}, f32[64,512]{1,0:T(8,128)S(1)}, u32[]{:S(2)}, u32[]{:S(2)}) collective-permute-start(f32[64,512]{1,0:T(8,128)S(1)} %get-tuple-element.24), channel_id=1, source_target_pairs={{128,96},{384,352}} | collective-permute-start | bytes 393224 | tf_op jit(solution)/shard_map/ppermute | solution.py:105
  24.5 1.3 %collective-permute-start.2 = (f32[64,512]{1,0:T(8,128)S(1)}, f32[64,512]{1,0:T(8,128)S(1)}, u32[]{:S(2)}, u32[]{:S(2)}) collective-permute-start(f32[64,512]{1,0:T(8,128)S(1)} %get-tuple-element.24), channel_id=1, source_target_pairs={{128,32},{384,288}} | collective-permute-start | bytes 393224 | tf_op jit(solution)/shard_map/ppermute | solution.py:105
  25.8 1.2 %collective-permute-done.3.refs_1_ = f32[64,512]{1,0:T(8,128)S(1)} collective-permute-done((f32[64,512]{1,0:T(8,128)S(1)}, f32[64,512]{1,0:T(8,128)S(1)}, u32[]{:S(2)}, u32[]{:S(2)}) %collective-permute-start.3) | collective-permute-done | bytes 131104 | tf_op jit(solution)/shard_map/ppermute | solution.py:105
  27.0 1.3 %collective-permute-start.5 = (f32[64,512]{1,0:T(8,128)}, f32[64,512]{1,0:T(8,128)S(1)}, u32[]{:S(2)}, u32[]{:S(2)}) collective-permute-start(f32[64,512]{1,0:T(8,128)} %get-tuple-element.25), channel_id=1, source_target_pairs={{128,224},{384,480}} | collective-permute-start | bytes 393224 | tf_op jit(solution)/shard_map/ppermute | solution.py:105
  28.3 2.0 %collective-permute-start.4 = (f32[64,512]{1,0:T(8,128)}, f32[64,512]{1,0:T(8,128)}, u32[]{:S(2)}, u32[]{:S(2)}) collective-permute-start(f32[64,512]{1,0:T(8,128)} %get-tuple-element.25), channel_id=1, source_target_pairs={{128,160},{384,416}} | collective-permute-start | bytes 393224 | tf_op jit(solution)/shard_map/ppermute | solution.py:105
  30.3 0.1 pad_add_fusion.4.pick_ref
  30.4 0.8 collective-permute-done.5.refs_3_
  31.1 1.3 %collective-permute-done.4.refs_2_ = f32[64,512]{1,0:T(8,128)} collective-permute-done((f32[64,512]{1,0:T(8,128)}, f32[64,512]{1,0:T(8,128)}, u32[]{:S(2)}, u32[]{:S(2)}) %collective-permute-start.4) | collective-permute-done | bytes 131104 | tf_op jit(solution)/shard_map/ppermute | solution.py:105
  32.4 1.6 %shard_map.39 = (f32[64,512]{1,0:T(8,128)}, f32[64,512]{1,0:T(8,128)}) custom-call(s32[2]{0:T(128)S(1)} %pad_add_fusion.4.pick_ref, f32[64,512]{1,0:T(8,128)S(1)} %collective-permute-done.2.refs_0_, f32[64,512]{1,0:T(8,128)S(1)} %collective-permute-done.3.refs_1_, f32[64,512]{1,0:T(8,128)} %collective-permute-done.4.refs_2_, ...), custom_call_target="tpu_custom_call" | custom-call | tf_op jit(solution)/shard_map/pallas_call | solution.py:85
  34.1 0.7 collective-permute-start.8
  34.8 0.7 collective-permute-start.9
  35.5 0.7 shard_map.40
  36.2 0.7 collective-permute-start.11
  36.8 1.3 %collective-permute-start.10 = (f32[64,512]{1,0:T(8,128)}, f32[64,512]{1,0:T(8,128)S(1)}, u32[]{:S(2)}, u32[]{:S(2)}) collective-permute-start(f32[64,512]{1,0:T(8,128)} %get-tuple-element.35), channel_id=1, source_target_pairs={{16,0},{48,32},{80,64},{112,96},{144,128},{176,160},{208,192},{240... | collective-permute-start | bytes 393224 | tf_op jit(solution)/shard_map/ppermute | solution.py:105
  38.1 1.3 %collective-permute-start.12 = (f32[64,512]{1,0:T(8,128)S(1)}, f32[64,512]{1,0:T(8,128)}, u32[]{:S(2)}, u32[]{:S(2)}) collective-permute-start(f32[64,512]{1,0:T(8,128)S(1)} %get-tuple-element.36.refs_3_), channel_id=1, source_target_pairs={{16,24},{48,56},{80,88},{112,120},{144,152},{176,184},{208,216},{2... | collective-permute-start | bytes 393224 | tf_op jit(solution)/shard_map/ppermute | solution.py:105
  39.5 15.1 %collective-permute-done.10.refs_0_ = f32[64,512]{1,0:T(8,128)S(1)} collective-permute-done((f32[64,512]{1,0:T(8,128)}, f32[64,512]{1,0:T(8,128)S(1)}, u32[]{:S(2)}, u32[]{:S(2)}) %collective-permute-start.10) | collective-permute-done | bytes 131104 | tf_op jit(solution)/shard_map/ppermute | solution.py:105
  54.7 0.7 copy-done.4
  55.3 0.9 %copy-done.5 = f32[64,512]{1,0:T(8,128)S(1)} copy-done((f32[64,512]{1,0:T(8,128)S(1)}, f32[64,512]{1,0:T(8,128)}, u32[]{:S(2)}) %copy-start.5) | copy-done | bytes 131096
  56.2 1.5 %shard_map.41.refs_0_ = f32[64,512]{1,0:T(8,128)S(1)} custom-call(s32[2]{0:T(128)S(1)} %pad_add_fusion.3.pick_ref, f32[64,512]{1,0:T(8,128)S(1)} %copy-done.5, f32[64,512]{1,0:T(8,128)S(1)} %collective-permute-done.11.refs_1_, f32[64,512]{1,0:T(8,128)} %collective-permute-done.12.refs_2_, f32[64,512]{1,0:T(8,128)S(1)} %get-tuple-element.36.refs_3_, ...), custom_call_target="tpu_custom_call" | custom-call | tf_op jit(solution)/shard_map/pallas_call | solution.py:85
  57.8 1.3 %collective-permute-start.14 = (f32[64,512]{1,0:T(8,128)S(1)}, f32[64,512]{1,0:T(8,128)S(1)}, u32[]{:S(2)}, u32[]{:S(2)}) collective-permute-start(f32[64,512]{1,0:T(8,128)S(1)} %shard_map.41.refs_0_), channel_id=1, source_target_pairs={{0,4},{8,12},{16,20},{24,28},{32,36},{40,44},{48,52},{56,60},{64,6... | collective-permute-start | bytes 393224 | tf_op jit(solution)/shard_map/ppermute | solution.py:105
  59.1 0.1 pad_add_fusion.2.pick_ref
  59.2 0.9 %collective-permute-done.14.refs_1_ = f32[64,512]{1,0:T(8,128)S(1)} collective-permute-done((f32[64,512]{1,0:T(8,128)S(1)}, f32[64,512]{1,0:T(8,128)S(1)}, u32[]{:S(2)}, u32[]{:S(2)}) %collective-permute-start.14) | collective-permute-done | bytes 131104 | tf_op jit(solution)/shard_map/ppermute | solution.py:105
  60.0 2.3 %shard_map.42 = f32[64,512]{1,0:T(8,128)S(1)} custom-call(s32[2]{0:T(128)S(1)} %pad_add_fusion.2.pick_ref, f32[64,512]{1,0:T(8,128)S(1)} %shard_map.41.refs_0_, f32[64,512]{1,0:T(8,128)S(1)} %collective-permute-done.14.refs_1_, f32[1024,512]{1,0:T(8,128)S(1)} %copy-done.1, f32[512,512]{1,0:T(8,128)S(1)} %collective-permute-done.6.refs_5_.refs_3_.refs_2_, ...), custom_call_target="tpu_custom_call" | custom-call | tf_op jit(solution)/shard_map/pallas_call | solution.py:85
  62.3 1.9 %collective-permute-start.15 = (f32[64,512]{1,0:T(8,128)S(1)}, f32[64,512]{1,0:T(8,128)}, u32[]{:S(2)}, u32[]{:S(2)}) collective-permute-start(f32[64,512]{1,0:T(8,128)S(1)} %shard_map.42), channel_id=1, source_target_pairs={{0,1},{4,5},{8,9},{12,13},{16,17},{20,21},{24,25},{28,29},{32,33},... | collective-permute-start | bytes 393224 | tf_op jit(solution)/shard_map/ppermute | solution.py:105
  64.3 1.3 %collective-permute-start.18 = (f32[64,512]{1,0:T(8,128)S(1)}, f32[64,512]{1,0:T(8,128)S(1)}, u32[]{:S(2)}, u32[]{:S(2)}) collective-permute-start(f32[64,512]{1,0:T(8,128)S(1)} %shard_map.42), channel_id=1, source_target_pairs={{0,3},{4,7},{8,11},{12,15},{16,19},{20,23},{24,27},{28,31},{32,35}... | collective-permute-start | bytes 393224 | tf_op jit(solution)/shard_map/ppermute | solution.py:105
  65.6 1.3 %collective-permute-start.17 = (f32[64,512]{1,0:T(8,128)S(1)}, f32[64,512]{1,0:T(8,128)S(1)}, u32[]{:S(2)}, u32[]{:S(2)}) collective-permute-start(f32[64,512]{1,0:T(8,128)S(1)} %shard_map.42), channel_id=1, source_target_pairs={{0,2},{4,6},{8,10},{12,14},{16,18},{20,22},{24,26},{28,30},{32,34}... | collective-permute-start | bytes 393224 | tf_op jit(solution)/shard_map/ppermute | solution.py:105
  66.9 1.6 %shard_map.43 = (f32[64,512]{1,0:T(8,128)S(1)}, f32[64,512]{1,0:T(8,128)}) custom-call(s32[2]{0:T(128)S(1)} %pad_add_fusion.1.pick_ref, f32[64,512]{1,0:T(8,128)} %collective-permute-done.15.refs_0_, f32[1024,512]{1,0:T(8,128)S(1)} %copy-done.1, f32[512,512]{1,0:T(8,128)S(1)} %collective-permute-done.6.refs_5_.refs_3_.refs_2_), custom_call_target="tpu_custom_call" | custom-call | tf_op jit(solution)/shard_map/pallas_call | solution.py:85
  68.5 0.6 copy-done.6
  69.2 1.3 %collective-permute-start.16 = (f32[64,512]{1,0:T(8,128)}, f32[64,512]{1,0:T(8,128)}, u32[]{:S(2)}, u32[]{:S(2)}) collective-permute-start(f32[64,512]{1,0:T(8,128)} %get-tuple-element.37), channel_id=1, source_target_pairs={{1,0},{5,4},{9,8},{13,12},{17,16},{21,20},{25,24},{29,28},{33,32},... | collective-permute-start | bytes 393224 | tf_op jit(solution)/shard_map/ppermute | solution.py:105
  70.5 0.1 pad_add_fusion.pick_ref
  70.6 0.1 pad_add_fusion.5.pick_ref
  70.7 1.2 %copy-done.2 = f32[512,512]{1,0:T(8,128)S(1)} copy-done((f32[512,512]{1,0:T(8,128)S(1)}, f32[512,512]{1,0:T(8,128)}, u32[]{:S(2)}) %copy-start.2) | copy-done | bytes 1048600
  71.9 0.9 %copy-done.7 = f32[64,512]{1,0:T(8,128)S(1)} copy-done((f32[64,512]{1,0:T(8,128)S(1)}, f32[64,512]{1,0:T(8,128)}, u32[]{:S(2)}) %copy-start.7) | copy-done | bytes 131096
  72.8 0.6 shard_map.44.refs_1_
  73.4 3.1 %collective-permute-done.16.refs_0_ = f32[64,512]{1,0:T(8,128)} collective-permute-done((f32[64,512]{1,0:T(8,128)}, f32[64,512]{1,0:T(8,128)}, u32[]{:S(2)}, u32[]{:S(2)}) %collective-permute-start.16) | collective-permute-done | bytes 131104 | tf_op jit(solution)/shard_map/ppermute | solution.py:105
  76.5 2.1 %shard_map.45 = f32[64,512]{1,0:T(8,128)} custom-call(s32[2]{0:T(128)S(1)} %pad_add_fusion.pick_ref, f32[64,512]{1,0:T(8,128)} %collective-permute-done.16.refs_0_, f32[64,512]{1,0:T(8,128)S(1)} %shard_map.44.refs_1_, f32[512,512]{1,0:T(8,128)S(1)} %copy-done.2), custom_call_target="tpu_custom_call" | custom-call | tf_op jit(solution)/shard_map/pallas_call | solution.py:85
  (22 shorter events, 0.2 us)
Async XLA Ops:
  0.0 1.6 %copy-start = (f32[1024,512]{1,0:T(8,128)S(1)}, f32[1024,512]{1,0:T(8,128)}, u32[]{:S(2)}) copy-start(f32[1024,512]{1,0:T(8,128)} %refs_3_.1) | copy-start | bytes 6291460
  1.6 0.9 %copy-start.3 = (f32[512,64]{0,1:T(8,128)S(1)}, f32[512,64]{0,1:T(8,128)}, u32[]{:S(2)}) copy-start(f32[512,64]{0,1:T(8,128)} %param.5) | copy-start | bytes 393220
  2.5 1.6 %copy-start.1 = (f32[1024,512]{1,0:T(8,128)S(1)}, f32[1024,512]{1,0:T(8,128)}, u32[]{:S(2)}) copy-start(f32[1024,512]{1,0:T(8,128)} %refs_3_.1) | copy-start | bytes 6291460
  5.7 26.8 %collective-permute-start.7 = (f32[512,512]{1,0:T(8,128)}, f32[512,512]{1,0:T(8,128)}, u32[]{:S(2)}, u32[]{:S(2)}) collective-permute-start(f32[512,512]{1,0:T(8,128)} %get-tuple-element.39), channel_id=1, source_target_pairs={{2,3},{6,7},{10,11},{14,15},{18,19},{22,23},{26,27},{30,31},{34,35... | collective-permute-start | bytes 3145736 | tf_op jit(solution)/shard_map/ppermute | solution.py:105
  7.0 25.5 %collective-permute-start.6 = (f32[512,512]{1,0:T(8,128)}, f32[512,512]{1,0:T(8,128)S(1)}, u32[]{:S(2)}, u32[]{:S(2)}) collective-permute-start(f32[512,512]{1,0:T(8,128)} %get-tuple-element.40), channel_id=1, source_target_pairs={{2,1},{3,2},{6,5},{7,6},{10,9},{11,10},{14,13},{15,14},{18,17},{19... | collective-permute-start | bytes 3145736 | tf_op jit(solution)/shard_map/ppermute | solution.py:105
  8.3 31.3 %collective-permute-start.13 = (f32[512,512]{1,0:T(8,128)}, f32[512,512]{1,0:T(8,128)}, u32[]{:S(2)}, u32[]{:S(2)}) collective-permute-start(f32[512,512]{1,0:T(8,128)} %get-tuple-element.40), channel_id=1, source_target_pairs={{40,32},{56,48},{104,96},{168,160},{184,176},{232,224},{296,288},{... | collective-permute-start | bytes 3145736 | tf_op jit(solution)/shard_map/ppermute | solution.py:105
  9.9 2.0 %collective-permute-start = (f32[64,512]{1,0:T(8,128)}, f32[64,512]{1,0:T(8,128)S(1)}, u32[]{:S(2)}, u32[]{:S(2)}) collective-permute-start(f32[64,512]{1,0:T(8,128)} %get-tuple-element.22), channel_id=1, source_target_pairs={{256,128}} | collective-permute-start | bytes 393224 | tf_op jit(solution)/shard_map/ppermute | solution.py:105
  10.6 6.9 %collective-permute-start.1 = (f32[64,512]{1,0:T(8,128)S(1)}, f32[64,512]{1,0:T(8,128)S(1)}, u32[]{:S(2)}, u32[]{:S(2)}) collective-permute-start(f32[64,512]{1,0:T(8,128)S(1)} %get-tuple-element.23), channel_id=1, source_target_pairs={{256,384}} | collective-permute-start | bytes 393224 | tf_op jit(solution)/shard_map/ppermute | solution.py:105
  18.9 8.1 %collective-permute-start.3 = (f32[64,512]{1,0:T(8,128)S(1)}, f32[64,512]{1,0:T(8,128)S(1)}, u32[]{:S(2)}, u32[]{:S(2)}) collective-permute-start(f32[64,512]{1,0:T(8,128)S(1)} %get-tuple-element.24), channel_id=1, source_target_pairs={{128,96},{384,352}} | collective-permute-start | bytes 393224 | tf_op jit(solution)/shard_map/ppermute | solution.py:105
  24.5 3.8 %collective-permute-start.2 = (f32[64,512]{1,0:T(8,128)S(1)}, f32[64,512]{1,0:T(8,128)S(1)}, u32[]{:S(2)}, u32[]{:S(2)}) collective-permute-start(f32[64,512]{1,0:T(8,128)S(1)} %get-tuple-element.24), channel_id=1, source_target_pairs={{128,32},{384,288}} | collective-permute-start | bytes 393224 | tf_op jit(solution)/shard_map/ppermute | solution.py:105
  27.0 4.1 %collective-permute-start.5 = (f32[64,512]{1,0:T(8,128)}, f32[64,512]{1,0:T(8,128)S(1)}, u32[]{:S(2)}, u32[]{:S(2)}) collective-permute-start(f32[64,512]{1,0:T(8,128)} %get-tuple-element.25), channel_id=1, source_target_pairs={{128,224},{384,480}} | collective-permute-start | bytes 393224 | tf_op jit(solution)/shard_map/ppermute | solution.py:105
  28.3 4.1 %collective-permute-start.4 = (f32[64,512]{1,0:T(8,128)}, f32[64,512]{1,0:T(8,128)}, u32[]{:S(2)}, u32[]{:S(2)}) collective-permute-start(f32[64,512]{1,0:T(8,128)} %get-tuple-element.25), channel_id=1, source_target_pairs={{128,160},{384,416}} | collective-permute-start | bytes 393224 | tf_op jit(solution)/shard_map/ppermute | solution.py:105
  34.1 1.4 %collective-permute-start.8 = (f32[64,512]{1,0:T(8,128)}, f32[64,512]{1,0:T(8,128)S(1)}, u32[]{:S(2)}, u32[]{:S(2)}) collective-permute-start(f32[64,512]{1,0:T(8,128)} %get-tuple-element.33), channel_id=1, source_target_pairs={{32,16},{96,80},{160,144},{224,208},{288,272},{352,336},{416,400},... | collective-permute-start | bytes 393224 | tf_op jit(solution)/shard_map/ppermute | solution.py:105
  34.8 0.7 collective-permute-start.9
  36.2 3.4 %collective-permute-start.11 = (f32[64,512]{1,0:T(8,128)}, f32[64,512]{1,0:T(8,128)S(1)}, u32[]{:S(2)}, u32[]{:S(2)}) collective-permute-start(f32[64,512]{1,0:T(8,128)} %get-tuple-element.35), channel_id=1, source_target_pairs={{16,8},{48,40},{80,72},{112,104},{144,136},{176,168},{208,200},{24... | collective-permute-start | bytes 393224 | tf_op jit(solution)/shard_map/ppermute | solution.py:105
  36.8 17.8 %collective-permute-start.10 = (f32[64,512]{1,0:T(8,128)}, f32[64,512]{1,0:T(8,128)S(1)}, u32[]{:S(2)}, u32[]{:S(2)}) collective-permute-start(f32[64,512]{1,0:T(8,128)} %get-tuple-element.35), channel_id=1, source_target_pairs={{16,0},{48,32},{80,64},{112,96},{144,128},{176,160},{208,192},{240... | collective-permute-start | bytes 393224 | tf_op jit(solution)/shard_map/ppermute | solution.py:105
  38.1 17.2 %collective-permute-start.12 = (f32[64,512]{1,0:T(8,128)S(1)}, f32[64,512]{1,0:T(8,128)}, u32[]{:S(2)}, u32[]{:S(2)}) collective-permute-start(f32[64,512]{1,0:T(8,128)S(1)} %get-tuple-element.36.refs_3_), channel_id=1, source_target_pairs={{16,24},{48,56},{80,88},{112,120},{144,152},{176,184},{208,216},{2... | collective-permute-start | bytes 393224 | tf_op jit(solution)/shard_map/ppermute | solution.py:105
  54.7 0.7 copy-start.4
  55.3 0.9 %copy-start.5 = (f32[64,512]{1,0:T(8,128)S(1)}, f32[64,512]{1,0:T(8,128)}, u32[]{:S(2)}) copy-start(f32[64,512]{1,0:T(8,128)} %copy-done.4) | copy-start | bytes 393220
  57.8 2.3 %collective-permute-start.14 = (f32[64,512]{1,0:T(8,128)S(1)}, f32[64,512]{1,0:T(8,128)S(1)}, u32[]{:S(2)}, u32[]{:S(2)}) collective-permute-start(f32[64,512]{1,0:T(8,128)S(1)} %shard_map.41.refs_0_), channel_id=1, source_target_pairs={{0,4},{8,12},{16,20},{24,28},{32,36},{40,44},{48,52},{56,60},{64,6... | collective-permute-start | bytes 393224 | tf_op jit(solution)/shard_map/ppermute | solution.py:105
  62.3 4.6 %collective-permute-start.15 = (f32[64,512]{1,0:T(8,128)S(1)}, f32[64,512]{1,0:T(8,128)}, u32[]{:S(2)}, u32[]{:S(2)}) collective-permute-start(f32[64,512]{1,0:T(8,128)S(1)} %shard_map.42), channel_id=1, source_target_pairs={{0,1},{4,5},{8,9},{12,13},{16,17},{20,21},{24,25},{28,29},{32,33},... | collective-permute-start | bytes 393224 | tf_op jit(solution)/shard_map/ppermute | solution.py:105
  64.3 6.3 %collective-permute-start.18 = (f32[64,512]{1,0:T(8,128)S(1)}, f32[64,512]{1,0:T(8,128)S(1)}, u32[]{:S(2)}, u32[]{:S(2)}) collective-permute-start(f32[64,512]{1,0:T(8,128)S(1)} %shard_map.42), channel_id=1, source_target_pairs={{0,3},{4,7},{8,11},{12,15},{16,19},{20,23},{24,27},{28,31},{32,35}... | collective-permute-start | bytes 393224 | tf_op jit(solution)/shard_map/ppermute | solution.py:105
  65.6 5.0 %collective-permute-start.17 = (f32[64,512]{1,0:T(8,128)S(1)}, f32[64,512]{1,0:T(8,128)S(1)}, u32[]{:S(2)}, u32[]{:S(2)}) collective-permute-start(f32[64,512]{1,0:T(8,128)S(1)} %shard_map.42), channel_id=1, source_target_pairs={{0,2},{4,6},{8,10},{12,14},{16,18},{20,22},{24,26},{28,30},{32,34}... | collective-permute-start | bytes 393224 | tf_op jit(solution)/shard_map/ppermute | solution.py:105
  68.5 0.7 copy-start.6
  69.2 7.3 %collective-permute-start.16 = (f32[64,512]{1,0:T(8,128)}, f32[64,512]{1,0:T(8,128)}, u32[]{:S(2)}, u32[]{:S(2)}) collective-permute-start(f32[64,512]{1,0:T(8,128)} %get-tuple-element.37), channel_id=1, source_target_pairs={{1,0},{5,4},{9,8},{13,12},{17,16},{21,20},{25,24},{29,28},{33,32},... | collective-permute-start | bytes 393224 | tf_op jit(solution)/shard_map/ppermute | solution.py:105
  70.6 1.2 %copy-start.2 = (f32[512,512]{1,0:T(8,128)S(1)}, f32[512,512]{1,0:T(8,128)}, u32[]{:S(2)}) copy-start(f32[512,512]{1,0:T(8,128)} %refs_2_.7) | copy-start | bytes 3145732
  71.9 0.9 %copy-start.7 = (f32[64,512]{1,0:T(8,128)S(1)}, f32[64,512]{1,0:T(8,128)}, u32[]{:S(2)}) copy-start(f32[64,512]{1,0:T(8,128)} %copy-done.6) | copy-start | bytes 393220

commit v3 on v1

v3 whole, which is shorter than its diff:
```python
import jax
import jax.numpy as jnp
from jax import lax
from jax.experimental import pallas as pl
from jax.experimental.pallas import tpu as pltpu
from jax.sharding import PartitionSpec as P

AXES = ("wide", "narrow")
Y, Z, CORES, X = 4, 16, 2, 4
SNAPS, MODES = 512, 64


def at(y, z, core, x):
    return ((y * Z + z) * CORES + core) * X + x


EVERY = [(y, z, core, x) for y in range(Y) for z in range(Z) for core in range(CORES) for x in range(X)]


def split(value):
    high = value.astype(jnp.bfloat16)
    return high, (value - high.astype(jnp.float32)).astype(jnp.bfloat16)


def times(coefficient, factor):
    dims = (((1,), (1,)), ((), ()))
    c_high, c_low = split(coefficient)
    f_high, f_low = split(factor)
    both = lax.dot_general(
        jnp.concatenate([c_high, c_low], 0), f_high, dims, preferred_element_type=jnp.float32
    )
    cross = lax.dot_general(c_high, f_low, dims, preferred_element_type=jnp.float32)
    return both[:MODES] + (both[MODES:] + cross)


WORK_8, WORK_7 = 20 * 10**9, 20 * 10**9


def place():
    wide, x = lax.axis_index("wide"), lax.axis_index("narrow")
    return wide // (CORES * Z), (wide // CORES) % Z, wide % CORES, x


FACTOR = (SNAPS, SNAPS)
COEF = (MODES, SNAPS)
HBM, VMEM = pl.BlockSpec(memory_space=pltpu.HBM), pl.BlockSpec(memory_space=pltpu.VMEM)


def kernel_call(body, operands, near, outs, scratch, work=0, limit=12):
    return pl.pallas_call(
        body,
        out_shape=[
            pltpu.VMEM(shape, jnp.float32) if keep else jax.ShapeDtypeStruct(shape, jnp.float32)
            for shape, keep in outs
        ],
        in_specs=[VMEM if n else HBM for n in near],
        out_specs=[VMEM if keep else HBM for _, keep in outs],
        scratch_shapes=scratch,
        compiler_params=pltpu.CompilerParams(vmem_limit_bytes=limit << 20),
        cost_estimate=pl.CostEstimate(flops=work, bytes_accessed=0, transcendentals=0),
    )(*operands)


def half(ref, which):
    return ref.at[pl.ds(which * SNAPS, SNAPS), :]


def root_kernel(factors, basis, up, low, own, upper, other, held, sems):
    y, z, core, x = place()
    loads = [pltpu.make_async_copy(half(factors, h), half(own, h), sems.at[h]) for h in (0, 1)]
    root = (y == 2) & (z == 0) & (core == 0) & (x == 0)
    swap = (core == 1) & (x == 0)
    base = pltpu.make_async_copy(basis, held, sems.at[2])
    for load in loads:
        load.start()
    pl.when(root)(base.start)
    cut = pltpu.make_async_copy(half(own, 0), upper, sems.at[3])
    cut_up = pltpu.make_async_copy(half(own, 0), other, sems.at[4])
    cut_low = pltpu.make_async_copy(half(own, 1), other, sems.at[4])
    loads[0].wait()
    cut.start()
    pl.when(swap)(cut_up.start)
    loads[1].wait()
    pl.when(~swap)(cut_low.start)

    @pl.when(root)
    def _():
        base.wait()
        up[...] = times(held[...], own[:SNAPS, :])
        low[...] = times(held[...], own[SNAPS:, :])

    cut.wait()
    cut_low.wait()


def level_8_kernel(from_a, from_b, own, up, low):
    y, z, core, x = place()
    for y_here, coef in ((1, from_a), (3, from_b)):
        @pl.when((y == y_here) & (z == 0) & (core == 0) & (x == 0))
        def _():
            up[...] = times(coef[...], own[:SNAPS, :])
            low[...] = times(coef[...], own[SNAPS:, :])


def level_7_6_kernel(c_0, c_1, c_2, c_3, own, early_a, early_b, up, low, block, held, sem):
    y, z, core, x = place()
    for z_here, source, coefs in ((4, early_a, (c_0, c_2)), (12, early_b, (c_1, c_3))):
        @pl.when((z == z_here) & (core == 0) & (x == 0))
        def _():
            load = pltpu.make_async_copy(source, block, sem)
            load.start()
            for odd, coef in enumerate(coefs):
                @pl.when(y % 2 == odd)
                def _():
                    held[...] = coef[...]
            load.wait()
            held[...] = times(held[...], block[...])
            up[...] = times(held[...], own[:SNAPS, :])
            low[...] = times(held[...], own[SNAPS:, :])


def level_5_kernel(c_left, c_right, own, early_a, early_b, leaf, up, low, kept_a, kept_b, kept_leaf, sems):
    y, z, core, x = place()
    loads = [
        pltpu.make_async_copy(source, target, sems.at[i])
        for i, (source, target) in enumerate(((early_a, kept_a), (early_b, kept_b), (leaf, kept_leaf)))
    ]
    for load in loads:
        load.start()
    for z_here, coef in ((2, c_left), (6, c_right)):
        @pl.when((z % 8 == z_here) & (core == 0) & (x == 0))
        def _():
            up[...] = times(coef[...], own[:SNAPS, :])
            low[...] = times(coef[...], own[SNAPS:, :])
    for load in loads:
        load.wait()


def level_4_kernel(c_0, c_1, c_3, c_own, own, kept_a, early_c, out, held, block, sem):
    y, z, core, x = place()

    @pl.when((core == 0) & (x == 0))
    def _():
        is_late = (z == LATE[0]) | (z == LATE[1]) | (z == LATE[2])
        load = pltpu.make_async_copy(early_c, block, sem)
        pl.when(is_late)(load.start)
        for k, coef in ((0, c_0), (1, c_1), (3, c_3), (2, c_own)):
            @pl.when(z % 4 == k)
            def _():
                held[...] = coef[...]

        @pl.when(z % 2 == 1)
        def _():
            out[...] = times(held[...], own[SNAPS:, :])

        @pl.when(is_late)
        def _():
            load.wait()
            out[...] = times(held[...], block[...])

        @pl.when((z % 2 == 0) & ~is_late)
        def _():
            out[...] = times(held[...], kept_a[...])


def level_3_kernel(here, over, own, kept_a, kept_b, out):
    y, z, core, x = place()

    @pl.when((core == 1) & (x == 0))
    def _():
        out[...] = times(over[...], own[SNAPS:, :])

    @pl.when((core == 0) & (x == 0) & (z == 12))
    def _():
        out[...] = times(here[...], kept_a[...])

    @pl.when((core == 0) & (x == 0) & (z != 12))
    def _():
        out[...] = times(here[...], kept_b[...])


def level_2_kernel(coef, own, kept_a, keep, first):
    y, z, core, x = place()

    @pl.when(x == 1)
    def _():
        keep[...] = times(coef[...], kept_a[...])
        first[...] = times(keep[...], own[:SNAPS, :])


def leaf_kernel(c1, c2_x2, c2_x3, own, kept_a, kept_b, leaf, out, held):
    y, z, core, x = place()

    @pl.when(x == 1)
    def _():
        held[...] = times(c1[...], own[SNAPS:, :])

    @pl.when(x == 2)
    def _():
        held[...] = times(times(c2_x2[...], own[SNAPS:, :]), kept_a[...])

    @pl.when(x == 3)
    def _():
        held[...] = times(times(c2_x3[...], kept_b[...]), own[SNAPS:, :])

    @pl.when(x != 0)
    def _():
        out[...] = times(held[...], leaf[...])


def last_kernel(first, others, leaf, out):
    y, z, core, x = place()

    @pl.when(x == 0)
    def _():
        out[...] = times(first[...], leaf[...])

    @pl.when(x != 0)
    def _():
        out[...] = others[...]


LATE = (4, 6, 12)


def send(block, route):
    return lax.ppermute(block, AXES, route)


def on_device(node_factors, leaf_q, modal_basis):
    DMA = pltpu.SemaphoreType.DMA
    coef, block = pltpu.VMEM(COEF, jnp.float32), pltpu.VMEM(FACTOR, jnp.float32)

    up, low, own, upper, other = kernel_call(
        root_kernel, [node_factors, modal_basis.T], [0, 0],
        [(COEF, 1), (COEF, 1), (node_factors.shape, 1), (FACTOR, 0), (FACTOR, 0)], [coef, DMA((5,))],
        limit=56,
    )
    to_y1 = send(up, [(at(2, 0, 0, 0), at(1, 0, 0, 0))])
    to_y3 = send(low, [(at(2, 0, 0, 0), at(3, 0, 0, 0))])

    early_a = send(
        upper,
        [(at(y, z, c, x), at(y, z, c, x - 1)) for y, z, c, x in EVERY if x >= 2]
        + [(at(y, 8, 0, 0), at(y, 4, 0, 0)) for y in range(Y)]
        + [(at(y, z + 1, 0, 0), at(y, z, 0, 0)) for y in range(Y) for z in range(0, Z, 2) if z not in LATE]
        + [(at(y, 12, 1, 0), at(y, 12, 0, 0)) for y in range(Y)],
    )
    early_b = send(
        other,
        [(at(y, z, c, 2), at(y, z, c, 3)) for y, z, c, x in EVERY if x == 2]
        + [(at(y, 8, 0, 0), at(y, 12, 0, 0)) for y in range(Y)]
        + [(at(y, z, 1, 0), at(y, z, 0, 0)) for y in range(Y) for z in range(Z) if z != 12],
    )
    early_c = send(upper, [(at(y, z + 1, 0, 0), at(y, z, 0, 0)) for y in range(Y) for z in LATE])

    up, low = kernel_call(
        level_8_kernel, [to_y1, to_y3, own], [1, 1, 1], [(COEF, 1), (COEF, 1)], [], WORK_8
    )
    c7 = [
        send(block_, [(at(y, 0, 0, 0), at(y - 1 + k, zt, 0, 0)) for y in (1, 3)])
        for k, block_ in enumerate((up, low)) for zt in (4, 12)
    ]
    *c7, early_a, early_b = lax.optimization_barrier((*c7, early_a, early_b))
    up, low = kernel_call(
        level_7_6_kernel, [*c7, own, early_a, early_b], [1] * 5 + [0] * 2,
        [(COEF, 1), (COEF, 1)], [block, coef, DMA], WORK_7,
    )
    c5 = [
        send(block_, [(at(y, z, 0, 0), at(y, z + step, 0, 0)) for y in range(Y) for z in (4, 12)])
        for block_, step in ((up, -2), (low, 2))
    ]
    up, low, kept_a, kept_b, kept_leaf = kernel_call(
        level_5_kernel, [*c5, own, early_a, early_b, leaf_q], [1] * 3 + [0] * 3,
        [(COEF, 1), (COEF, 1)] + [(FACTOR, 1)] * 3, [DMA((3,))],
    )
    c4 = [
        send(block_, [(at(y, z, 0, 0), at(y, z + step, 0, 0)) for y in range(Y) for z in range(2, Z, 4)])
        for block_, step in ((up, -2), (up, -1), (low, 1))
    ]
    (c3,) = kernel_call(
        level_4_kernel, [*c4, low, own, kept_a, early_c], [1] * 6 + [0], [(COEF, 1)], [coef, block, DMA]
    )
    over = send(c3, [(at(y, z, 0, 0), at(y, z, 1, 0)) for y in range(Y) for z in range(Z)])
    (c2,) = kernel_call(level_3_kernel, [c3, over, own, kept_a, kept_b], [1] * 5, [(COEF, 1)], [])
    spread = [
        send(c2, [(at(y, z, c, 0), at(y, z, c, xt)) for y, z, c, x in EVERY if x == 0])
        for xt in (1, 2, 3)
    ]
    c1, first = kernel_call(
        level_2_kernel, [spread[0], own, kept_a], [1] * 3, [(COEF, 1), (COEF, 1)], []
    )
    first = send(first, [(at(y, z, c, 1), at(y, z, c, 0)) for y, z, c, x in EVERY if x == 0])
    (modes,) = kernel_call(
        leaf_kernel, [c1, *spread[1:], own, kept_a, kept_b, kept_leaf], [1] * 7, [(COEF, 1)], [coef]
    )
    (modes,) = pl.pallas_call(
        last_kernel,
        out_shape=[jax.ShapeDtypeStruct(COEF, jnp.float32)],
        in_specs=[VMEM] * 3,
        out_specs=[VMEM],
        compiler_params=pltpu.CompilerParams(vmem_limit_bytes=12 << 20),
    )(first, modes, kept_leaf)
    return modes.T


def solution(mesh):
    return jax.shard_map(
        on_device,
        mesh=mesh,
        in_specs=(P(AXES, None), P(AXES, None), P()),
        out_specs=P(AXES, None),
        check_vma=False,
    )
```

time: 88.6 us -> 68.2 us (0.77)
  the two profiles are of different devices: /device:TPU:93 before, /device:TPU:24 now
where the time goes in v3:
time: 68.2 us; the launch traced here: 67.7 us
  waiting for transfers between devices  33.1 us (49%)
  starting transfers between devices  28.5 us (42%)
  Pallas kernels  5.76 us (8%)
    ppermute x19, waiting for transfers between devices, send(): return lax.ppermute(block, AXES, route)  33.1 us
    ppermute x19, starting transfers between devices, send(): return lax.ppermute(block, AXES, route)  28.5 us
    pallas_call x8, Pallas kernels, kernel_call(): pl.pallas_call(body, out_shape=[pltpu.VMEM(shape, jnp.float32) if keep el...  4.64 us
  transfers between devices with their start and end apart: 19, of which 8 were waited for; matrix products, arithmetic and copies ran while one was open for 0% of the time, Pallas kernels for 2%

profile of v3, /device:TPU:24, one launch (start us, length us, event | category | flops | bytes accessed | tf_op | source)
XLA Modules:
  0.0 67.7 jit_solution(9234131261734287016)
XLA Ops:
  0.0 2.6 %shard_map.37 = (f32[64,512]{1,0:T(8,128)S(1)}, f32[64,512]{1,0:T(8,128)S(1)}, f32[1024,512]{1,0:T(8,128)S(1)}, f32[512,512]{1,0:T(8,128)}, f32[512,512]{1,0:T(8,128)}) custom-call(f32[1024,512]{1,0:T(8,128)} %factors.1, f32[64,512]{1,0:T(8,128)} %bitcast.2), custom_call_target="tpu_custom_call" | custom-call | tf_op jit(solution)/shard_map/pallas_call | solution.py:50
  2.6 0.7 collective-permute-start
  3.3 1.3 %collective-permute-start.1 = (f32[64,512]{1,0:T(8,128)S(1)}, f32[64,512]{1,0:T(8,128)S(1)}, u32[]{:S(2)}, u32[]{:S(2)}) collective-permute-start(f32[64,512]{1,0:T(8,128)S(1)} %get-tuple-element.28), channel_id=1, source_target_pairs={{256,384}} | collective-permute-start | bytes 393224 | tf_op jit(solution)/shard_map/ppermute | solution.py:227
  4.6 1.3 %collective-permute-start.7 = (f32[512,512]{1,0:T(8,128)}, f32[512,512]{1,0:T(8,128)S(1)}, u32[]{:S(2)}, u32[]{:S(2)}) collective-permute-start(f32[512,512]{1,0:T(8,128)} %get-tuple-element.33), channel_id=1, source_target_pairs={{2,3},{6,7},{10,11},{14,15},{18,19},{22,23},{26,27},{30,31},{34,35... | collective-permute-start | bytes 3145736 | tf_op jit(solution)/shard_map/ppermute | solution.py:227
  5.9 1.3 %collective-permute-start.6 = (f32[512,512]{1,0:T(8,128)}, f32[512,512]{1,0:T(8,128)S(1)}, u32[]{:S(2)}, u32[]{:S(2)}) collective-permute-start(f32[512,512]{1,0:T(8,128)} %get-tuple-element.32), channel_id=1, source_target_pairs={{2,1},{3,2},{6,5},{7,6},{10,9},{11,10},{14,13},{15,14},{18,17},{19... | collective-permute-start | bytes 3145736 | tf_op jit(solution)/shard_map/ppermute | solution.py:227
  7.2 0.0 collective-permute-done.from_a
  7.2 3.0 %collective-permute-done.1.from_b = f32[64,512]{1,0:T(8,128)S(1)} collective-permute-done((f32[64,512]{1,0:T(8,128)S(1)}, f32[64,512]{1,0:T(8,128)S(1)}, u32[]{:S(2)}, u32[]{:S(2)}) %collective-permute-start.1) | collective-permute-done | bytes 131104 | tf_op jit(solution)/shard_map/ppermute | solution.py:227
  10.1 0.0 copy-start.1
  10.1 0.8 %shard_map.38 = (f32[64,512]{1,0:T(8,128)S(1)}, f32[64,512]{1,0:T(8,128)S(1)}) custom-call(f32[64,512]{1,0:T(8,128)S(1)} %collective-permute-done.from_a, f32[64,512]{1,0:T(8,128)S(1)} %collective-permute-done.1.from_b, f32[1024,512]{1,0:T(8,128)S(1)} %get-tuple-element.29.own), custom_call_target="tpu_custom_call" | custom-call | flops 20000000000 | tf_op jit(solution)/shard_map/pallas_call | solution.py:50
  10.9 8.8 %collective-permute-start.3 = (f32[64,512]{1,0:T(8,128)S(1)}, f32[64,512]{1,0:T(8,128)S(1)}, u32[]{:S(2)}, u32[]{:S(2)}) collective-permute-start(f32[64,512]{1,0:T(8,128)S(1)} %get-tuple-element.30), channel_id=1, source_target_pairs={{128,96},{384,352}} | collective-permute-start | bytes 393224 | tf_op jit(solution)/shard_map/ppermute | solution.py:227
  19.7 1.3 %collective-permute-start.2 = (f32[64,512]{1,0:T(8,128)S(1)}, f32[64,512]{1,0:T(8,128)S(1)}, u32[]{:S(2)}, u32[]{:S(2)}) collective-permute-start(f32[64,512]{1,0:T(8,128)S(1)} %get-tuple-element.30), channel_id=1, source_target_pairs={{128,32},{384,288}} | collective-permute-start | bytes 393224 | tf_op jit(solution)/shard_map/ppermute | solution.py:227
  21.0 0.0 copy-start
  21.0 1.4 %collective-permute-start.5 = (f32[64,512]{1,0:T(8,128)S(1)}, f32[64,512]{1,0:T(8,128)S(1)}, u32[]{:S(2)}, u32[]{:S(2)}) collective-permute-start(f32[64,512]{1,0:T(8,128)S(1)} %get-tuple-element.31), channel_id=1, source_target_pairs={{128,224},{384,480}} | collective-permute-start | bytes 393224 | tf_op jit(solution)/shard_map/ppermute | solution.py:227
  22.5 0.0 collective-permute-done.3.c_1
  22.5 1.3 %collective-permute-start.4 = (f32[64,512]{1,0:T(8,128)S(1)}, f32[64,512]{1,0:T(8,128)S(1)}, u32[]{:S(2)}, u32[]{:S(2)}) collective-permute-start(f32[64,512]{1,0:T(8,128)S(1)} %get-tuple-element.31), channel_id=1, source_target_pairs={{128,160},{384,416}} | collective-permute-start | bytes 393224 | tf_op jit(solution)/shard_map/ppermute | solution.py:227
  23.8 0.0 collective-permute-done.2.c_0
  23.8 0.0 copy-done.1
  23.8 0.7 %collective-permute-start.13 = (f32[512,512]{1,0:T(8,128)S(1)}, f32[512,512]{1,0:T(8,128)S(1)}, u32[]{:S(2)}, u32[]{:S(2)}) collective-permute-start(f32[512,512]{1,0:T(8,128)S(1)} %copy-done.1), channel_id=1, source_target_pairs={{40,32},{56,48},{104,96},{168,160},{184,176},{232,224},{296,288},{... | collective-permute-start | bytes 3145736 | tf_op jit(solution)/shard_map/ppermute | solution.py:227
  24.5 0.4 collective-permute-done.5.c_3
  24.9 1.3 %collective-permute-done.4.c_2 = f32[64,512]{1,0:T(8,128)S(1)} collective-permute-done((f32[64,512]{1,0:T(8,128)S(1)}, f32[64,512]{1,0:T(8,128)S(1)}, u32[]{:S(2)}, u32[]{:S(2)}) %collective-permute-start.4) | collective-permute-done | bytes 131104 | tf_op jit(solution)/shard_map/ppermute | solution.py:227
  26.3 0.0 collective-permute-done.7.early_b
  26.3 0.0 collective-permute-done.6.early_a
  26.3 0.7 collective-permute-start.8
  27.0 0.7 collective-permute-start.9
  27.6 0.0 collective-permute-done.8.c_left
  27.7 0.0 collective-permute-done.9.c_right
  27.7 0.0 copy-done
  27.7 0.3 shard_map.40
  28.0 0.7 collective-permute-start.11
  28.6 1.3 %collective-permute-start.10 = (f32[64,512]{1,0:T(8,128)S(1)}, f32[64,512]{1,0:T(8,128)S(1)}, u32[]{:S(2)}, u32[]{:S(2)}) collective-permute-start(f32[64,512]{1,0:T(8,128)S(1)} %get-tuple-element.42), channel_id=1, source_target_pairs={{16,0},{48,32},{80,64},{112,96},{144,128},{176,160},{208,192},{240... | collective-permute-start | bytes 393224 | tf_op jit(solution)/shard_map/ppermute | solution.py:227
  29.9 0.7 collective-permute-start.12
  30.6 0.0 collective-permute-done.13.early_c
  30.6 0.0 collective-permute-done.11.c_1
  30.6 19.8 %collective-permute-done.10.c_0 = f32[64,512]{1,0:T(8,128)S(1)} collective-permute-done((f32[64,512]{1,0:T(8,128)S(1)}, f32[64,512]{1,0:T(8,128)S(1)}, u32[]{:S(2)}, u32[]{:S(2)}) %collective-permute-start.10) | collective-permute-done | bytes 131104 | tf_op jit(solution)/shard_map/ppermute | solution.py:227
  50.4 0.0 collective-permute-done.12.c_3
  50.4 0.5 shard_map.41.here
  50.9 1.3 %collective-permute-start.14 = (f32[64,512]{1,0:T(8,128)S(1)}, f32[64,512]{1,0:T(8,128)S(1)}, u32[]{:S(2)}, u32[]{:S(2)}) collective-permute-start(f32[64,512]{1,0:T(8,128)S(1)} %shard_map.41.here), channel_id=1, source_target_pairs={{0,4},{8,12},{16,20},{24,28},{32,36},{40,44},{48,52},{56,60},{64,6... | collective-permute-start | bytes 393224 | tf_op jit(solution)/shard_map/ppermute | solution.py:227
  52.2 1.0 %collective-permute-done.14.over = f32[64,512]{1,0:T(8,128)S(1)} collective-permute-done((f32[64,512]{1,0:T(8,128)S(1)}, f32[64,512]{1,0:T(8,128)S(1)}, u32[]{:S(2)}, u32[]{:S(2)}) %collective-permute-start.14) | collective-permute-done | bytes 131104 | tf_op jit(solution)/shard_map/ppermute | solution.py:227
  53.2 0.5 shard_map.42
  53.7 1.3 %collective-permute-start.15 = (f32[64,512]{1,0:T(8,128)S(1)}, f32[64,512]{1,0:T(8,128)S(1)}, u32[]{:S(2)}, u32[]{:S(2)}) collective-permute-start(f32[64,512]{1,0:T(8,128)S(1)} %shard_map.42), channel_id=1, source_target_pairs={{0,1},{4,5},{8,9},{12,13},{16,17},{20,21},{24,25},{28,29},{32,33},... | collective-permute-start | bytes 393224 | tf_op jit(solution)/shard_map/ppermute | solution.py:227
  55.0 1.3 %collective-permute-start.18 = (f32[64,512]{1,0:T(8,128)S(1)}, f32[64,512]{1,0:T(8,128)S(1)}, u32[]{:S(2)}, u32[]{:S(2)}) collective-permute-start(f32[64,512]{1,0:T(8,128)S(1)} %shard_map.42), channel_id=1, source_target_pairs={{0,3},{4,7},{8,11},{12,15},{16,19},{20,23},{24,27},{28,31},{32,35}... | collective-permute-start | bytes 393224 | tf_op jit(solution)/shard_map/ppermute | solution.py:227
  56.3 1.3 %collective-permute-start.17 = (f32[64,512]{1,0:T(8,128)S(1)}, f32[64,512]{1,0:T(8,128)S(1)}, u32[]{:S(2)}, u32[]{:S(2)}) collective-permute-start(f32[64,512]{1,0:T(8,128)S(1)} %shard_map.42), channel_id=1, source_target_pairs={{0,2},{4,6},{8,10},{12,14},{16,18},{20,22},{24,26},{28,30},{32,34}... | collective-permute-start | bytes 393224 | tf_op jit(solution)/shard_map/ppermute | solution.py:227
  57.6 1.1 %collective-permute-done.15.coef = f32[64,512]{1,0:T(8,128)S(1)} collective-permute-done((f32[64,512]{1,0:T(8,128)S(1)}, f32[64,512]{1,0:T(8,128)S(1)}, u32[]{:S(2)}, u32[]{:S(2)}) %collective-permute-start.15) | collective-permute-done | bytes 131104 | tf_op jit(solution)/shard_map/ppermute | solution.py:227
  58.6 1.3 %collective-permute-start.16 = (f32[64,512]{1,0:T(8,128)S(1)}, f32[64,512]{1,0:T(8,128)S(1)}, u32[]{:S(2)}, u32[]{:S(2)}) collective-permute-start(f32[64,512]{1,0:T(8,128)S(1)} %get-tuple-element.46), channel_id=1, source_target_pairs={{1,0},{5,4},{9,8},{13,12},{17,16},{21,20},{25,24},{29,28},{33,32},... | collective-permute-start | bytes 393224 | tf_op jit(solution)/shard_map/ppermute | solution.py:227
  59.9 0.0 collective-permute-done.18.c2_x3
  59.9 1.4 %collective-permute-done.17.c2_x2 = f32[64,512]{1,0:T(8,128)S(1)} collective-permute-done((f32[64,512]{1,0:T(8,128)S(1)}, f32[64,512]{1,0:T(8,128)S(1)}, u32[]{:S(2)}, u32[]{:S(2)}) %collective-permute-start.17) | collective-permute-done | bytes 131104 | tf_op jit(solution)/shard_map/ppermute | solution.py:227
  61.3 5.2 %collective-permute-done.16.first = f32[64,512]{1,0:T(8,128)S(1)} collective-permute-done((f32[64,512]{1,0:T(8,128)S(1)}, f32[64,512]{1,0:T(8,128)S(1)}, u32[]{:S(2)}, u32[]{:S(2)}) %collective-permute-start.16) | collective-permute-done | bytes 131104 | tf_op jit(solution)/shard_map/ppermute | solution.py:227
  66.6 1.1 %shard_map.45 = f32[64,512]{1,0:T(8,128)} custom-call(f32[64,512]{1,0:T(8,128)S(1)} %collective-permute-done.16.first, f32[64,512]{1,0:T(8,128)S(1)} %shard_map.44.others, f32[512,512]{1,0:T(8,128)S(1)} %get-tuple-element.48.leaf), custom_call_target="tpu_custom_call" | custom-call | tf_op jit(solution)/shard_map/pallas_call | solution.py:297
  (3 shorter events, 0.0 us)
Async XLA Ops:
  2.6 4.6 %collective-permute-start = (f32[64,512]{1,0:T(8,128)S(1)}, f32[64,512]{1,0:T(8,128)S(1)}, u32[]{:S(2)}, u32[]{:S(2)}) collective-permute-start(f32[64,512]{1,0:T(8,128)S(1)} %get-tuple-element.27), channel_id=1, source_target_pairs={{256,128}} | collective-permute-start | bytes 393224 | tf_op jit(solution)/shard_map/ppermute | solution.py:227
  3.3 6.9 %collective-permute-start.1 = (f32[64,512]{1,0:T(8,128)S(1)}, f32[64,512]{1,0:T(8,128)S(1)}, u32[]{:S(2)}, u32[]{:S(2)}) collective-permute-start(f32[64,512]{1,0:T(8,128)S(1)} %get-tuple-element.28), channel_id=1, source_target_pairs={{256,384}} | collective-permute-start | bytes 393224 | tf_op jit(solution)/shard_map/ppermute | solution.py:227
  4.6 21.7 %collective-permute-start.7 = (f32[512,512]{1,0:T(8,128)}, f32[512,512]{1,0:T(8,128)S(1)}, u32[]{:S(2)}, u32[]{:S(2)}) collective-permute-start(f32[512,512]{1,0:T(8,128)} %get-tuple-element.33), channel_id=1, source_target_pairs={{2,3},{6,7},{10,11},{14,15},{18,19},{22,23},{26,27},{30,31},{34,35... | collective-permute-start | bytes 3145736 | tf_op jit(solution)/shard_map/ppermute | solution.py:227
  5.9 20.4 %collective-permute-start.6 = (f32[512,512]{1,0:T(8,128)}, f32[512,512]{1,0:T(8,128)S(1)}, u32[]{:S(2)}, u32[]{:S(2)}) collective-permute-start(f32[512,512]{1,0:T(8,128)} %get-tuple-element.32), channel_id=1, source_target_pairs={{2,1},{3,2},{6,5},{7,6},{10,9},{11,10},{14,13},{15,14},{18,17},{19... | collective-permute-start | bytes 3145736 | tf_op jit(solution)/shard_map/ppermute | solution.py:227
  10.1 13.6 %copy-start.1 = (f32[512,512]{1,0:T(8,128)S(1)}, f32[512,512]{1,0:T(8,128)}, u32[]{:S(2)}) copy-start(f32[512,512]{1,0:T(8,128)} %get-tuple-element.32) | copy-start | bytes 3145732
  10.9 11.5 %collective-permute-start.3 = (f32[64,512]{1,0:T(8,128)S(1)}, f32[64,512]{1,0:T(8,128)S(1)}, u32[]{:S(2)}, u32[]{:S(2)}) collective-permute-start(f32[64,512]{1,0:T(8,128)S(1)} %get-tuple-element.30), channel_id=1, source_target_pairs={{128,96},{384,352}} | collective-permute-start | bytes 393224 | tf_op jit(solution)/shard_map/ppermute | solution.py:227
  19.7 4.1 %collective-permute-start.2 = (f32[64,512]{1,0:T(8,128)S(1)}, f32[64,512]{1,0:T(8,128)S(1)}, u32[]{:S(2)}, u32[]{:S(2)}) collective-permute-start(f32[64,512]{1,0:T(8,128)S(1)} %get-tuple-element.30), channel_id=1, source_target_pairs={{128,32},{384,288}} | collective-permute-start | bytes 393224 | tf_op jit(solution)/shard_map/ppermute | solution.py:227
  21.0 6.7 %copy-start = (f32[512,512]{1,0:T(8,128)S(1)}, f32[512,512]{1,0:T(8,128)}, u32[]{:S(2)}) copy-start(f32[512,512]{1,0:T(8,128)} %leaf.1) | copy-start | bytes 3145732
  21.0 3.9 %collective-permute-start.5 = (f32[64,512]{1,0:T(8,128)S(1)}, f32[64,512]{1,0:T(8,128)S(1)}, u32[]{:S(2)}, u32[]{:S(2)}) collective-permute-start(f32[64,512]{1,0:T(8,128)S(1)} %get-tuple-element.31), channel_id=1, source_target_pairs={{128,224},{384,480}} | collective-permute-start | bytes 393224 | tf_op jit(solution)/shard_map/ppermute | solution.py:227
  22.5 3.8 %collective-permute-start.4 = (f32[64,512]{1,0:T(8,128)S(1)}, f32[64,512]{1,0:T(8,128)S(1)}, u32[]{:S(2)}, u32[]{:S(2)}) collective-permute-start(f32[64,512]{1,0:T(8,128)S(1)} %get-tuple-element.31), channel_id=1, source_target_pairs={{128,160},{384,416}} | collective-permute-start | bytes 393224 | tf_op jit(solution)/shard_map/ppermute | solution.py:227
  23.8 6.8 %collective-permute-start.13 = (f32[512,512]{1,0:T(8,128)S(1)}, f32[512,512]{1,0:T(8,128)S(1)}, u32[]{:S(2)}, u32[]{:S(2)}) collective-permute-start(f32[512,512]{1,0:T(8,128)S(1)} %copy-done.1), channel_id=1, source_target_pairs={{40,32},{56,48},{104,96},{168,160},{184,176},{232,224},{296,288},{... | collective-permute-start | bytes 3145736 | tf_op jit(solution)/shard_map/ppermute | solution.py:227
  26.3 1.4 %collective-permute-start.8 = (f32[64,512]{1,0:T(8,128)S(1)}, f32[64,512]{1,0:T(8,128)S(1)}, u32[]{:S(2)}, u32[]{:S(2)}) collective-permute-start(f32[64,512]{1,0:T(8,128)S(1)} %get-tuple-element.40), channel_id=1, source_target_pairs={{32,16},{96,80},{160,144},{224,208},{288,272},{352,336},{416,400},... | collective-permute-start | bytes 393224 | tf_op jit(solution)/shard_map/ppermute | solution.py:227
  27.0 0.7 %collective-permute-start.9 = (f32[64,512]{1,0:T(8,128)S(1)}, f32[64,512]{1,0:T(8,128)S(1)}, u32[]{:S(2)}, u32[]{:S(2)}) collective-permute-start(f32[64,512]{1,0:T(8,128)S(1)} %get-tuple-element.41), channel_id=1, source_target_pairs={{32,48},{96,112},{160,176},{224,240},{288,304},{352,368},{416,432}... | collective-permute-start | bytes 393224 | tf_op jit(solution)/shard_map/ppermute | solution.py:227
  28.0 2.7 %collective-permute-start.11 = (f32[64,512]{1,0:T(8,128)S(1)}, f32[64,512]{1,0:T(8,128)S(1)}, u32[]{:S(2)}, u32[]{:S(2)}) collective-permute-start(f32[64,512]{1,0:T(8,128)S(1)} %get-tuple-element.42), channel_id=1, source_target_pairs={{16,8},{48,40},{80,72},{112,104},{144,136},{176,168},{208,200},{24... | collective-permute-start | bytes 393224 | tf_op jit(solution)/shard_map/ppermute | solution.py:227
  28.6 21.8 %collective-permute-start.10 = (f32[64,512]{1,0:T(8,128)S(1)}, f32[64,512]{1,0:T(8,128)S(1)}, u32[]{:S(2)}, u32[]{:S(2)}) collective-permute-start(f32[64,512]{1,0:T(8,128)S(1)} %get-tuple-element.42), channel_id=1, source_target_pairs={{16,0},{48,32},{80,64},{112,96},{144,128},{176,160},{208,192},{240... | collective-permute-start | bytes 393224 | tf_op jit(solution)/shard_map/ppermute | solution.py:227
  29.9 20.5 %collective-permute-start.12 = (f32[64,512]{1,0:T(8,128)S(1)}, f32[64,512]{1,0:T(8,128)S(1)}, u32[]{:S(2)}, u32[]{:S(2)}) collective-permute-start(f32[64,512]{1,0:T(8,128)S(1)} %get-tuple-element.43.c_own), channel_id=1, source_target_pairs={{16,24},{48,56},{80,88},{112,120},{144,152},{176,184},{208,216},{2... | collective-permute-start | bytes 393224 | tf_op jit(solution)/shard_map/ppermute | solution.py:227
  50.9 2.3 %collective-permute-start.14 = (f32[64,512]{1,0:T(8,128)S(1)}, f32[64,512]{1,0:T(8,128)S(1)}, u32[]{:S(2)}, u32[]{:S(2)}) collective-permute-start(f32[64,512]{1,0:T(8,128)S(1)} %shard_map.41.here), channel_id=1, source_target_pairs={{0,4},{8,12},{16,20},{24,28},{32,36},{40,44},{48,52},{56,60},{64,6... | collective-permute-start | bytes 393224 | tf_op jit(solution)/shard_map/ppermute | solution.py:227
  53.7 5.0 %collective-permute-start.15 = (f32[64,512]{1,0:T(8,128)S(1)}, f32[64,512]{1,0:T(8,128)S(1)}, u32[]{:S(2)}, u32[]{:S(2)}) collective-permute-start(f32[64,512]{1,0:T(8,128)S(1)} %shard_map.42), channel_id=1, source_target_pairs={{0,1},{4,5},{8,9},{12,13},{16,17},{20,21},{24,25},{28,29},{32,33},... | collective-permute-start | bytes 393224 | tf_op jit(solution)/shard_map/ppermute | solution.py:227
  55.0 5.0 %collective-permute-start.18 = (f32[64,512]{1,0:T(8,128)S(1)}, f32[64,512]{1,0:T(8,128)S(1)}, u32[]{:S(2)}, u32[]{:S(2)}) collective-permute-start(f32[64,512]{1,0:T(8,128)S(1)} %shard_map.42), channel_id=1, source_target_pairs={{0,3},{4,7},{8,11},{12,15},{16,19},{20,23},{24,27},{28,31},{32,35}... | collective-permute-start | bytes 393224 | tf_op jit(solution)/shard_map/ppermute | solution.py:227
  56.3 5.1 %collective-permute-start.17 = (f32[64,512]{1,0:T(8,128)S(1)}, f32[64,512]{1,0:T(8,128)S(1)}, u32[]{:S(2)}, u32[]{:S(2)}) collective-permute-start(f32[64,512]{1,0:T(8,128)S(1)} %shard_map.42), channel_id=1, source_target_pairs={{0,2},{4,6},{8,10},{12,14},{16,18},{20,22},{24,26},{28,30},{32,34}... | collective-permute-start | bytes 393224 | tf_op jit(solution)/shard_map/ppermute | solution.py:227
  58.6 7.9 %collective-permute-start.16 = (f32[64,512]{1,0:T(8,128)S(1)}, f32[64,512]{1,0:T(8,128)S(1)}, u32[]{:S(2)}, u32[]{:S(2)}) collective-permute-start(f32[64,512]{1,0:T(8,128)S(1)} %get-tuple-element.46), channel_id=1, source_target_pairs={{1,0},{5,4},{9,8},{13,12},{17,16},{21,20},{25,24},{29,28},{33,32},... | collective-permute-start | bytes 393224 | tf_op jit(solution)/shard_map/ppermute | solution.py:227

commit v4 on v3

--- a/solution.py
+++ b/solution.py
@@ -33,7 +33,7 @@
     return both[:MODES] + (both[MODES:] + cross)
 
 
-WORK_8, WORK_7 = 20 * 10**9, 20 * 10**9
+WORK_8, WORK_7 = 0, 20 * 10**9
 
 
 def place():
@@ -65,33 +65,36 @@
     return ref.at[pl.ds(which * SNAPS, SNAPS), :]
 
 
-def root_kernel(factors, basis, up, low, own, upper, other, held, sems):
-    y, z, core, x = place()
-    loads = [pltpu.make_async_copy(half(factors, h), half(own, h), sems.at[h]) for h in (0, 1)]
-    root = (y == 2) & (z == 0) & (core == 0) & (x == 0)
-    swap = (core == 1) & (x == 0)
-    base = pltpu.make_async_copy(basis, held, sems.at[2])
-    for load in loads:
+def cut_kernel(factors, own, upper, other, sems):
+    y, z, core, x = place()
+    middle = (z == 8) & (core == 0) & (x == 0)
+    swap = middle | ((core == 1) & (x == 0))
+    cut = pltpu.make_async_copy(half(factors, 0), upper, sems.at[0])
+    cut_other = pltpu.make_async_copy(half(factors, 1), upper, sems.at[0])
+    cut_up = pltpu.make_async_copy(half(factors, 0), other, sems.at[1])
+    cut_low = pltpu.make_async_copy(half(factors, 1), other, sems.at[1])
+    load = pltpu.make_async_copy(factors, own, sems.at[2])
+    pl.when(middle)(cut_other.start)
+    pl.when(~middle)(cut.start)
+    pl.when(swap)(cut_up.start)
+    pl.when(~swap)(cut_low.start)
+    load.start()
+    cut.wait()
+    cut_low.wait()
+    load.wait()
+
+
+def root_kernel(basis, own, up, low, held, sem):
+    y, z, core, x = place()
+
+    @pl.when((y == 2) & (z == 0) & (core == 0) & (x == 0))
+    def _():
+        load = pltpu.make_async_copy(basis, held, sem)
         load.start()
-    pl.when(root)(base.start)
-    cut = pltpu.make_async_copy(half(own, 0), upper, sems.at[3])
-    cut_up = pltpu.make_async_copy(half(own, 0), other, sems.at[4])
-    cut_low = pltpu.make_async_copy(half(own, 1), other, sems.at[4])
-    loads[0].wait()
-    cut.start()
-    pl.when(swap)(cut_up.start)
-    loads[1].wait()
-    pl.when(~swap)(cut_low.start)
-
-    @pl.when(root)
-    def _():
-        base.wait()
+        load.wait()
         up[...] = times(held[...], own[:SNAPS, :])
         low[...] = times(held[...], own[SNAPS:, :])
 
-    cut.wait()
-    cut_low.wait()
-
 
 def level_8_kernel(from_a, from_b, own, up, low):
     y, z, core, x = place()
@@ -104,7 +107,7 @@
 
 def level_7_6_kernel(c_0, c_1, c_2, c_3, own, early_a, early_b, up, low, block, held, sem):
     y, z, core, x = place()
-    for z_here, source, coefs in ((4, early_a, (c_0, c_2)), (12, early_b, (c_1, c_3))):
+    for z_here, source, coefs in ((4, early_b, (c_0, c_2)), (12, early_a, (c_1, c_3))):
         @pl.when((z == z_here) & (core == 0) & (x == 0))
         def _():
             load = pltpu.make_async_copy(source, block, sem)
@@ -170,11 +173,11 @@
     def _():
         out[...] = times(over[...], own[SNAPS:, :])
 
-    @pl.when((core == 0) & (x == 0) & (z == 12))
+    @pl.when((core == 0) & (x == 0) & (z == 4))
     def _():
         out[...] = times(here[...], kept_a[...])
 
-    @pl.when((core == 0) & (x == 0) & (z != 12))
+    @pl.when((core == 0) & (x == 0) & (z != 4))
     def _():
         out[...] = times(here[...], kept_b[...])
 
@@ -231,10 +234,12 @@
     DMA = pltpu.SemaphoreType.DMA
     coef, block = pltpu.VMEM(COEF, jnp.float32), pltpu.VMEM(FACTOR, jnp.float32)
 
-    up, low, own, upper, other = kernel_call(
-        root_kernel, [node_factors, modal_basis.T], [0, 0],
-        [(COEF, 1), (COEF, 1), (node_factors.shape, 1), (FACTOR, 0), (FACTOR, 0)], [coef, DMA((5,))],
-        limit=56,
+    own, upper, other = kernel_call(
+        cut_kernel, [node_factors], [0], [(node_factors.shape, 1), (FACTOR, 1), (FACTOR, 1)],
+        [DMA((3,))], limit=56,
+    )
+    up, low = kernel_call(
+        root_kernel, [modal_basis.T, own], [0, 1], [(COEF, 1), (COEF, 1)], [coef, DMA]
     )
     to_y1 = send(up, [(at(2, 0, 0, 0), at(1, 0, 0, 0))])
     to_y3 = send(low, [(at(2, 0, 0, 0), at(3, 0, 0, 0))])
@@ -242,15 +247,15 @@
     early_a = send(
         upper,
         [(at(y, z, c, x), at(y, z, c, x - 1)) for y, z, c, x in EVERY if x >= 2]
-        + [(at(y, 8, 0, 0), at(y, 4, 0, 0)) for y in range(Y)]
+        + [(at(y, 8, 0, 0), at(y, 12, 0, 0)) for y in range(Y)]
         + [(at(y, z + 1, 0, 0), at(y, z, 0, 0)) for y in range(Y) for z in range(0, Z, 2) if z not in LATE]
-        + [(at(y, 12, 1, 0), at(y, 12, 0, 0)) for y in range(Y)],
+        + [(at(y, 4, 1, 0), at(y, 4, 0, 0)) for y in range(Y)],
     )
     early_b = send(
         other,
         [(at(y, z, c, 2), at(y, z, c, 3)) for y, z, c, x in EVERY if x == 2]
-        + [(at(y, 8, 0, 0), at(y, 12, 0, 0)) for y in range(Y)]
-        + [(at(y, z, 1, 0), at(y, z, 0, 0)) for y in range(Y) for z in range(Z) if z != 12],
+        + [(at(y, 8, 0, 0), at(y, 4, 0, 0)) for y in range(Y)]
+        + [(at(y, z, 1, 0), at(y, z, 0, 0)) for y in range(Y) for z in range(Z) if z != 4],
     )
     early_c = send(upper, [(at(y, z + 1, 0, 0), at(y, z, 0, 0)) for y in range(Y) for z in LATE])
 

time: 68.2 us -> 62.6 us (0.918)
  starting transfers between devices: 28.5 us -> 25.7 us
  waiting for transfers between devices: 33.1 us -> 30.7 us
    ppermute x19, starting transfers between devices: 28.5 us -> 25.7 us  [send(): return lax.ppermute(block, AXES, route)]
    ppermute x19, waiting for transfers between devices: 33.1 us -> 30.7 us  [send(): return lax.ppermute(block, AXES, route)]
    pallas_call x8 -> x9, Pallas kernels: 4.64 us -> 4.39 us  [kernel_call(): pl.pallas_call(body, out_shape=[pltpu.VMEM(shape, jnp.float32) if keep el...]
where the time goes in v4:
time: 62.6 us; the launch traced here: 62.2 us
  waiting for transfers between devices  30.7 us (49%)
  starting transfers between devices  25.7 us (41%)
  Pallas kernels  5.5 us (9%)
    ppermute x19, waiting for transfers between devices, send(): return lax.ppermute(block, AXES, route)  30.7 us
    ppermute x19, starting transfers between devices, send(): return lax.ppermute(block, AXES, route)  25.7 us
    pallas_call x9, Pallas kernels, kernel_call(): pl.pallas_call(body, out_shape=[pltpu.VMEM(shape, jnp.float32) if keep el...  4.39 us
  transfers between devices with their start and end apart: 19, of which 8 were waited for; matrix products, arithmetic and copies ran while one was open for 0% of the time, Pallas kernels for 2%

profile of v4, /device:TPU:24, one launch (start us, length us, event | category | flops | bytes accessed | tf_op | source)
XLA Modules:
  0.0 62.2 jit_solution(8116413808515020700)
XLA Ops:
  0.0 0.0 copy-start.1
  0.0 2.3 %shard_map.37 = (f32[1024,512]{1,0:T(8,128)S(1)}, f32[512,512]{1,0:T(8,128)S(1)}, f32[512,512]{1,0:T(8,128)S(1)}) custom-call(f32[1024,512]{1,0:T(8,128)} %factors.1), custom_call_target="tpu_custom_call" | custom-call | tf_op jit(solution)/shard_map/pallas_call | solution.py:50
  2.3 1.3 %collective-permute-start.7 = (f32[512,512]{1,0:T(8,128)S(1)}, f32[512,512]{1,0:T(8,128)S(1)}, u32[]{:S(2)}, u32[]{:S(2)}) collective-permute-start(f32[512,512]{1,0:T(8,128)S(1)} %get-tuple-element.33), channel_id=1, source_target_pairs={{2,3},{6,7},{10,11},{14,15},{18,19},{22,23},{26,27},{30,31},{34,35... | collective-permute-start | bytes 3145736 | tf_op jit(solution)/shard_map/ppermute | solution.py:230
  3.6 1.3 %collective-permute-start.6 = (f32[512,512]{1,0:T(8,128)S(1)}, f32[512,512]{1,0:T(8,128)S(1)}, u32[]{:S(2)}, u32[]{:S(2)}) collective-permute-start(f32[512,512]{1,0:T(8,128)S(1)} %get-tuple-element.32), channel_id=1, source_target_pairs={{2,1},{3,2},{6,5},{7,6},{10,9},{11,10},{14,13},{15,14},{18,17},{19... | collective-permute-start | bytes 3145736 | tf_op jit(solution)/shard_map/ppermute | solution.py:230
  4.9 0.0 copy-done.1
  5.0 0.7 %collective-permute-start = (f32[64,512]{1,0:T(8,128)S(1)}, f32[64,512]{1,0:T(8,128)S(1)}, u32[]{:S(2)}, u32[]{:S(2)}) collective-permute-start(f32[64,512]{1,0:T(8,128)S(1)} %get-tuple-element.28), channel_id=1, source_target_pairs={{256,128}} | collective-permute-start | bytes 393224 | tf_op jit(solution)/shard_map/ppermute | solution.py:230
  5.6 1.3 %collective-permute-start.1 = (f32[64,512]{1,0:T(8,128)S(1)}, f32[64,512]{1,0:T(8,128)S(1)}, u32[]{:S(2)}, u32[]{:S(2)}) collective-permute-start(f32[64,512]{1,0:T(8,128)S(1)} %get-tuple-element.29), channel_id=1, source_target_pairs={{256,384}} | collective-permute-start | bytes 393224 | tf_op jit(solution)/shard_map/ppermute | solution.py:230
  6.9 0.0 collective-permute-done.from_a
  7.0 5.6 %collective-permute-done.1.from_b = f32[64,512]{1,0:T(8,128)S(1)} collective-permute-done((f32[64,512]{1,0:T(8,128)S(1)}, f32[64,512]{1,0:T(8,128)S(1)}, u32[]{:S(2)}, u32[]{:S(2)}) %collective-permute-start.1) | collective-permute-done | bytes 131104 | tf_op jit(solution)/shard_map/ppermute | solution.py:230
  12.5 0.8 %shard_map.39 = (f32[64,512]{1,0:T(8,128)S(1)}, f32[64,512]{1,0:T(8,128)S(1)}) custom-call(f32[64,512]{1,0:T(8,128)S(1)} %collective-permute-done.from_a, f32[64,512]{1,0:T(8,128)S(1)} %collective-permute-done.1.from_b, f32[1024,512]{1,0:T(8,128)S(1)} %get-tuple-element.27.own), custom_call_target="tpu_custom_call" | custom-call | tf_op jit(solution)/shard_map/pallas_call | solution.py:50
  13.3 6.0 %collective-permute-start.3 = (f32[64,512]{1,0:T(8,128)S(1)}, f32[64,512]{1,0:T(8,128)S(1)}, u32[]{:S(2)}, u32[]{:S(2)}) collective-permute-start(f32[64,512]{1,0:T(8,128)S(1)} %get-tuple-element.30), channel_id=1, source_target_pairs={{128,96},{384,352}} | collective-permute-start | bytes 393224 | tf_op jit(solution)/shard_map/ppermute | solution.py:230
  19.3 1.3 %collective-permute-start.2 = (f32[64,512]{1,0:T(8,128)S(1)}, f32[64,512]{1,0:T(8,128)S(1)}, u32[]{:S(2)}, u32[]{:S(2)}) collective-permute-start(f32[64,512]{1,0:T(8,128)S(1)} %get-tuple-element.30), channel_id=1, source_target_pairs={{128,32},{384,288}} | collective-permute-start | bytes 393224 | tf_op jit(solution)/shard_map/ppermute | solution.py:230
  20.6 0.0 copy-start
  20.6 1.4 %collective-permute-start.5 = (f32[64,512]{1,0:T(8,128)S(1)}, f32[64,512]{1,0:T(8,128)S(1)}, u32[]{:S(2)}, u32[]{:S(2)}) collective-permute-start(f32[64,512]{1,0:T(8,128)S(1)} %get-tuple-element.31), channel_id=1, source_target_pairs={{128,224},{384,480}} | collective-permute-start | bytes 393224 | tf_op jit(solution)/shard_map/ppermute | solution.py:230
  22.1 0.0 collective-permute-done.3.c_1
  22.1 1.3 %collective-permute-start.4 = (f32[64,512]{1,0:T(8,128)S(1)}, f32[64,512]{1,0:T(8,128)S(1)}, u32[]{:S(2)}, u32[]{:S(2)}) collective-permute-start(f32[64,512]{1,0:T(8,128)S(1)} %get-tuple-element.31), channel_id=1, source_target_pairs={{128,160},{384,416}} | collective-permute-start | bytes 393224 | tf_op jit(solution)/shard_map/ppermute | solution.py:230
  23.4 0.0 collective-permute-done.2.c_0
  23.4 0.7 %collective-permute-start.13 = (f32[512,512]{1,0:T(8,128)S(1)}, f32[512,512]{1,0:T(8,128)S(1)}, u32[]{:S(2)}, u32[]{:S(2)}) collective-permute-start(f32[512,512]{1,0:T(8,128)S(1)} %get-tuple-element.32), channel_id=1, source_target_pairs={{40,32},{56,48},{104,96},{168,160},{184,176},{232,224},{296,288},{... | collective-permute-start | bytes 3145736 | tf_op jit(solution)/shard_map/ppermute | solution.py:230
  24.1 0.4 collective-permute-done.5.c_3
  24.6 1.3 %collective-permute-done.4.c_2 = f32[64,512]{1,0:T(8,128)S(1)} collective-permute-done((f32[64,512]{1,0:T(8,128)S(1)}, f32[64,512]{1,0:T(8,128)S(1)}, u32[]{:S(2)}, u32[]{:S(2)}) %collective-permute-start.4) | collective-permute-done | bytes 131104 | tf_op jit(solution)/shard_map/ppermute | solution.py:230
  25.9 0.0 collective-permute-done.7.early_b
  25.9 0.0 collective-permute-done.6.early_a
  25.9 0.7 %collective-permute-start.8 = (f32[64,512]{1,0:T(8,128)S(1)}, f32[64,512]{1,0:T(8,128)S(1)}, u32[]{:S(2)}, u32[]{:S(2)}) collective-permute-start(f32[64,512]{1,0:T(8,128)S(1)} %get-tuple-element.40), channel_id=1, source_target_pairs={{32,16},{96,80},{160,144},{224,208},{288,272},{352,336},{416,400},... | collective-permute-start | bytes 393224 | tf_op jit(solution)/shard_map/ppermute | solution.py:230
  26.6 0.7 %collective-permute-start.9 = (f32[64,512]{1,0:T(8,128)S(1)}, f32[64,512]{1,0:T(8,128)S(1)}, u32[]{:S(2)}, u32[]{:S(2)}) collective-permute-start(f32[64,512]{1,0:T(8,128)S(1)} %get-tuple-element.41), channel_id=1, source_target_pairs={{32,48},{96,112},{160,176},{224,240},{288,304},{352,368},{416,432}... | collective-permute-start | bytes 393224 | tf_op jit(solution)/shard_map/ppermute | solution.py:230
  27.3 0.0 collective-permute-done.8.c_left
  27.3 0.0 collective-permute-done.9.c_right
  27.3 0.0 copy-done
  27.3 0.3 shard_map.41
  27.6 0.7 %collective-permute-start.11 = (f32[64,512]{1,0:T(8,128)S(1)}, f32[64,512]{1,0:T(8,128)S(1)}, u32[]{:S(2)}, u32[]{:S(2)}) collective-permute-start(f32[64,512]{1,0:T(8,128)S(1)} %get-tuple-element.42), channel_id=1, source_target_pairs={{16,8},{48,40},{80,72},{112,104},{144,136},{176,168},{208,200},{24... | collective-permute-start | bytes 393224 | tf_op jit(solution)/shard_map/ppermute | solution.py:230
  28.3 1.3 %collective-permute-start.10 = (f32[64,512]{1,0:T(8,128)S(1)}, f32[64,512]{1,0:T(8,128)S(1)}, u32[]{:S(2)}, u32[]{:S(2)}) collective-permute-start(f32[64,512]{1,0:T(8,128)S(1)} %get-tuple-element.42), channel_id=1, source_target_pairs={{16,0},{48,32},{80,64},{112,96},{144,128},{176,160},{208,192},{240... | collective-permute-start | bytes 393224 | tf_op jit(solution)/shard_map/ppermute | solution.py:230
  29.6 0.7 %collective-permute-start.12 = (f32[64,512]{1,0:T(8,128)S(1)}, f32[64,512]{1,0:T(8,128)S(1)}, u32[]{:S(2)}, u32[]{:S(2)}) collective-permute-start(f32[64,512]{1,0:T(8,128)S(1)} %get-tuple-element.43.c_own), channel_id=1, source_target_pairs={{16,24},{48,56},{80,88},{112,120},{144,152},{176,184},{208,216},{2... | collective-permute-start | bytes 393224 | tf_op jit(solution)/shard_map/ppermute | solution.py:230
  30.2 0.0 collective-permute-done.13.early_c
  30.2 0.0 collective-permute-done.11.c_1
  30.3 14.7 %collective-permute-done.10.c_0 = f32[64,512]{1,0:T(8,128)S(1)} collective-permute-done((f32[64,512]{1,0:T(8,128)S(1)}, f32[64,512]{1,0:T(8,128)S(1)}, u32[]{:S(2)}, u32[]{:S(2)}) %collective-permute-start.10) | collective-permute-done | bytes 131104 | tf_op jit(solution)/shard_map/ppermute | solution.py:230
  45.0 0.0 collective-permute-done.12.c_3
  45.0 0.5 shard_map.42.here
  45.5 1.3 %collective-permute-start.14 = (f32[64,512]{1,0:T(8,128)S(1)}, f32[64,512]{1,0:T(8,128)S(1)}, u32[]{:S(2)}, u32[]{:S(2)}) collective-permute-start(f32[64,512]{1,0:T(8,128)S(1)} %shard_map.42.here), channel_id=1, source_target_pairs={{0,4},{8,12},{16,20},{24,28},{32,36},{40,44},{48,52},{56,60},{64,6... | collective-permute-start | bytes 393224 | tf_op jit(solution)/shard_map/ppermute | solution.py:230
  46.8 1.0 %collective-permute-done.14.over = f32[64,512]{1,0:T(8,128)S(1)} collective-permute-done((f32[64,512]{1,0:T(8,128)S(1)}, f32[64,512]{1,0:T(8,128)S(1)}, u32[]{:S(2)}, u32[]{:S(2)}) %collective-permute-start.14) | collective-permute-done | bytes 131104 | tf_op jit(solution)/shard_map/ppermute | solution.py:230
  47.8 0.5 shard_map.43
  48.2 1.3 %collective-permute-start.15 = (f32[64,512]{1,0:T(8,128)S(1)}, f32[64,512]{1,0:T(8,128)S(1)}, u32[]{:S(2)}, u32[]{:S(2)}) collective-permute-start(f32[64,512]{1,0:T(8,128)S(1)} %shard_map.43), channel_id=1, source_target_pairs={{0,1},{4,5},{8,9},{12,13},{16,17},{20,21},{24,25},{28,29},{32,33},... | collective-permute-start | bytes 393224 | tf_op jit(solution)/shard_map/ppermute | solution.py:230
  49.5 1.3 %collective-permute-start.18 = (f32[64,512]{1,0:T(8,128)S(1)}, f32[64,512]{1,0:T(8,128)S(1)}, u32[]{:S(2)}, u32[]{:S(2)}) collective-permute-start(f32[64,512]{1,0:T(8,128)S(1)} %shard_map.43), channel_id=1, source_target_pairs={{0,3},{4,7},{8,11},{12,15},{16,19},{20,23},{24,27},{28,31},{32,35}... | collective-permute-start | bytes 393224 | tf_op jit(solution)/shard_map/ppermute | solution.py:230
  50.8 1.3 %collective-permute-start.17 = (f32[64,512]{1,0:T(8,128)S(1)}, f32[64,512]{1,0:T(8,128)S(1)}, u32[]{:S(2)}, u32[]{:S(2)}) collective-permute-start(f32[64,512]{1,0:T(8,128)S(1)} %shard_map.43), channel_id=1, source_target_pairs={{0,2},{4,6},{8,10},{12,14},{16,18},{20,22},{24,26},{28,30},{32,34}... | collective-permute-start | bytes 393224 | tf_op jit(solution)/shard_map/ppermute | solution.py:230
  52.1 1.1 %collective-permute-done.15.coef = f32[64,512]{1,0:T(8,128)S(1)} collective-permute-done((f32[64,512]{1,0:T(8,128)S(1)}, f32[64,512]{1,0:T(8,128)S(1)}, u32[]{:S(2)}, u32[]{:S(2)}) %collective-permute-start.15) | collective-permute-done | bytes 131104 | tf_op jit(solution)/shard_map/ppermute | solution.py:230
  53.2 1.3 %collective-permute-start.16 = (f32[64,512]{1,0:T(8,128)S(1)}, f32[64,512]{1,0:T(8,128)S(1)}, u32[]{:S(2)}, u32[]{:S(2)}) collective-permute-start(f32[64,512]{1,0:T(8,128)S(1)} %get-tuple-element.46), channel_id=1, source_target_pairs={{1,0},{5,4},{9,8},{13,12},{17,16},{21,20},{25,24},{29,28},{33,32},... | collective-permute-start | bytes 393224 | tf_op jit(solution)/shard_map/ppermute | solution.py:230
  54.5 0.0 collective-permute-done.18.c2_x3
  54.5 1.4 %collective-permute-done.17.c2_x2 = f32[64,512]{1,0:T(8,128)S(1)} collective-permute-done((f32[64,512]{1,0:T(8,128)S(1)}, f32[64,512]{1,0:T(8,128)S(1)}, u32[]{:S(2)}, u32[]{:S(2)}) %collective-permute-start.17) | collective-permute-done | bytes 131104 | tf_op jit(solution)/shard_map/ppermute | solution.py:230
  55.9 5.2 %collective-permute-done.16.first = f32[64,512]{1,0:T(8,128)S(1)} collective-permute-done((f32[64,512]{1,0:T(8,128)S(1)}, f32[64,512]{1,0:T(8,128)S(1)}, u32[]{:S(2)}, u32[]{:S(2)}) %collective-permute-start.16) | collective-permute-done | bytes 131104 | tf_op jit(solution)/shard_map/ppermute | solution.py:230
  61.1 1.1 %shard_map.46 = f32[64,512]{1,0:T(8,128)} custom-call(f32[64,512]{1,0:T(8,128)S(1)} %collective-permute-done.16.first, f32[64,512]{1,0:T(8,128)S(1)} %shard_map.45.others, f32[512,512]{1,0:T(8,128)S(1)} %get-tuple-element.48.leaf), custom_call_target="tpu_custom_call" | custom-call | tf_op jit(solution)/shard_map/pallas_call | solution.py:302
  (4 shorter events, 0.1 us)
Async XLA Ops:
  0.0 4.9 %copy-start.1 = (f32[512,64]{0,1:T(8,128)S(1)}, f32[512,64]{0,1:T(8,128)}, u32[]{:S(2)}) copy-start(f32[512,64]{0,1:T(8,128)} %param.5) | copy-start | bytes 393220
  2.3 23.6 %collective-permute-start.7 = (f32[512,512]{1,0:T(8,128)S(1)}, f32[512,512]{1,0:T(8,128)S(1)}, u32[]{:S(2)}, u32[]{:S(2)}) collective-permute-start(f32[512,512]{1,0:T(8,128)S(1)} %get-tuple-element.33), channel_id=1, source_target_pairs={{2,3},{6,7},{10,11},{14,15},{18,19},{22,23},{26,27},{30,31},{34,35... | collective-permute-start | bytes 3145736 | tf_op jit(solution)/shard_map/ppermute | solution.py:230
  3.6 22.3 %collective-permute-start.6 = (f32[512,512]{1,0:T(8,128)S(1)}, f32[512,512]{1,0:T(8,128)S(1)}, u32[]{:S(2)}, u32[]{:S(2)}) collective-permute-start(f32[512,512]{1,0:T(8,128)S(1)} %get-tuple-element.32), channel_id=1, source_target_pairs={{2,1},{3,2},{6,5},{7,6},{10,9},{11,10},{14,13},{15,14},{18,17},{19... | collective-permute-start | bytes 3145736 | tf_op jit(solution)/shard_map/ppermute | solution.py:230
  5.0 2.0 %collective-permute-start = (f32[64,512]{1,0:T(8,128)S(1)}, f32[64,512]{1,0:T(8,128)S(1)}, u32[]{:S(2)}, u32[]{:S(2)}) collective-permute-start(f32[64,512]{1,0:T(8,128)S(1)} %get-tuple-element.28), channel_id=1, source_target_pairs={{256,128}} | collective-permute-start | bytes 393224 | tf_op jit(solution)/shard_map/ppermute | solution.py:230
  5.6 6.9 %collective-permute-start.1 = (f32[64,512]{1,0:T(8,128)S(1)}, f32[64,512]{1,0:T(8,128)S(1)}, u32[]{:S(2)}, u32[]{:S(2)}) collective-permute-start(f32[64,512]{1,0:T(8,128)S(1)} %get-tuple-element.29), channel_id=1, source_target_pairs={{256,384}} | collective-permute-start | bytes 393224 | tf_op jit(solution)/shard_map/ppermute | solution.py:230
  13.3 8.8 %collective-permute-start.3 = (f32[64,512]{1,0:T(8,128)S(1)}, f32[64,512]{1,0:T(8,128)S(1)}, u32[]{:S(2)}, u32[]{:S(2)}) collective-permute-start(f32[64,512]{1,0:T(8,128)S(1)} %get-tuple-element.30), channel_id=1, source_target_pairs={{128,96},{384,352}} | collective-permute-start | bytes 393224 | tf_op jit(solution)/shard_map/ppermute | solution.py:230
  19.3 4.1 %collective-permute-start.2 = (f32[64,512]{1,0:T(8,128)S(1)}, f32[64,512]{1,0:T(8,128)S(1)}, u32[]{:S(2)}, u32[]{:S(2)}) collective-permute-start(f32[64,512]{1,0:T(8,128)S(1)} %get-tuple-element.30), channel_id=1, source_target_pairs={{128,32},{384,288}} | collective-permute-start | bytes 393224 | tf_op jit(solution)/shard_map/ppermute | solution.py:230
  20.6 6.7 %copy-start = (f32[512,512]{1,0:T(8,128)S(1)}, f32[512,512]{1,0:T(8,128)}, u32[]{:S(2)}) copy-start(f32[512,512]{1,0:T(8,128)} %leaf.1) | copy-start | bytes 3145732
  20.6 3.9 %collective-permute-start.5 = (f32[64,512]{1,0:T(8,128)S(1)}, f32[64,512]{1,0:T(8,128)S(1)}, u32[]{:S(2)}, u32[]{:S(2)}) collective-permute-start(f32[64,512]{1,0:T(8,128)S(1)} %get-tuple-element.31), channel_id=1, source_target_pairs={{128,224},{384,480}} | collective-permute-start | bytes 393224 | tf_op jit(solution)/shard_map/ppermute | solution.py:230
  22.1 3.8 %collective-permute-start.4 = (f32[64,512]{1,0:T(8,128)S(1)}, f32[64,512]{1,0:T(8,128)S(1)}, u32[]{:S(2)}, u32[]{:S(2)}) collective-permute-start(f32[64,512]{1,0:T(8,128)S(1)} %get-tuple-element.31), channel_id=1, source_target_pairs={{128,160},{384,416}} | collective-permute-start | bytes 393224 | tf_op jit(solution)/shard_map/ppermute | solution.py:230
  23.4 6.8 %collective-permute-start.13 = (f32[512,512]{1,0:T(8,128)S(1)}, f32[512,512]{1,0:T(8,128)S(1)}, u32[]{:S(2)}, u32[]{:S(2)}) collective-permute-start(f32[512,512]{1,0:T(8,128)S(1)} %get-tuple-element.32), channel_id=1, source_target_pairs={{40,32},{56,48},{104,96},{168,160},{184,176},{232,224},{296,288},{... | collective-permute-start | bytes 3145736 | tf_op jit(solution)/shard_map/ppermute | solution.py:230
  25.9 1.4 %collective-permute-start.8 = (f32[64,512]{1,0:T(8,128)S(1)}, f32[64,512]{1,0:T(8,128)S(1)}, u32[]{:S(2)}, u32[]{:S(2)}) collective-permute-start(f32[64,512]{1,0:T(8,128)S(1)} %get-tuple-element.40), channel_id=1, source_target_pairs={{32,16},{96,80},{160,144},{224,208},{288,272},{352,336},{416,400},... | collective-permute-start | bytes 393224 | tf_op jit(solution)/shard_map/ppermute | solution.py:230
  26.6 0.7 %collective-permute-start.9 = (f32[64,512]{1,0:T(8,128)S(1)}, f32[64,512]{1,0:T(8,128)S(1)}, u32[]{:S(2)}, u32[]{:S(2)}) collective-permute-start(f32[64,512]{1,0:T(8,128)S(1)} %get-tuple-element.41), channel_id=1, source_target_pairs={{32,48},{96,112},{160,176},{224,240},{288,304},{352,368},{416,432}... | collective-permute-start | bytes 393224 | tf_op jit(solution)/shard_map/ppermute | solution.py:230
  27.6 2.7 %collective-permute-start.11 = (f32[64,512]{1,0:T(8,128)S(1)}, f32[64,512]{1,0:T(8,128)S(1)}, u32[]{:S(2)}, u32[]{:S(2)}) collective-permute-start(f32[64,512]{1,0:T(8,128)S(1)} %get-tuple-element.42), channel_id=1, source_target_pairs={{16,8},{48,40},{80,72},{112,104},{144,136},{176,168},{208,200},{24... | collective-permute-start | bytes 393224 | tf_op jit(solution)/shard_map/ppermute | solution.py:230
  28.3 16.7 %collective-permute-start.10 = (f32[64,512]{1,0:T(8,128)S(1)}, f32[64,512]{1,0:T(8,128)S(1)}, u32[]{:S(2)}, u32[]{:S(2)}) collective-permute-start(f32[64,512]{1,0:T(8,128)S(1)} %get-tuple-element.42), channel_id=1, source_target_pairs={{16,0},{48,32},{80,64},{112,96},{144,128},{176,160},{208,192},{240... | collective-permute-start | bytes 393224 | tf_op jit(solution)/shard_map/ppermute | solution.py:230
  29.6 15.4 %collective-permute-start.12 = (f32[64,512]{1,0:T(8,128)S(1)}, f32[64,512]{1,0:T(8,128)S(1)}, u32[]{:S(2)}, u32[]{:S(2)}) collective-permute-start(f32[64,512]{1,0:T(8,128)S(1)} %get-tuple-element.43.c_own), channel_id=1, source_target_pairs={{16,24},{48,56},{80,88},{112,120},{144,152},{176,184},{208,216},{2... | collective-permute-start | bytes 393224 | tf_op jit(solution)/shard_map/ppermute | solution.py:230
  45.5 2.3 %collective-permute-start.14 = (f32[64,512]{1,0:T(8,128)S(1)}, f32[64,512]{1,0:T(8,128)S(1)}, u32[]{:S(2)}, u32[]{:S(2)}) collective-permute-start(f32[64,512]{1,0:T(8,128)S(1)} %shard_map.42.here), channel_id=1, source_target_pairs={{0,4},{8,12},{16,20},{24,28},{32,36},{40,44},{48,52},{56,60},{64,6... | collective-permute-start | bytes 393224 | tf_op jit(solution)/shard_map/ppermute | solution.py:230
  48.2 5.0 %collective-permute-start.15 = (f32[64,512]{1,0:T(8,128)S(1)}, f32[64,512]{1,0:T(8,128)S(1)}, u32[]{:S(2)}, u32[]{:S(2)}) collective-permute-start(f32[64,512]{1,0:T(8,128)S(1)} %shard_map.43), channel_id=1, source_target_pairs={{0,1},{4,5},{8,9},{12,13},{16,17},{20,21},{24,25},{28,29},{32,33},... | collective-permute-start | bytes 393224 | tf_op jit(solution)/shard_map/ppermute | solution.py:230
  49.5 5.0 %collective-permute-start.18 = (f32[64,512]{1,0:T(8,128)S(1)}, f32[64,512]{1,0:T(8,128)S(1)}, u32[]{:S(2)}, u32[]{:S(2)}) collective-permute-start(f32[64,512]{1,0:T(8,128)S(1)} %shard_map.43), channel_id=1, source_target_pairs={{0,3},{4,7},{8,11},{12,15},{16,19},{20,23},{24,27},{28,31},{32,35}... | collective-permute-start | bytes 393224 | tf_op jit(solution)/shard_map/ppermute | solution.py:230
  50.8 5.1 %collective-permute-start.17 = (f32[64,512]{1,0:T(8,128)S(1)}, f32[64,512]{1,0:T(8,128)S(1)}, u32[]{:S(2)}, u32[]{:S(2)}) collective-permute-start(f32[64,512]{1,0:T(8,128)S(1)} %shard_map.43), channel_id=1, source_target_pairs={{0,2},{4,6},{8,10},{12,14},{16,18},{20,22},{24,26},{28,30},{32,34}... | collective-permute-start | bytes 393224 | tf_op jit(solution)/shard_map/ppermute | solution.py:230
  53.2 7.9 %collective-permute-start.16 = (f32[64,512]{1,0:T(8,128)S(1)}, f32[64,512]{1,0:T(8,128)S(1)}, u32[]{:S(2)}, u32[]{:S(2)}) collective-permute-start(f32[64,512]{1,0:T(8,128)S(1)} %get-tuple-element.46), channel_id=1, source_target_pairs={{1,0},{5,4},{9,8},{13,12},{17,16},{21,20},{25,24},{29,28},{33,32},... | collective-permute-start | bytes 393224 | tf_op jit(solution)/shard_map/ppermute | solution.py:230

commit v5 on v3

v5 whole, which is shorter than its diff:
```python
import jax
import jax.numpy as jnp
from jax import lax
from jax.experimental import pallas as pl
from jax.experimental.pallas import tpu as pltpu
from jax.sharding import PartitionSpec as P

AXES = ("wide", "narrow")
Y, Z, CORES, X = 4, 16, 2, 4
SNAPS, MODES = 512, 64


def at(y, z, core, x):
    return ((y * Z + z) * CORES + core) * X + x


EVERY = [(y, z, core, x) for y in range(Y) for z in range(Z) for core in range(CORES) for x in range(X)]


def split(value):
    high = value.astype(jnp.bfloat16)
    return high, (value - high.astype(jnp.float32)).astype(jnp.bfloat16)


def times(coefficient, factor):
    dims = (((1,), (1,)), ((), ()))
    c_high, c_low = split(coefficient)
    f_high, f_low = split(factor)
    both = lax.dot_general(
        jnp.concatenate([c_high, c_low], 0), f_high, dims, preferred_element_type=jnp.float32
    )
    cross = lax.dot_general(c_high, f_low, dims, preferred_element_type=jnp.float32)
    return both[:MODES] + (both[MODES:] + cross)


WORK_8, WORK_7, WORK_5 = 0, 3 * 10**9, 0


def place():
    wide, x = lax.axis_index("wide"), lax.axis_index("narrow")
    return wide // (CORES * Z), (wide // CORES) % Z, wide % CORES, x


FACTOR = (SNAPS, SNAPS)
COEF = (MODES, SNAPS)
HBM, VMEM = pl.BlockSpec(memory_space=pltpu.HBM), pl.BlockSpec(memory_space=pltpu.VMEM)


def kernel_call(body, operands, near, outs, scratch, work=0, limit=12):
    return pl.pallas_call(
        body,
        out_shape=[
            pltpu.VMEM(shape, jnp.float32) if keep else jax.ShapeDtypeStruct(shape, jnp.float32)
            for shape, keep in outs
        ],
        in_specs=[VMEM if n else HBM for n in near],
        out_specs=[VMEM for _ in outs],
        scratch_shapes=scratch,
        compiler_params=pltpu.CompilerParams(vmem_limit_bytes=limit << 20),
        cost_estimate=pl.CostEstimate(flops=work, bytes_accessed=0, transcendentals=0),
    )(*operands)


def half(ref, which):
    return ref.at[pl.ds(which * SNAPS, SNAPS), :]


def cut_kernel(factors, upper, other, sems):
    y, z, core, x = place()
    swap = (core == 1) & (x == 0)
    cut = pltpu.make_async_copy(half(factors, 0), upper, sems.at[0])
    cut_up = pltpu.make_async_copy(half(factors, 0), other, sems.at[1])
    cut_low = pltpu.make_async_copy(half(factors, 1), other, sems.at[1])
    cut.start()
    pl.when(swap)(cut_up.start)
    pl.when(~swap)(cut_low.start)
    cut.wait()
    cut_low.wait()


def root_kernel(basis, upper, other, up, low):
    y, z, core, x = place()

    @pl.when((y == 2) & (z == 0) & (core == 0) & (x == 0))
    def _():
        up[...] = times(basis[...], upper[...])
        low[...] = times(basis[...], other[...])


def level_8_kernel(from_a, from_b, upper, other, up, low):
    y, z, core, x = place()
    for y_here, coef in ((1, from_a), (3, from_b)):
        @pl.when((y == y_here) & (z == 0) & (core == 0) & (x == 0))
        def _():
            low[...] = times(coef[...], other[...])
            up[...] = times(coef[...], upper[...])


def level_7_6_kernel(c4_odd, c4_even, c12_odd, c12_even, own, early_a, early_b, up, low, held):
    y, z, core, x = place()
    for z_here, source, coefs in ((4, early_a, (c4_even, c4_odd)), (12, early_b, (c12_even, c12_odd))):
        @pl.when((z == z_here) & (core == 0) & (x == 0))
        def _():
            for odd, coef in enumerate(coefs):
                @pl.when(y % 2 == odd)
                def _():
                    held[...] = coef[...]
            held[...] = times(held[...], source[...])
            up[...] = times(held[...], own[:SNAPS, :])
            low[...] = times(held[...], own[SNAPS:, :])


def level_5_kernel(c_left, c_right, own, up, low):
    y, z, core, x = place()
    for z_here, coef in ((2, c_left), (6, c_right)):
        @pl.when((z % 8 == z_here) & (core == 0) & (x == 0))
        def _():
            up[...] = times(coef[...], own[:SNAPS, :])
            low[...] = times(coef[...], own[SNAPS:, :])


def level_4_kernel(c_0, c_1, c_3, c_own, own, early_a, early_c, early_d, out, held):
    y, z, core, x = place()

    @pl.when((core == 0) & (x == 0))
    def _():
        is_late = (z == LATE[0]) | (z == LATE[1]) | (z == LATE[2])
        for k, coef in ((0, c_0), (1, c_1), (3, c_3), (2, c_own)):
            @pl.when(z % 4 == k)
            def _():
                held[...] = coef[...]

        @pl.when(z % 2 == 1)
        def _():
            out[...] = times(held[...], own[SNAPS:, :])

        @pl.when(is_late)
        def _():
            out[...] = times(held[...], early_c[...])

        @pl.when((z % 2 == 0) & ~is_late)
        def _():
            out[...] = times(held[...], early_a[...])


def level_3_kernel(here, over, own, early_a, early_b, out):
    y, z, core, x = place()

    @pl.when((core == 1) & (x == 0))
    def _():
        out[...] = times(over[...], own[SNAPS:, :])

    @pl.when((core == 0) & (x == 0) & (z == 12))
    def _():
        out[...] = times(here[...], early_a[...])

    @pl.when((core == 0) & (x == 0) & (z != 12))
    def _():
        out[...] = times(here[...], early_b[...])


def leaf_kernel(c2, c2_x1, c2_x2, c2_x3, own, early_a, early_b, early_d, early_e, leaf, out, held):
    y, z, core, x = place()

    for source, mine in ((early_a, (core == 1) | (z % 2 == 1)), (early_d, (core == 0) & (z % 2 == 0))):
        @pl.when((x == 0) & mine)
        def _():
            held[...] = times(times(c2[...], early_e[...]), source[...])

    @pl.when(x == 1)
    def _():
        held[...] = times(times(c2_x1[...], early_a[...]), own[SNAPS:, :])

    @pl.when(x == 2)
    def _():
        held[...] = times(times(c2_x2[...], own[SNAPS:, :]), early_a[...])

    @pl.when(x == 3)
    def _():
        held[...] = times(times(c2_x3[...], early_b[...]), own[SNAPS:, :])

    out[...] = times(held[...], leaf[...])


LATE = (4, 6, 12)


def send(block, route):
    return lax.ppermute(block, AXES, route)


def on_device(node_factors, leaf_q, modal_basis):
    DMA = pltpu.SemaphoreType.DMA
    coef, block = pltpu.VMEM(COEF, jnp.float32), pltpu.VMEM(FACTOR, jnp.float32)

    upper, other = kernel_call(
        cut_kernel, [node_factors], [0], [(FACTOR, 1), (FACTOR, 1)], [DMA((2,))], limit=58
    )
    up, low = kernel_call(root_kernel, [modal_basis.T, upper, other], [1] * 3, [(COEF, 1), (COEF, 1)], [])
    to_y1 = send(up, [(at(2, 0, 0, 0), at(1, 0, 0, 0))])
    to_y3 = send(low, [(at(2, 0, 0, 0), at(3, 0, 0, 0))])

    early_a = send(
        upper,
        [(at(y, z, c, x), at(y, z, c, x - 1)) for y, z, c, x in EVERY if x >= 2]
        + [(at(y, 8, 0, 0), at(y, 4, 0, 0)) for y in range(Y)]
        + [(at(y, z + 1, 0, 0), at(y, z, 0, 0)) for y in range(Y) for z in range(0, Z, 2) if z not in LATE]
        + [(at(y, 12, 1, 0), at(y, 12, 0, 0)) for y in range(Y)]
        + [(at(y, z, c, 1), at(y, z, c, 0)) for y, z, c, x in EVERY if x == 1 and (c == 1 or z % 2 == 1)],
    )
    early_b = send(
        other,
        [(at(y, z, c, 2), at(y, z, c, 3)) for y, z, c, x in EVERY if x == 2]
        + [(at(y, 8, 0, 0), at(y, 12, 0, 0)) for y in range(Y)]
        + [(at(y, z, 1, 0), at(y, z, 0, 0)) for y in range(Y) for z in range(Z) if z != 12],
    )
    early_d = send(upper, [(at(y, z, 0, 1), at(y, z, 0, 0)) for y in range(Y) for z in range(0, Z, 2)])
    early_e = send(upper, [(at(y, z, c, 2), at(y, z, c, 0)) for y, z, c, x in EVERY if x == 2])

    up, low = kernel_call(
        level_8_kernel, [to_y1, to_y3, upper, other], [1] * 4, [(COEF, 1), (COEF, 1)], [], WORK_8
    )
    c7 = [
        send(block_, [(at(y, 0, 0, 0), at(y - 1 + k, zt, 0, 0)) for y in (1, 3)])
        for zt in (4, 12) for k, block_ in ((1, low), (0, up))
    ]
    *c7, upper = lax.optimization_barrier((*c7, upper))
    early_c = send(upper, [(at(y, z + 1, 0, 0), at(y, z, 0, 0)) for y in range(Y) for z in LATE])
    *c7, early_a, early_b = lax.optimization_barrier((*c7, early_a, early_b))
    up, low = kernel_call(
        level_7_6_kernel, [*c7, node_factors, early_a, early_b], [1] * 7, [(COEF, 1), (COEF, 1)], [coef], WORK_7
    )
    c5 = [
        send(block_, [(at(y, z, 0, 0), at(y, z + step, 0, 0)) for y in range(Y) for z in (4, 12)])
        for block_, step in ((up, -2), (low, 2))
    ]
    up, low = kernel_call(
        level_5_kernel, [*c5, node_factors], [1] * 3, [(COEF, 1), (COEF, 1)], [], WORK_5
    )
    c4 = [
        send(block_, [(at(y, z, 0, 0), at(y, z + step, 0, 0)) for y in range(Y) for z in range(2, Z, 4)])
        for block_, step in ((up, -2), (up, -1), (low, 1))
    ]
    (c3,) = kernel_call(
        level_4_kernel, [*c4, low, node_factors, early_a, early_c, early_d], [1] * 7 + [0], [(COEF, 1)], [coef]
    )
    over = send(c3, [(at(y, z, 0, 0), at(y, z, 1, 0)) for y in range(Y) for z in range(Z)])
    (c2,) = kernel_call(
        level_3_kernel, [c3, over, node_factors, early_a, early_b], [1] * 5, [(COEF, 1)], []
    )
    spread = [
        send(c2, [(at(y, z, c, 0), at(y, z, c, xt)) for y, z, c, x in EVERY if x == 0])
        for xt in (1, 2, 3)
    ]
    (modes,) = kernel_call(
        leaf_kernel, [c2, *spread, node_factors, early_a, early_b, early_d, early_e, leaf_q], [1] * 10,
        [(COEF, 0)], [coef],
    )
    return modes.T


def solution(mesh):
    return jax.shard_map(
        on_device,
        mesh=mesh,
        in_specs=(P(AXES, None), P(AXES, None), P()),
        out_specs=P(AXES, None),
        check_vma=False,
    )
```

time: 68.2 us -> 58 us (0.85)
  waiting for transfers between devices: 33.1 us -> 26.1 us
  starting transfers between devices: 28.5 us -> 25.7 us
    ppermute x19 -> x20, waiting for transfers between devices: 33.1 us -> 26.1 us  [send(): return lax.ppermute(block, AXES, route)]
    ppermute x19 -> x20, starting transfers between devices: 28.5 us -> 25.7 us  [send(): return lax.ppermute(block, AXES, route)]
    pallas_call x1 -> x0, Pallas kernels: 1.12 us -> none  [on_device(): pl.pallas_call(last_kernel, out_shape=[jax.ShapeDtypeStruct(COEF, jnp.flo...]
    pallas_call x8, Pallas kernels: 4.64 us -> 5.45 us  [kernel_call(): pl.pallas_call(body, out_shape=[pltpu.VMEM(shape, jnp.float32) if keep el...]
  transfers between devices with their start and end apart: 19 -> 20, of which waited for: 8 -> 6; matrix products, arithmetic and copies ran while one was open for 0% -> 0% of each run, Pallas kernels for 2% -> 3%
where the time goes in v5:
time: 58 us; the launch traced here: 57.6 us
  waiting for transfers between devices  26.1 us (45%)
  starting transfers between devices  25.7 us (44%)
  Pallas kernels  5.45 us (9%)
    ppermute x20, waiting for transfers between devices, send(): return lax.ppermute(block, AXES, route)  26.1 us
    ppermute x20, starting transfers between devices, send(): return lax.ppermute(block, AXES, route)  25.7 us
    pallas_call x8, Pallas kernels, kernel_call(): pl.pallas_call(body, out_shape=[pltpu.VMEM(shape, jnp.float32) if keep el...  5.45 us
  transfers between devices with their start and end apart: 20, of which 6 were waited for; matrix products, arithmetic and copies ran while one was open for 0% of the time, Pallas kernels for 3%

profile of v5, /device:TPU:24, one launch (start us, length us, event | category | flops | bytes accessed | tf_op | source)
XLA Modules:
  0.0 57.6 jit_solution(5454347261068298540)
XLA Ops:
  0.0 1.6 %shard_map.37 = (f32[512,512]{1,0:T(8,128)S(1)}, f32[512,512]{1,0:T(8,128)S(1)}) custom-call(f32[1024,512]{1,0:T(8,128)} %own.9), custom_call_target="tpu_custom_call" | custom-call | tf_op jit(solution)/shard_map/pallas_call | solution.py:50
  1.6 1.3 %collective-permute-start.6 = (f32[512,512]{1,0:T(8,128)S(1)}, f32[512,512]{1,0:T(8,128)S(1)}, u32[]{:S(2)}, u32[]{:S(2)}) collective-permute-start(f32[512,512]{1,0:T(8,128)S(1)} %get-tuple-element.46.upper), channel_id=1, source_target_pairs={{2,1},{3,2},{6,5},{7,6},{10,9},{11,10},{14,13},{15,14},{18,17},{19... | collective-permute-start | bytes 3145736 | tf_op jit(solution)/shard_map/ppermute | solution.py:189
  2.9 1.3 %collective-permute-start.7 = (f32[512,512]{1,0:T(8,128)S(1)}, f32[512,512]{1,0:T(8,128)S(1)}, u32[]{:S(2)}, u32[]{:S(2)}) collective-permute-start(f32[512,512]{1,0:T(8,128)S(1)} %get-tuple-element.27.other), channel_id=1, source_target_pairs={{2,3},{6,7},{10,11},{14,15},{18,19},{22,23},{26,27},{30,31},{34,35... | collective-permute-start | bytes 3145736 | tf_op jit(solution)/shard_map/ppermute | solution.py:189
  4.2 0.0 copy-done.2
  4.2 0.0 copy-start
  4.3 0.8 %collective-permute-start = (f32[64,512]{1,0:T(8,128)S(1)}, f32[64,512]{1,0:T(8,128)S(1)}, u32[]{:S(2)}, u32[]{:S(2)}) collective-permute-start(f32[64,512]{1,0:T(8,128)S(1)} %get-tuple-element.28), channel_id=1, source_target_pairs={{256,128}} | collective-permute-start | bytes 393224 | tf_op jit(solution)/shard_map/ppermute | solution.py:189
  5.1 1.3 %collective-permute-start.1 = (f32[64,512]{1,0:T(8,128)S(1)}, f32[64,512]{1,0:T(8,128)S(1)}, u32[]{:S(2)}, u32[]{:S(2)}) collective-permute-start(f32[64,512]{1,0:T(8,128)S(1)} %get-tuple-element.29), channel_id=1, source_target_pairs={{256,384}} | collective-permute-start | bytes 393224 | tf_op jit(solution)/shard_map/ppermute | solution.py:189
  6.4 0.0 collective-permute-done.from_a
  6.4 5.6 %collective-permute-done.1.from_b = f32[64,512]{1,0:T(8,128)S(1)} collective-permute-done((f32[64,512]{1,0:T(8,128)S(1)}, f32[64,512]{1,0:T(8,128)S(1)}, u32[]{:S(2)}, u32[]{:S(2)}) %collective-permute-start.1) | collective-permute-done | bytes 131104 | tf_op jit(solution)/shard_map/ppermute | solution.py:189
  11.9 0.8 %shard_map.39 = (f32[64,512]{1,0:T(8,128)S(1)}, f32[64,512]{1,0:T(8,128)S(1)}) custom-call(f32[64,512]{1,0:T(8,128)S(1)} %collective-permute-done.from_a, f32[64,512]{1,0:T(8,128)S(1)} %collective-permute-done.1.from_b, f32[512,512]{1,0:T(8,128)S(1)} %get-tuple-element.46.upper, f32[512,512]{1,0:T(8,128)S(1)} %get-tuple-element.27.other), custom_call_target="tpu_custom_call" | custom-call | tf_op jit(solution)/shard_map/pallas_call | solution.py:50
  12.7 2.2 %collective-permute-start.2 = (f32[64,512]{1,0:T(8,128)S(1)}, f32[64,512]{1,0:T(8,128)S(1)}, u32[]{:S(2)}, u32[]{:S(2)}) collective-permute-start(f32[64,512]{1,0:T(8,128)S(1)} %get-tuple-element.30), channel_id=1, source_target_pairs={{128,160},{384,416}} | collective-permute-start | bytes 393224 | tf_op jit(solution)/shard_map/ppermute | solution.py:189
  14.9 1.3 %collective-permute-start.3 = (f32[64,512]{1,0:T(8,128)S(1)}, f32[64,512]{1,0:T(8,128)S(1)}, u32[]{:S(2)}, u32[]{:S(2)}) collective-permute-start(f32[64,512]{1,0:T(8,128)S(1)} %get-tuple-element.31), channel_id=1, source_target_pairs={{128,32},{384,288}} | collective-permute-start | bytes 393224 | tf_op jit(solution)/shard_map/ppermute | solution.py:189
  16.2 3.7 %collective-permute-start.4 = (f32[64,512]{1,0:T(8,128)S(1)}, f32[64,512]{1,0:T(8,128)S(1)}, u32[]{:S(2)}, u32[]{:S(2)}) collective-permute-start(f32[64,512]{1,0:T(8,128)S(1)} %get-tuple-element.30), channel_id=1, source_target_pairs={{128,224},{384,480}} | collective-permute-start | bytes 393224 | tf_op jit(solution)/shard_map/ppermute | solution.py:189
  19.9 0.0 collective-permute-done.2.c4_odd
  19.9 1.3 %collective-permute-start.5 = (f32[64,512]{1,0:T(8,128)S(1)}, f32[64,512]{1,0:T(8,128)S(1)}, u32[]{:S(2)}, u32[]{:S(2)}) collective-permute-start(f32[64,512]{1,0:T(8,128)S(1)} %get-tuple-element.31), channel_id=1, source_target_pairs={{128,96},{384,352}} | collective-permute-start | bytes 393224 | tf_op jit(solution)/shard_map/ppermute | solution.py:189
  21.2 0.0 collective-permute-done.3.c4_even
  21.2 1.3 %collective-permute-start.14 = (f32[512,512]{1,0:T(8,128)S(1)}, f32[512,512]{1,0:T(8,128)S(1)}, u32[]{:S(2)}, u32[]{:S(2)}) collective-permute-start(f32[512,512]{1,0:T(8,128)S(1)} %get-tuple-element.46.upper), channel_id=1, source_target_pairs={{1,0},{17,16},{33,32},{49,48},{65,64},{81,80},{97,96},{113,112},{1... | collective-permute-start | bytes 3145736 | tf_op jit(solution)/shard_map/ppermute | solution.py:189
  22.5 0.0 collective-permute-done.4.c12_odd
  22.6 1.3 %collective-permute-done.5.c12_even = f32[64,512]{1,0:T(8,128)S(1)} collective-permute-done((f32[64,512]{1,0:T(8,128)S(1)}, f32[64,512]{1,0:T(8,128)S(1)}, u32[]{:S(2)}, u32[]{:S(2)}) %collective-permute-start.5) | collective-permute-done | bytes 131104 | tf_op jit(solution)/shard_map/ppermute | solution.py:189
  23.8 0.7 %collective-permute-start.13 = (f32[512,512]{1,0:T(8,128)S(1)}, f32[512,512]{1,0:T(8,128)S(1)}, u32[]{:S(2)}, u32[]{:S(2)}) collective-permute-start(f32[512,512]{1,0:T(8,128)S(1)} %get-tuple-element.46.upper), channel_id=1, source_target_pairs={{40,32},{56,48},{104,96},{168,160},{184,176},{232,224},{296,288},{... | collective-permute-start | bytes 3145736 | tf_op jit(solution)/shard_map/ppermute | solution.py:189
  24.6 1.3 %collective-permute-start.19 = (f32[512,512]{1,0:T(8,128)S(1)}, f32[512,512]{1,0:T(8,128)S(1)}, u32[]{:S(2)}, u32[]{:S(2)}) collective-permute-start(f32[512,512]{1,0:T(8,128)S(1)} %get-tuple-element.46.upper), channel_id=1, source_target_pairs={{2,0},{6,4},{10,8},{14,12},{18,16},{22,20},{26,24},{30,28},{34,32}... | collective-permute-start | bytes 3145736 | tf_op jit(solution)/shard_map/ppermute | solution.py:189
  25.9 0.0 collective-permute-done.6.early_a
  25.9 0.0 collective-permute-done.7.early_b
  25.9 0.0 copy-done
  25.9 0.7 %collective-permute-start.8 = (f32[64,512]{1,0:T(8,128)S(1)}, f32[64,512]{1,0:T(8,128)S(1)}, u32[]{:S(2)}, u32[]{:S(2)}) collective-permute-start(f32[64,512]{1,0:T(8,128)S(1)} %get-tuple-element.42), channel_id=1, source_target_pairs={{32,16},{96,80},{160,144},{224,208},{288,272},{352,336},{416,400},... | collective-permute-start | bytes 393224 | tf_op jit(solution)/shard_map/ppermute | solution.py:189
  26.6 0.7 %collective-permute-start.9 = (f32[64,512]{1,0:T(8,128)S(1)}, f32[64,512]{1,0:T(8,128)S(1)}, u32[]{:S(2)}, u32[]{:S(2)}) collective-permute-start(f32[64,512]{1,0:T(8,128)S(1)} %get-tuple-element.43), channel_id=1, source_target_pairs={{32,48},{96,112},{160,176},{224,240},{288,304},{352,368},{416,432}... | collective-permute-start | bytes 393224 | tf_op jit(solution)/shard_map/ppermute | solution.py:189
  27.3 0.0 collective-permute-done.8.c_left
  27.3 0.0 collective-permute-done.9.c_right
  27.4 1.3 %collective-permute-start.10 = (f32[64,512]{1,0:T(8,128)S(1)}, f32[64,512]{1,0:T(8,128)S(1)}, u32[]{:S(2)}, u32[]{:S(2)}) collective-permute-start(f32[64,512]{1,0:T(8,128)S(1)} %get-tuple-element.44), channel_id=1, source_target_pairs={{16,0},{48,32},{80,64},{112,96},{144,128},{176,160},{208,192},{240... | collective-permute-start | bytes 393224 | tf_op jit(solution)/shard_map/ppermute | solution.py:189
  28.7 0.7 %collective-permute-start.11 = (f32[64,512]{1,0:T(8,128)S(1)}, f32[64,512]{1,0:T(8,128)S(1)}, u32[]{:S(2)}, u32[]{:S(2)}) collective-permute-start(f32[64,512]{1,0:T(8,128)S(1)} %get-tuple-element.44), channel_id=1, source_target_pairs={{16,8},{48,40},{80,72},{112,104},{144,136},{176,168},{208,200},{24... | collective-permute-start | bytes 393224 | tf_op jit(solution)/shard_map/ppermute | solution.py:189
  29.3 8.6 %collective-permute-done.14.early_d = f32[512,512]{1,0:T(8,128)S(1)} collective-permute-done((f32[512,512]{1,0:T(8,128)S(1)}, f32[512,512]{1,0:T(8,128)S(1)}, u32[]{:S(2)}, u32[]{:S(2)}) %collective-permute-start.14) | collective-permute-done | bytes 1048608 | tf_op jit(solution)/shard_map/ppermute | solution.py:189
  37.9 0.7 %collective-permute-start.12 = (f32[64,512]{1,0:T(8,128)S(1)}, f32[64,512]{1,0:T(8,128)S(1)}, u32[]{:S(2)}, u32[]{:S(2)}) collective-permute-start(f32[64,512]{1,0:T(8,128)S(1)} %get-tuple-element.45.c_own), channel_id=1, source_target_pairs={{16,24},{48,56},{80,88},{112,120},{144,152},{176,184},{208,216},{2... | collective-permute-start | bytes 393224 | tf_op jit(solution)/shard_map/ppermute | solution.py:189
  38.6 3.1 %collective-permute-done.10.c_0 = f32[64,512]{1,0:T(8,128)S(1)} collective-permute-done((f32[64,512]{1,0:T(8,128)S(1)}, f32[64,512]{1,0:T(8,128)S(1)}, u32[]{:S(2)}, u32[]{:S(2)}) %collective-permute-start.10) | collective-permute-done | bytes 131104 | tf_op jit(solution)/shard_map/ppermute | solution.py:189
  41.8 0.0 collective-permute-done.11.c_1
  41.8 0.0 collective-permute-done.12.c_3
  41.8 0.0 collective-permute-done.13.early_c
  41.8 0.5 shard_map.42.here
  42.3 1.4 %collective-permute-start.15 = (f32[64,512]{1,0:T(8,128)S(1)}, f32[64,512]{1,0:T(8,128)S(1)}, u32[]{:S(2)}, u32[]{:S(2)}) collective-permute-start(f32[64,512]{1,0:T(8,128)S(1)} %shard_map.42.here), channel_id=1, source_target_pairs={{0,4},{8,12},{16,20},{24,28},{32,36},{40,44},{48,52},{56,60},{64,6... | collective-permute-start | bytes 393224 | tf_op jit(solution)/shard_map/ppermute | solution.py:189
  43.7 1.0 %collective-permute-done.15.over = f32[64,512]{1,0:T(8,128)S(1)} collective-permute-done((f32[64,512]{1,0:T(8,128)S(1)}, f32[64,512]{1,0:T(8,128)S(1)}, u32[]{:S(2)}, u32[]{:S(2)}) %collective-permute-start.15) | collective-permute-done | bytes 131104 | tf_op jit(solution)/shard_map/ppermute | solution.py:189
  44.7 0.5 shard_map.43.c2
  45.2 1.3 %collective-permute-start.16 = (f32[64,512]{1,0:T(8,128)S(1)}, f32[64,512]{1,0:T(8,128)S(1)}, u32[]{:S(2)}, u32[]{:S(2)}) collective-permute-start(f32[64,512]{1,0:T(8,128)S(1)} %shard_map.43.c2), channel_id=1, source_target_pairs={{0,1},{4,5},{8,9},{12,13},{16,17},{20,21},{24,25},{28,29},{32,33},... | collective-permute-start | bytes 393224 | tf_op jit(solution)/shard_map/ppermute | solution.py:189
  46.5 1.3 %collective-permute-start.17 = (f32[64,512]{1,0:T(8,128)S(1)}, f32[64,512]{1,0:T(8,128)S(1)}, u32[]{:S(2)}, u32[]{:S(2)}) collective-permute-start(f32[64,512]{1,0:T(8,128)S(1)} %shard_map.43.c2), channel_id=1, source_target_pairs={{0,2},{4,6},{8,10},{12,14},{16,18},{20,22},{24,26},{28,30},{32,34}... | collective-permute-start | bytes 393224 | tf_op jit(solution)/shard_map/ppermute | solution.py:189
  47.8 1.3 %collective-permute-start.18 = (f32[64,512]{1,0:T(8,128)S(1)}, f32[64,512]{1,0:T(8,128)S(1)}, u32[]{:S(2)}, u32[]{:S(2)}) collective-permute-start(f32[64,512]{1,0:T(8,128)S(1)} %shard_map.43.c2), channel_id=1, source_target_pairs={{0,3},{4,7},{8,11},{12,15},{16,19},{20,23},{24,27},{28,31},{32,35}... | collective-permute-start | bytes 393224 | tf_op jit(solution)/shard_map/ppermute | solution.py:189
  49.1 6.5 %collective-permute-done.19.early_e = f32[512,512]{1,0:T(8,128)S(1)} collective-permute-done((f32[512,512]{1,0:T(8,128)S(1)}, f32[512,512]{1,0:T(8,128)S(1)}, u32[]{:S(2)}, u32[]{:S(2)}) %collective-permute-start.19) | collective-permute-done | bytes 1048608 | tf_op jit(solution)/shard_map/ppermute | solution.py:189
  55.6 0.0 collective-permute-done.16.c2_x1
  55.6 0.0 collective-permute-done.17.c2_x2
  55.6 0.0 collective-permute-done.18.c2_x3
  55.6 2.0 %shard_map.44 = f32[64,512]{1,0:T(8,128)} custom-call(f32[64,512]{1,0:T(8,128)S(1)} %shard_map.43.c2, f32[64,512]{1,0:T(8,128)S(1)} %collective-permute-done.16.c2_x1, f32[64,512]{1,0:T(8,128)S(1)} %collective-permute-done.17.c2_x2, f32[64,512]{1,0:T(8,128)S(1)} %collective-permute-done.18.c2_x3, f32[1024,512]{1,0:T(8,128)S(1)} %copy-done, ...), custom_call_target="tpu_custom_call" | custom-call | tf_op jit(solution)/shard_map/pallas_call | solution.py:50
  (6 shorter events, 0.1 us)
Async XLA Ops:
  0.0 4.2 %copy-start.2 = (f32[512,64]{0,1:T(8,128)S(1)}, f32[512,64]{0,1:T(8,128)}, u32[]{:S(2)}) copy-start(f32[512,64]{0,1:T(8,128)} %param.5) | copy-start | bytes 393220
  1.6 24.3 %collective-permute-start.6 = (f32[512,512]{1,0:T(8,128)S(1)}, f32[512,512]{1,0:T(8,128)S(1)}, u32[]{:S(2)}, u32[]{:S(2)}) collective-permute-start(f32[512,512]{1,0:T(8,128)S(1)} %get-tuple-element.46.upper), channel_id=1, source_target_pairs={{2,1},{3,2},{6,5},{7,6},{10,9},{11,10},{14,13},{15,14},{18,17},{19... | collective-permute-start | bytes 3145736 | tf_op jit(solution)/shard_map/ppermute | solution.py:189
  2.9 23.0 %collective-permute-start.7 = (f32[512,512]{1,0:T(8,128)S(1)}, f32[512,512]{1,0:T(8,128)S(1)}, u32[]{:S(2)}, u32[]{:S(2)}) collective-permute-start(f32[512,512]{1,0:T(8,128)S(1)} %get-tuple-element.27.other), channel_id=1, source_target_pairs={{2,3},{6,7},{10,11},{14,15},{18,19},{22,23},{26,27},{30,31},{34,35... | collective-permute-start | bytes 3145736 | tf_op jit(solution)/shard_map/ppermute | solution.py:189
  4.2 21.7 %copy-start = (f32[1024,512]{1,0:T(8,128)S(1)}, f32[1024,512]{1,0:T(8,128)}, u32[]{:S(2)}) copy-start(f32[1024,512]{1,0:T(8,128)} %own.9) | copy-start | bytes 6291460
  4.3 2.1 %collective-permute-start = (f32[64,512]{1,0:T(8,128)S(1)}, f32[64,512]{1,0:T(8,128)S(1)}, u32[]{:S(2)}, u32[]{:S(2)}) collective-permute-start(f32[64,512]{1,0:T(8,128)S(1)} %get-tuple-element.28), channel_id=1, source_target_pairs={{256,128}} | collective-permute-start | bytes 393224 | tf_op jit(solution)/shard_map/ppermute | solution.py:189
  5.1 6.9 %collective-permute-start.1 = (f32[64,512]{1,0:T(8,128)S(1)}, f32[64,512]{1,0:T(8,128)S(1)}, u32[]{:S(2)}, u32[]{:S(2)}) collective-permute-start(f32[64,512]{1,0:T(8,128)S(1)} %get-tuple-element.29), channel_id=1, source_target_pairs={{256,384}} | collective-permute-start | bytes 393224 | tf_op jit(solution)/shard_map/ppermute | solution.py:189
  12.7 7.2 %collective-permute-start.2 = (f32[64,512]{1,0:T(8,128)S(1)}, f32[64,512]{1,0:T(8,128)S(1)}, u32[]{:S(2)}, u32[]{:S(2)}) collective-permute-start(f32[64,512]{1,0:T(8,128)S(1)} %get-tuple-element.30), channel_id=1, source_target_pairs={{128,160},{384,416}} | collective-permute-start | bytes 393224 | tf_op jit(solution)/shard_map/ppermute | solution.py:189
  14.9 6.3 %collective-permute-start.3 = (f32[64,512]{1,0:T(8,128)S(1)}, f32[64,512]{1,0:T(8,128)S(1)}, u32[]{:S(2)}, u32[]{:S(2)}) collective-permute-start(f32[64,512]{1,0:T(8,128)S(1)} %get-tuple-element.31), channel_id=1, source_target_pairs={{128,32},{384,288}} | collective-permute-start | bytes 393224 | tf_op jit(solution)/shard_map/ppermute | solution.py:189
  16.2 6.3 %collective-permute-start.4 = (f32[64,512]{1,0:T(8,128)S(1)}, f32[64,512]{1,0:T(8,128)S(1)}, u32[]{:S(2)}, u32[]{:S(2)}) collective-permute-start(f32[64,512]{1,0:T(8,128)S(1)} %get-tuple-element.30), channel_id=1, source_target_pairs={{128,224},{384,480}} | collective-permute-start | bytes 393224 | tf_op jit(solution)/shard_map/ppermute | solution.py:189
  19.9 3.9 %collective-permute-start.5 = (f32[64,512]{1,0:T(8,128)S(1)}, f32[64,512]{1,0:T(8,128)S(1)}, u32[]{:S(2)}, u32[]{:S(2)}) collective-permute-start(f32[64,512]{1,0:T(8,128)S(1)} %get-tuple-element.31), channel_id=1, source_target_pairs={{128,96},{384,352}} | collective-permute-start | bytes 393224 | tf_op jit(solution)/shard_map/ppermute | solution.py:189
  21.2 16.7 %collective-permute-start.14 = (f32[512,512]{1,0:T(8,128)S(1)}, f32[512,512]{1,0:T(8,128)S(1)}, u32[]{:S(2)}, u32[]{:S(2)}) collective-permute-start(f32[512,512]{1,0:T(8,128)S(1)} %get-tuple-element.46.upper), channel_id=1, source_target_pairs={{1,0},{17,16},{33,32},{49,48},{65,64},{81,80},{97,96},{113,112},{1... | collective-permute-start | bytes 3145736 | tf_op jit(solution)/shard_map/ppermute | solution.py:189
  23.8 17.9 %collective-permute-start.13 = (f32[512,512]{1,0:T(8,128)S(1)}, f32[512,512]{1,0:T(8,128)S(1)}, u32[]{:S(2)}, u32[]{:S(2)}) collective-permute-start(f32[512,512]{1,0:T(8,128)S(1)} %get-tuple-element.46.upper), channel_id=1, source_target_pairs={{40,32},{56,48},{104,96},{168,160},{184,176},{232,224},{296,288},{... | collective-permute-start | bytes 3145736 | tf_op jit(solution)/shard_map/ppermute | solution.py:189
  24.6 31.0 %collective-permute-start.19 = (f32[512,512]{1,0:T(8,128)S(1)}, f32[512,512]{1,0:T(8,128)S(1)}, u32[]{:S(2)}, u32[]{:S(2)}) collective-permute-start(f32[512,512]{1,0:T(8,128)S(1)} %get-tuple-element.46.upper), channel_id=1, source_target_pairs={{2,0},{6,4},{10,8},{14,12},{18,16},{22,20},{26,24},{30,28},{34,32}... | collective-permute-start | bytes 3145736 | tf_op jit(solution)/shard_map/ppermute | solution.py:189
  25.9 1.4 %collective-permute-start.8 = (f32[64,512]{1,0:T(8,128)S(1)}, f32[64,512]{1,0:T(8,128)S(1)}, u32[]{:S(2)}, u32[]{:S(2)}) collective-permute-start(f32[64,512]{1,0:T(8,128)S(1)} %get-tuple-element.42), channel_id=1, source_target_pairs={{32,16},{96,80},{160,144},{224,208},{288,272},{352,336},{416,400},... | collective-permute-start | bytes 393224 | tf_op jit(solution)/shard_map/ppermute | solution.py:189
  26.6 0.7 %collective-permute-start.9 = (f32[64,512]{1,0:T(8,128)S(1)}, f32[64,512]{1,0:T(8,128)S(1)}, u32[]{:S(2)}, u32[]{:S(2)}) collective-permute-start(f32[64,512]{1,0:T(8,128)S(1)} %get-tuple-element.43), channel_id=1, source_target_pairs={{32,48},{96,112},{160,176},{224,240},{288,304},{352,368},{416,432}... | collective-permute-start | bytes 393224 | tf_op jit(solution)/shard_map/ppermute | solution.py:189
  27.4 14.4 %collective-permute-start.10 = (f32[64,512]{1,0:T(8,128)S(1)}, f32[64,512]{1,0:T(8,128)S(1)}, u32[]{:S(2)}, u32[]{:S(2)}) collective-permute-start(f32[64,512]{1,0:T(8,128)S(1)} %get-tuple-element.44), channel_id=1, source_target_pairs={{16,0},{48,32},{80,64},{112,96},{144,128},{176,160},{208,192},{240... | collective-permute-start | bytes 393224 | tf_op jit(solution)/shard_map/ppermute | solution.py:189
  28.7 13.1 %collective-permute-start.11 = (f32[64,512]{1,0:T(8,128)S(1)}, f32[64,512]{1,0:T(8,128)S(1)}, u32[]{:S(2)}, u32[]{:S(2)}) collective-permute-start(f32[64,512]{1,0:T(8,128)S(1)} %get-tuple-element.44), channel_id=1, source_target_pairs={{16,8},{48,40},{80,72},{112,104},{144,136},{176,168},{208,200},{24... | collective-permute-start | bytes 393224 | tf_op jit(solution)/shard_map/ppermute | solution.py:189
  37.9 3.8 %collective-permute-start.12 = (f32[64,512]{1,0:T(8,128)S(1)}, f32[64,512]{1,0:T(8,128)S(1)}, u32[]{:S(2)}, u32[]{:S(2)}) collective-permute-start(f32[64,512]{1,0:T(8,128)S(1)} %get-tuple-element.45.c_own), channel_id=1, source_target_pairs={{16,24},{48,56},{80,88},{112,120},{144,152},{176,184},{208,216},{2... | collective-permute-start | bytes 393224 | tf_op jit(solution)/shard_map/ppermute | solution.py:189
  42.3 13.3 %copy-start.1 = (f32[512,512]{1,0:T(8,128)S(1)}, f32[512,512]{1,0:T(8,128)}, u32[]{:S(2)}) copy-start(f32[512,512]{1,0:T(8,128)} %leaf.1) | copy-start | bytes 3145732
  42.3 2.4 %collective-permute-start.15 = (f32[64,512]{1,0:T(8,128)S(1)}, f32[64,512]{1,0:T(8,128)S(1)}, u32[]{:S(2)}, u32[]{:S(2)}) collective-permute-start(f32[64,512]{1,0:T(8,128)S(1)} %shard_map.42.here), channel_id=1, source_target_pairs={{0,4},{8,12},{16,20},{24,28},{32,36},{40,44},{48,52},{56,60},{64,6... | collective-permute-start | bytes 393224 | tf_op jit(solution)/shard_map/ppermute | solution.py:189
  45.2 10.4 %collective-permute-start.16 = (f32[64,512]{1,0:T(8,128)S(1)}, f32[64,512]{1,0:T(8,128)S(1)}, u32[]{:S(2)}, u32[]{:S(2)}) collective-permute-start(f32[64,512]{1,0:T(8,128)S(1)} %shard_map.43.c2), channel_id=1, source_target_pairs={{0,1},{4,5},{8,9},{12,13},{16,17},{20,21},{24,25},{28,29},{32,33},... | collective-permute-start | bytes 393224 | tf_op jit(solution)/shard_map/ppermute | solution.py:189
  46.5 9.1 %collective-permute-start.17 = (f32[64,512]{1,0:T(8,128)S(1)}, f32[64,512]{1,0:T(8,128)S(1)}, u32[]{:S(2)}, u32[]{:S(2)}) collective-permute-start(f32[64,512]{1,0:T(8,128)S(1)} %shard_map.43.c2), channel_id=1, source_target_pairs={{0,2},{4,6},{8,10},{12,14},{16,18},{20,22},{24,26},{28,30},{32,34}... | collective-permute-start | bytes 393224 | tf_op jit(solution)/shard_map/ppermute | solution.py:189
  47.8 7.8 %collective-permute-start.18 = (f32[64,512]{1,0:T(8,128)S(1)}, f32[64,512]{1,0:T(8,128)S(1)}, u32[]{:S(2)}, u32[]{:S(2)}) collective-permute-start(f32[64,512]{1,0:T(8,128)S(1)} %shard_map.43.c2), channel_id=1, source_target_pairs={{0,3},{4,7},{8,11},{12,15},{16,19},{20,23},{24,27},{28,31},{32,35}... | collective-permute-start | bytes 393224 | tf_op jit(solution)/shard_map/ppermute | solution.py:189

commit v6 on v5

--- a/solution.py
+++ b/solution.py
@@ -33,7 +33,7 @@
     return both[:MODES] + (both[MODES:] + cross)
 
 
-WORK_8, WORK_7, WORK_5 = 0, 3 * 10**9, 0
+WORK_8, WORK_7, WORK_5 = 0, 3 * 10**9, 7 * 10**9
 
 
 def place():
@@ -87,13 +87,15 @@
         low[...] = times(basis[...], other[...])
 
 
-def level_8_kernel(from_a, from_b, upper, other, up, low):
+def level_8_kernel(from_a, from_b, upper, other, up, low, up_far, low_far):
     y, z, core, x = place()
     for y_here, coef in ((1, from_a), (3, from_b)):
         @pl.when((y == y_here) & (z == 0) & (core == 0) & (x == 0))
         def _():
             low[...] = times(coef[...], other[...])
             up[...] = times(coef[...], upper[...])
+            low_far[...] = low[...]
+            up_far[...] = up[...]
 
 
 def level_7_6_kernel(c4_odd, c4_even, c12_odd, c12_even, own, early_a, early_b, up, low, held):
@@ -119,7 +121,7 @@
             low[...] = times(coef[...], own[SNAPS:, :])
 
 
-def level_4_kernel(c_0, c_1, c_3, c_own, own, early_a, early_c, early_d, out, held):
+def level_4_kernel(c_0, c_1, c_3, c_own, own, early_a, early_c, out, held):
     y, z, core, x = place()
 
     @pl.when((core == 0) & (x == 0))
@@ -159,13 +161,23 @@
         out[...] = times(here[...], early_b[...])
 
 
-def leaf_kernel(c2, c2_x1, c2_x2, c2_x3, own, early_a, early_b, early_d, early_e, leaf, out, held):
-    y, z, core, x = place()
-
-    for source, mine in ((early_a, (core == 1) | (z % 2 == 1)), (early_d, (core == 0) & (z % 2 == 0))):
-        @pl.when((x == 0) & mine)
-        def _():
-            held[...] = times(times(c2[...], early_e[...]), source[...])
+def pair_kernel(upper, early_a, out):
+    y, z, core, x = place()
+
+    @pl.when(x == 1)
+    def _():
+        a_high, a_low = split(upper[...])
+        b_high, b_low = split(early_a[...])
+        dot = lambda a, b: jnp.dot(a, b, preferred_element_type=jnp.float32)
+        out[...] = dot(a_high, b_high) + (dot(a_high, b_low) + dot(a_low, b_high))
+
+
+def leaf_kernel(c2, c2_x1, c2_x2, c2_x3, own, early_a, early_b, pair, leaf, out, held):
+    y, z, core, x = place()
+
+    @pl.when(x == 0)
+    def _():
+        held[...] = times(c2[...], pair[...])
 
     @pl.when(x == 1)
     def _():
@@ -205,8 +217,7 @@
         [(at(y, z, c, x), at(y, z, c, x - 1)) for y, z, c, x in EVERY if x >= 2]
         + [(at(y, 8, 0, 0), at(y, 4, 0, 0)) for y in range(Y)]
         + [(at(y, z + 1, 0, 0), at(y, z, 0, 0)) for y in range(Y) for z in range(0, Z, 2) if z not in LATE]
-        + [(at(y, 12, 1, 0), at(y, 12, 0, 0)) for y in range(Y)]
-        + [(at(y, z, c, 1), at(y, z, c, 0)) for y, z, c, x in EVERY if x == 1 and (c == 1 or z % 2 == 1)],
+        + [(at(y, 12, 1, 0), at(y, 12, 0, 0)) for y in range(Y)],
     )
     early_b = send(
         other,
@@ -214,15 +225,13 @@
         + [(at(y, 8, 0, 0), at(y, 12, 0, 0)) for y in range(Y)]
         + [(at(y, z, 1, 0), at(y, z, 0, 0)) for y in range(Y) for z in range(Z) if z != 12],
     )
-    early_d = send(upper, [(at(y, z, 0, 1), at(y, z, 0, 0)) for y in range(Y) for z in range(0, Z, 2)])
-    early_e = send(upper, [(at(y, z, c, 2), at(y, z, c, 0)) for y, z, c, x in EVERY if x == 2])
-
-    up, low = kernel_call(
-        level_8_kernel, [to_y1, to_y3, upper, other], [1] * 4, [(COEF, 1), (COEF, 1)], [], WORK_8
+
+    up, low, up_far, low_far = kernel_call(
+        level_8_kernel, [to_y1, to_y3, upper, other], [1] * 4, [(COEF, 1)] * 4, [], WORK_8
     )
     c7 = [
         send(block_, [(at(y, 0, 0, 0), at(y - 1 + k, zt, 0, 0)) for y in (1, 3)])
-        for zt in (4, 12) for k, block_ in ((1, low), (0, up))
+        for zt, k, block_ in ((4, 1, low), (4, 0, up), (12, 1, low_far), (12, 0, up_far))
     ]
     *c7, upper = lax.optimization_barrier((*c7, upper))
     early_c = send(upper, [(at(y, z + 1, 0, 0), at(y, z, 0, 0)) for y in range(Y) for z in LATE])
@@ -230,6 +239,9 @@
     up, low = kernel_call(
         level_7_6_kernel, [*c7, node_factors, early_a, early_b], [1] * 7, [(COEF, 1), (COEF, 1)], [coef], WORK_7
     )
+    early_x, up, low = lax.optimization_barrier((early_a, up, low))
+    (pair,) = kernel_call(pair_kernel, [upper, early_x], [1] * 2, [(FACTOR, 1)], [])
+    pair = send(pair, [(at(y, z, c, 1), at(y, z, c, 0)) for y, z, c, x in EVERY if x == 1])
     c5 = [
         send(block_, [(at(y, z, 0, 0), at(y, z + step, 0, 0)) for y in range(Y) for z in (4, 12)])
         for block_, step in ((up, -2), (low, 2))
@@ -242,7 +254,7 @@
         for block_, step in ((up, -2), (up, -1), (low, 1))
     ]
     (c3,) = kernel_call(
-        level_4_kernel, [*c4, low, node_factors, early_a, early_c, early_d], [1] * 7 + [0], [(COEF, 1)], [coef]
+        level_4_kernel, [*c4, low, node_factors, early_a, early_c], [1] * 7, [(COEF, 1)], [coef]
     )
     over = send(c3, [(at(y, z, 0, 0), at(y, z, 1, 0)) for y in range(Y) for z in range(Z)])
     (c2,) = kernel_call(
@@ -253,7 +265,7 @@
         for xt in (1, 2, 3)
     ]
     (modes,) = kernel_call(
-        leaf_kernel, [c2, *spread, node_factors, early_a, early_b, early_d, early_e, leaf_q], [1] * 10,
+        leaf_kernel, [c2, *spread, node_factors, early_a, early_b, pair, leaf_q], [1] * 9,
         [(COEF, 0)], [coef],
     )
     return modes.T

time: 58 us -> 57.8 us (level)
  waiting for transfers between devices: 26.1 us -> 27.6 us
  starting transfers between devices: 25.7 us -> 24.4 us
    ppermute x20 -> x19, waiting for transfers between devices: 26.1 us -> 27.6 us  [send(): return lax.ppermute(block, AXES, route)]
    ppermute x20 -> x19, starting transfers between devices: 25.7 us -> 24.4 us  [send(): return lax.ppermute(block, AXES, route)]
    pallas_call x8 -> x9, Pallas kernels: 5.45 us -> 5.06 us  [kernel_call(): pl.pallas_call(body, out_shape=[pltpu.VMEM(shape, jnp.float32) if keep el...]
  transfers between devices with their start and end apart: 20 -> 19, of which waited for: 6 -> 8; matrix products, arithmetic and copies ran while one was open for 0% -> 0% of each run, Pallas kernels for 3% -> 3%
where the time goes in v6:
time: 57.8 us; the launch traced here: 57.4 us
  waiting for transfers between devices  27.6 us (48%)
  starting transfers between devices  24.4 us (42%)
  Pallas kernels  5.06 us (9%)
    ppermute x19, waiting for transfers between devices, send(): return lax.ppermute(block, AXES, route)  27.6 us
    ppermute x19, starting transfers between devices, send(): return lax.ppermute(block, AXES, route)  24.4 us
    pallas_call x9, Pallas kernels, kernel_call(): pl.pallas_call(body, out_shape=[pltpu.VMEM(shape, jnp.float32) if keep el...  5.06 us
  transfers between devices with their start and end apart: 19, of which 8 were waited for; matrix products, arithmetic and copies ran while one was open for 0% of the time, Pallas kernels for 3%

profile of v6, /device:TPU:24, one launch (start us, length us, event | category | flops | bytes accessed | tf_op | source)
XLA Modules:
  0.0 57.4 jit_solution(9688272564470379626)
XLA Ops:
  0.0 1.6 %shard_map.37 = (f32[512,512]{1,0:T(8,128)S(1)}, f32[512,512]{1,0:T(8,128)S(1)}) custom-call(f32[1024,512]{1,0:T(8,128)} %own.9), custom_call_target="tpu_custom_call" | custom-call | tf_op jit(solution)/shard_map/pallas_call | solution.py:50
  1.6 1.3 %collective-permute-start.6 = (f32[512,512]{1,0:T(8,128)S(1)}, f32[512,512]{1,0:T(8,128)S(1)}, u32[]{:S(2)}, u32[]{:S(2)}) collective-permute-start(f32[512,512]{1,0:T(8,128)S(1)} %get-tuple-element.55.upper), channel_id=1, source_target_pairs={{2,1},{3,2},{6,5},{7,6},{10,9},{11,10},{14,13},{15,14},{18,17},{19... | collective-permute-start | bytes 3145736 | tf_op jit(solution)/shard_map/ppermute | solution.py:201
  2.9 1.3 %collective-permute-start.7 = (f32[512,512]{1,0:T(8,128)S(1)}, f32[512,512]{1,0:T(8,128)S(1)}, u32[]{:S(2)}, u32[]{:S(2)}) collective-permute-start(f32[512,512]{1,0:T(8,128)S(1)} %get-tuple-element.32.other), channel_id=1, source_target_pairs={{2,3},{6,7},{10,11},{14,15},{18,19},{22,23},{26,27},{30,31},{34,35... | collective-permute-start | bytes 3145736 | tf_op jit(solution)/shard_map/ppermute | solution.py:201
  4.2 0.0 copy-done.2
  4.2 0.0 copy-start
  4.3 0.8 %collective-permute-start = (f32[64,512]{1,0:T(8,128)S(1)}, f32[64,512]{1,0:T(8,128)S(1)}, u32[]{:S(2)}, u32[]{:S(2)}) collective-permute-start(f32[64,512]{1,0:T(8,128)S(1)} %get-tuple-element.33), channel_id=1, source_target_pairs={{256,128}} | collective-permute-start | bytes 393224 | tf_op jit(solution)/shard_map/ppermute | solution.py:201
  5.1 1.3 %collective-permute-start.1 = (f32[64,512]{1,0:T(8,128)S(1)}, f32[64,512]{1,0:T(8,128)S(1)}, u32[]{:S(2)}, u32[]{:S(2)}) collective-permute-start(f32[64,512]{1,0:T(8,128)S(1)} %get-tuple-element.34), channel_id=1, source_target_pairs={{256,384}} | collective-permute-start | bytes 393224 | tf_op jit(solution)/shard_map/ppermute | solution.py:201
  6.4 0.0 collective-permute-done.from_a
  6.4 5.6 %collective-permute-done.1.from_b = f32[64,512]{1,0:T(8,128)S(1)} collective-permute-done((f32[64,512]{1,0:T(8,128)S(1)}, f32[64,512]{1,0:T(8,128)S(1)}, u32[]{:S(2)}, u32[]{:S(2)}) %collective-permute-start.1) | collective-permute-done | bytes 131104 | tf_op jit(solution)/shard_map/ppermute | solution.py:201
  11.9 0.8 %shard_map.39 = (f32[64,512]{1,0:T(8,128)S(1)}, f32[64,512]{1,0:T(8,128)S(1)}, f32[64,512]{1,0:T(8,128)S(1)}, f32[64,512]{1,0:T(8,128)S(1)}) custom-call(f32[64,512]{1,0:T(8,128)S(1)} %collective-permute-done.from_a, f32[64,512]{1,0:T(8,128)S(1)} %collective-permute-done.1.from_b, f32[512,512]{1,0:T(8,128)S(1)} %get-tuple-element.55.upper, ...), custom_call_target="tpu_custom_call" | custom-call | tf_op jit(solution)/shard_map/pallas_call | solution.py:50
  12.7 2.2 %collective-permute-start.2 = (f32[64,512]{1,0:T(8,128)S(1)}, f32[64,512]{1,0:T(8,128)S(1)}, u32[]{:S(2)}, u32[]{:S(2)}) collective-permute-start(f32[64,512]{1,0:T(8,128)S(1)} %get-tuple-element.35), channel_id=1, source_target_pairs={{128,160},{384,416}} | collective-permute-start | bytes 393224 | tf_op jit(solution)/shard_map/ppermute | solution.py:201
  14.9 1.3 %collective-permute-start.3 = (f32[64,512]{1,0:T(8,128)S(1)}, f32[64,512]{1,0:T(8,128)S(1)}, u32[]{:S(2)}, u32[]{:S(2)}) collective-permute-start(f32[64,512]{1,0:T(8,128)S(1)} %get-tuple-element.36), channel_id=1, source_target_pairs={{128,32},{384,288}} | collective-permute-start | bytes 393224 | tf_op jit(solution)/shard_map/ppermute | solution.py:201
  16.2 3.7 %collective-permute-start.4 = (f32[64,512]{1,0:T(8,128)S(1)}, f32[64,512]{1,0:T(8,128)S(1)}, u32[]{:S(2)}, u32[]{:S(2)}) collective-permute-start(f32[64,512]{1,0:T(8,128)S(1)} %get-tuple-element.37), channel_id=1, source_target_pairs={{128,224},{384,480}} | collective-permute-start | bytes 393224 | tf_op jit(solution)/shard_map/ppermute | solution.py:201
  19.9 0.0 collective-permute-done.2.c4_odd
  19.9 1.3 %collective-permute-start.5 = (f32[64,512]{1,0:T(8,128)S(1)}, f32[64,512]{1,0:T(8,128)S(1)}, u32[]{:S(2)}, u32[]{:S(2)}) collective-permute-start(f32[64,512]{1,0:T(8,128)S(1)} %get-tuple-element.38), channel_id=1, source_target_pairs={{128,96},{384,352}} | collective-permute-start | bytes 393224 | tf_op jit(solution)/shard_map/ppermute | solution.py:201
  21.2 0.0 collective-permute-done.3.c4_even
  21.2 1.2 %collective-permute-done.4.c12_odd = f32[64,512]{1,0:T(8,128)S(1)} collective-permute-done((f32[64,512]{1,0:T(8,128)S(1)}, f32[64,512]{1,0:T(8,128)S(1)}, u32[]{:S(2)}, u32[]{:S(2)}) %collective-permute-start.4) | collective-permute-done | bytes 131104 | tf_op jit(solution)/shard_map/ppermute | solution.py:201
  22.4 1.4 %collective-permute-done.5.c12_even = f32[64,512]{1,0:T(8,128)S(1)} collective-permute-done((f32[64,512]{1,0:T(8,128)S(1)}, f32[64,512]{1,0:T(8,128)S(1)}, u32[]{:S(2)}, u32[]{:S(2)}) %collective-permute-start.5) | collective-permute-done | bytes 131104 | tf_op jit(solution)/shard_map/ppermute | solution.py:201
  23.8 0.7 %collective-permute-start.13 = (f32[512,512]{1,0:T(8,128)S(1)}, f32[512,512]{1,0:T(8,128)S(1)}, u32[]{:S(2)}, u32[]{:S(2)}) collective-permute-start(f32[512,512]{1,0:T(8,128)S(1)} %get-tuple-element.55.upper), channel_id=1, source_target_pairs={{40,32},{56,48},{104,96},{168,160},{184,176},{232,224},{296,288},{... | collective-permute-start | bytes 3145736 | tf_op jit(solution)/shard_map/ppermute | solution.py:201
  24.6 0.0 collective-permute-done.6.early_a
  24.6 0.0 collective-permute-done.7.early_b
  24.6 0.0 copy-done
  24.6 0.7 %collective-permute-start.8 = (f32[64,512]{1,0:T(8,128)S(1)}, f32[64,512]{1,0:T(8,128)S(1)}, u32[]{:S(2)}, u32[]{:S(2)}) collective-permute-start(f32[64,512]{1,0:T(8,128)S(1)} %get-tuple-element.51), channel_id=1, source_target_pairs={{32,16},{96,80},{160,144},{224,208},{288,272},{352,336},{416,400},... | collective-permute-start | bytes 393224 | tf_op jit(solution)/shard_map/ppermute | solution.py:201
  25.3 0.7 %collective-permute-start.9 = (f32[64,512]{1,0:T(8,128)S(1)}, f32[64,512]{1,0:T(8,128)S(1)}, u32[]{:S(2)}, u32[]{:S(2)}) collective-permute-start(f32[64,512]{1,0:T(8,128)S(1)} %get-tuple-element.52), channel_id=1, source_target_pairs={{32,48},{96,112},{160,176},{224,240},{288,304},{352,368},{416,432}... | collective-permute-start | bytes 393224 | tf_op jit(solution)/shard_map/ppermute | solution.py:201
  26.0 1.3 %collective-permute-start.18 = (f32[512,512]{1,0:T(8,128)S(1)}, f32[512,512]{1,0:T(8,128)S(1)}, u32[]{:S(2)}, u32[]{:S(2)}) collective-permute-start(f32[512,512]{1,0:T(8,128)S(1)} %shard_map.44), channel_id=1, source_target_pairs={{1,0},{5,4},{9,8},{13,12},{17,16},{21,20},{25,24},{29,28},{33,32},... | collective-permute-start | bytes 3145736 | tf_op jit(solution)/shard_map/ppermute | solution.py:201
  27.3 0.0 collective-permute-done.8.c_left
  27.3 0.0 collective-permute-done.9.c_right
  27.4 1.3 %collective-permute-start.10 = (f32[64,512]{1,0:T(8,128)S(1)}, f32[64,512]{1,0:T(8,128)S(1)}, u32[]{:S(2)}, u32[]{:S(2)}) collective-permute-start(f32[64,512]{1,0:T(8,128)S(1)} %get-tuple-element.53), channel_id=1, source_target_pairs={{16,0},{48,32},{80,64},{112,96},{144,128},{176,160},{208,192},{240... | collective-permute-start | bytes 393224 | tf_op jit(solution)/shard_map/ppermute | solution.py:201
  28.7 0.7 %collective-permute-start.11 = (f32[64,512]{1,0:T(8,128)S(1)}, f32[64,512]{1,0:T(8,128)S(1)}, u32[]{:S(2)}, u32[]{:S(2)}) collective-permute-start(f32[64,512]{1,0:T(8,128)S(1)} %get-tuple-element.53), channel_id=1, source_target_pairs={{16,8},{48,40},{80,72},{112,104},{144,136},{176,168},{208,200},{24... | collective-permute-start | bytes 393224 | tf_op jit(solution)/shard_map/ppermute | solution.py:201
  29.3 0.7 %collective-permute-start.12 = (f32[64,512]{1,0:T(8,128)S(1)}, f32[64,512]{1,0:T(8,128)S(1)}, u32[]{:S(2)}, u32[]{:S(2)}) collective-permute-start(f32[64,512]{1,0:T(8,128)S(1)} %get-tuple-element.54.c_own), channel_id=1, source_target_pairs={{16,24},{48,56},{80,88},{112,120},{144,152},{176,184},{208,216},{2... | collective-permute-start | bytes 393224 | tf_op jit(solution)/shard_map/ppermute | solution.py:201
  30.0 11.8 %collective-permute-done.10.c_0 = f32[64,512]{1,0:T(8,128)S(1)} collective-permute-done((f32[64,512]{1,0:T(8,128)S(1)}, f32[64,512]{1,0:T(8,128)S(1)}, u32[]{:S(2)}, u32[]{:S(2)}) %collective-permute-start.10) | collective-permute-done | bytes 131104 | tf_op jit(solution)/shard_map/ppermute | solution.py:201
  41.8 0.0 collective-permute-done.11.c_1
  41.8 0.0 collective-permute-done.12.c_3
  41.8 0.0 collective-permute-done.13.early_c
  41.8 0.5 shard_map.42.here
  42.4 0.0 copy-start.1
  42.4 1.4 %collective-permute-start.14 = (f32[64,512]{1,0:T(8,128)S(1)}, f32[64,512]{1,0:T(8,128)S(1)}, u32[]{:S(2)}, u32[]{:S(2)}) collective-permute-start(f32[64,512]{1,0:T(8,128)S(1)} %shard_map.42.here), channel_id=1, source_target_pairs={{0,4},{8,12},{16,20},{24,28},{32,36},{40,44},{48,52},{56,60},{64,6... | collective-permute-start | bytes 393224 | tf_op jit(solution)/shard_map/ppermute | solution.py:201
  43.8 1.0 %collective-permute-done.14.over = f32[64,512]{1,0:T(8,128)S(1)} collective-permute-done((f32[64,512]{1,0:T(8,128)S(1)}, f32[64,512]{1,0:T(8,128)S(1)}, u32[]{:S(2)}, u32[]{:S(2)}) %collective-permute-start.14) | collective-permute-done | bytes 131104 | tf_op jit(solution)/shard_map/ppermute | solution.py:201
  44.8 0.5 shard_map.43.c2
  45.2 1.3 %collective-permute-start.15 = (f32[64,512]{1,0:T(8,128)S(1)}, f32[64,512]{1,0:T(8,128)S(1)}, u32[]{:S(2)}, u32[]{:S(2)}) collective-permute-start(f32[64,512]{1,0:T(8,128)S(1)} %shard_map.43.c2), channel_id=1, source_target_pairs={{0,1},{4,5},{8,9},{12,13},{16,17},{20,21},{24,25},{28,29},{32,33},... | collective-permute-start | bytes 393224 | tf_op jit(solution)/shard_map/ppermute | solution.py:201
  46.5 1.3 %collective-permute-start.16 = (f32[64,512]{1,0:T(8,128)S(1)}, f32[64,512]{1,0:T(8,128)S(1)}, u32[]{:S(2)}, u32[]{:S(2)}) collective-permute-start(f32[64,512]{1,0:T(8,128)S(1)} %shard_map.43.c2), channel_id=1, source_target_pairs={{0,2},{4,6},{8,10},{12,14},{16,18},{20,22},{24,26},{28,30},{32,34}... | collective-permute-start | bytes 393224 | tf_op jit(solution)/shard_map/ppermute | solution.py:201
  47.8 1.3 %collective-permute-start.17 = (f32[64,512]{1,0:T(8,128)S(1)}, f32[64,512]{1,0:T(8,128)S(1)}, u32[]{:S(2)}, u32[]{:S(2)}) collective-permute-start(f32[64,512]{1,0:T(8,128)S(1)} %shard_map.43.c2), channel_id=1, source_target_pairs={{0,3},{4,7},{8,11},{12,15},{16,19},{20,23},{24,27},{28,31},{32,35}... | collective-permute-start | bytes 393224 | tf_op jit(solution)/shard_map/ppermute | solution.py:201
  49.1 1.3 %collective-permute-done.15.c2_x1 = f32[64,512]{1,0:T(8,128)S(1)} collective-permute-done((f32[64,512]{1,0:T(8,128)S(1)}, f32[64,512]{1,0:T(8,128)S(1)}, u32[]{:S(2)}, u32[]{:S(2)}) %collective-permute-start.15) | collective-permute-done | bytes 131104 | tf_op jit(solution)/shard_map/ppermute | solution.py:201
  50.4 2.5 %collective-permute-done.16.c2_x2 = f32[64,512]{1,0:T(8,128)S(1)} collective-permute-done((f32[64,512]{1,0:T(8,128)S(1)}, f32[64,512]{1,0:T(8,128)S(1)}, u32[]{:S(2)}, u32[]{:S(2)}) %collective-permute-start.16) | collective-permute-done | bytes 131104 | tf_op jit(solution)/shard_map/ppermute | solution.py:201
  52.9 0.0 collective-permute-done.17.c2_x3
  52.9 2.9 %collective-permute-done.18.pair = f32[512,512]{1,0:T(8,128)S(1)} collective-permute-done((f32[512,512]{1,0:T(8,128)S(1)}, f32[512,512]{1,0:T(8,128)S(1)}, u32[]{:S(2)}, u32[]{:S(2)}) %collective-permute-start.18) | collective-permute-done | bytes 1048608 | tf_op jit(solution)/shard_map/ppermute | solution.py:201
  55.8 0.0 copy-done.1
  55.8 1.6 %shard_map.45 = f32[64,512]{1,0:T(8,128)} custom-call(f32[64,512]{1,0:T(8,128)S(1)} %shard_map.43.c2, f32[64,512]{1,0:T(8,128)S(1)} %collective-permute-done.15.c2_x1, f32[64,512]{1,0:T(8,128)S(1)} %collective-permute-done.16.c2_x2, f32[64,512]{1,0:T(8,128)S(1)} %collective-permute-done.17.c2_x3, f32[1024,512]{1,0:T(8,128)S(1)} %copy-done, ...), custom_call_target="tpu_custom_call" | custom-call | tf_op jit(solution)/shard_map/pallas_call | solution.py:50
  (5 shorter events, 0.1 us)
Async XLA Ops:
  0.0 4.2 %copy-start.2 = (f32[512,64]{0,1:T(8,128)S(1)}, f32[512,64]{0,1:T(8,128)}, u32[]{:S(2)}) copy-start(f32[512,64]{0,1:T(8,128)} %param.5) | copy-start | bytes 393220
  1.6 23.0 %collective-permute-start.6 = (f32[512,512]{1,0:T(8,128)S(1)}, f32[512,512]{1,0:T(8,128)S(1)}, u32[]{:S(2)}, u32[]{:S(2)}) collective-permute-start(f32[512,512]{1,0:T(8,128)S(1)} %get-tuple-element.55.upper), channel_id=1, source_target_pairs={{2,1},{3,2},{6,5},{7,6},{10,9},{11,10},{14,13},{15,14},{18,17},{19... | collective-permute-start | bytes 3145736 | tf_op jit(solution)/shard_map/ppermute | solution.py:201
  2.9 21.7 %collective-permute-start.7 = (f32[512,512]{1,0:T(8,128)S(1)}, f32[512,512]{1,0:T(8,128)S(1)}, u32[]{:S(2)}, u32[]{:S(2)}) collective-permute-start(f32[512,512]{1,0:T(8,128)S(1)} %get-tuple-element.32.other), channel_id=1, source_target_pairs={{2,3},{6,7},{10,11},{14,15},{18,19},{22,23},{26,27},{30,31},{34,35... | collective-permute-start | bytes 3145736 | tf_op jit(solution)/shard_map/ppermute | solution.py:201
  4.2 20.4 %copy-start = (f32[1024,512]{1,0:T(8,128)S(1)}, f32[1024,512]{1,0:T(8,128)}, u32[]{:S(2)}) copy-start(f32[1024,512]{1,0:T(8,128)} %own.9) | copy-start | bytes 6291460
  4.3 2.1 %collective-permute-start = (f32[64,512]{1,0:T(8,128)S(1)}, f32[64,512]{1,0:T(8,128)S(1)}, u32[]{:S(2)}, u32[]{:S(2)}) collective-permute-start(f32[64,512]{1,0:T(8,128)S(1)} %get-tuple-element.33), channel_id=1, source_target_pairs={{256,128}} | collective-permute-start | bytes 393224 | tf_op jit(solution)/shard_map/ppermute | solution.py:201
  5.1 6.9 %collective-permute-start.1 = (f32[64,512]{1,0:T(8,128)S(1)}, f32[64,512]{1,0:T(8,128)S(1)}, u32[]{:S(2)}, u32[]{:S(2)}) collective-permute-start(f32[64,512]{1,0:T(8,128)S(1)} %get-tuple-element.34), channel_id=1, source_target_pairs={{256,384}} | collective-permute-start | bytes 393224 | tf_op jit(solution)/shard_map/ppermute | solution.py:201
  12.7 7.2 %collective-permute-start.2 = (f32[64,512]{1,0:T(8,128)S(1)}, f32[64,512]{1,0:T(8,128)S(1)}, u32[]{:S(2)}, u32[]{:S(2)}) collective-permute-start(f32[64,512]{1,0:T(8,128)S(1)} %get-tuple-element.35), channel_id=1, source_target_pairs={{128,160},{384,416}} | collective-permute-start | bytes 393224 | tf_op jit(solution)/shard_map/ppermute | solution.py:201
  14.9 6.3 %collective-permute-start.3 = (f32[64,512]{1,0:T(8,128)S(1)}, f32[64,512]{1,0:T(8,128)S(1)}, u32[]{:S(2)}, u32[]{:S(2)}) collective-permute-start(f32[64,512]{1,0:T(8,128)S(1)} %get-tuple-element.36), channel_id=1, source_target_pairs={{128,32},{384,288}} | collective-permute-start | bytes 393224 | tf_op jit(solution)/shard_map/ppermute | solution.py:201
  16.2 6.2 %collective-permute-start.4 = (f32[64,512]{1,0:T(8,128)S(1)}, f32[64,512]{1,0:T(8,128)S(1)}, u32[]{:S(2)}, u32[]{:S(2)}) collective-permute-start(f32[64,512]{1,0:T(8,128)S(1)} %get-tuple-element.37), channel_id=1, source_target_pairs={{128,224},{384,480}} | collective-permute-start | bytes 393224 | tf_op jit(solution)/shard_map/ppermute | solution.py:201
  19.9 3.9 %collective-permute-start.5 = (f32[64,512]{1,0:T(8,128)S(1)}, f32[64,512]{1,0:T(8,128)S(1)}, u32[]{:S(2)}, u32[]{:S(2)}) collective-permute-start(f32[64,512]{1,0:T(8,128)S(1)} %get-tuple-element.38), channel_id=1, source_target_pairs={{128,96},{384,352}} | collective-permute-start | bytes 393224 | tf_op jit(solution)/shard_map/ppermute | solution.py:201
  23.8 18.0 %collective-permute-start.13 = (f32[512,512]{1,0:T(8,128)S(1)}, f32[512,512]{1,0:T(8,128)S(1)}, u32[]{:S(2)}, u32[]{:S(2)}) collective-permute-start(f32[512,512]{1,0:T(8,128)S(1)} %get-tuple-element.55.upper), channel_id=1, source_target_pairs={{40,32},{56,48},{104,96},{168,160},{184,176},{232,224},{296,288},{... | collective-permute-start | bytes 3145736 | tf_op jit(solution)/shard_map/ppermute | solution.py:201
  24.6 2.7 %collective-permute-start.8 = (f32[64,512]{1,0:T(8,128)S(1)}, f32[64,512]{1,0:T(8,128)S(1)}, u32[]{:S(2)}, u32[]{:S(2)}) collective-permute-start(f32[64,512]{1,0:T(8,128)S(1)} %get-tuple-element.51), channel_id=1, source_target_pairs={{32,16},{96,80},{160,144},{224,208},{288,272},{352,336},{416,400},... | collective-permute-start | bytes 393224 | tf_op jit(solution)/shard_map/ppermute | solution.py:201
  25.3 2.0 %collective-permute-start.9 = (f32[64,512]{1,0:T(8,128)S(1)}, f32[64,512]{1,0:T(8,128)S(1)}, u32[]{:S(2)}, u32[]{:S(2)}) collective-permute-start(f32[64,512]{1,0:T(8,128)S(1)} %get-tuple-element.52), channel_id=1, source_target_pairs={{32,48},{96,112},{160,176},{224,240},{288,304},{352,368},{416,432}... | collective-permute-start | bytes 393224 | tf_op jit(solution)/shard_map/ppermute | solution.py:201
  26.0 29.8 %collective-permute-start.18 = (f32[512,512]{1,0:T(8,128)S(1)}, f32[512,512]{1,0:T(8,128)S(1)}, u32[]{:S(2)}, u32[]{:S(2)}) collective-permute-start(f32[512,512]{1,0:T(8,128)S(1)} %shard_map.44), channel_id=1, source_target_pairs={{1,0},{5,4},{9,8},{13,12},{17,16},{21,20},{25,24},{29,28},{33,32},... | collective-permute-start | bytes 3145736 | tf_op jit(solution)/shard_map/ppermute | solution.py:201
  27.4 14.5 %collective-permute-start.10 = (f32[64,512]{1,0:T(8,128)S(1)}, f32[64,512]{1,0:T(8,128)S(1)}, u32[]{:S(2)}, u32[]{:S(2)}) collective-permute-start(f32[64,512]{1,0:T(8,128)S(1)} %get-tuple-element.53), channel_id=1, source_target_pairs={{16,0},{48,32},{80,64},{112,96},{144,128},{176,160},{208,192},{240... | collective-permute-start | bytes 393224 | tf_op jit(solution)/shard_map/ppermute | solution.py:201
  28.7 13.2 %collective-permute-start.11 = (f32[64,512]{1,0:T(8,128)S(1)}, f32[64,512]{1,0:T(8,128)S(1)}, u32[]{:S(2)}, u32[]{:S(2)}) collective-permute-start(f32[64,512]{1,0:T(8,128)S(1)} %get-tuple-element.53), channel_id=1, source_target_pairs={{16,8},{48,40},{80,72},{112,104},{144,136},{176,168},{208,200},{24... | collective-permute-start | bytes 393224 | tf_op jit(solution)/shard_map/ppermute | solution.py:201
  29.3 12.5 %collective-permute-start.12 = (f32[64,512]{1,0:T(8,128)S(1)}, f32[64,512]{1,0:T(8,128)S(1)}, u32[]{:S(2)}, u32[]{:S(2)}) collective-permute-start(f32[64,512]{1,0:T(8,128)S(1)} %get-tuple-element.54.c_own), channel_id=1, source_target_pairs={{16,24},{48,56},{80,88},{112,120},{144,152},{176,184},{208,216},{2... | collective-permute-start | bytes 393224 | tf_op jit(solution)/shard_map/ppermute | solution.py:201
  42.4 13.4 %copy-start.1 = (f32[512,512]{1,0:T(8,128)S(1)}, f32[512,512]{1,0:T(8,128)}, u32[]{:S(2)}) copy-start(f32[512,512]{1,0:T(8,128)} %leaf.1) | copy-start | bytes 3145732
  42.4 2.4 %collective-permute-start.14 = (f32[64,512]{1,0:T(8,128)S(1)}, f32[64,512]{1,0:T(8,128)S(1)}, u32[]{:S(2)}, u32[]{:S(2)}) collective-permute-start(f32[64,512]{1,0:T(8,128)S(1)} %shard_map.42.here), channel_id=1, source_target_pairs={{0,4},{8,12},{16,20},{24,28},{32,36},{40,44},{48,52},{56,60},{64,6... | collective-permute-start | bytes 393224 | tf_op jit(solution)/shard_map/ppermute | solution.py:201
  45.2 5.2 %collective-permute-start.15 = (f32[64,512]{1,0:T(8,128)S(1)}, f32[64,512]{1,0:T(8,128)S(1)}, u32[]{:S(2)}, u32[]{:S(2)}) collective-permute-start(f32[64,512]{1,0:T(8,128)S(1)} %shard_map.43.c2), channel_id=1, source_target_pairs={{0,1},{4,5},{8,9},{12,13},{16,17},{20,21},{24,25},{28,29},{32,33},... | collective-permute-start | bytes 393224 | tf_op jit(solution)/shard_map/ppermute | solution.py:201
  46.5 6.4 %collective-permute-start.16 = (f32[64,512]{1,0:T(8,128)S(1)}, f32[64,512]{1,0:T(8,128)S(1)}, u32[]{:S(2)}, u32[]{:S(2)}) collective-permute-start(f32[64,512]{1,0:T(8,128)S(1)} %shard_map.43.c2), channel_id=1, source_target_pairs={{0,2},{4,6},{8,10},{12,14},{16,18},{20,22},{24,26},{28,30},{32,34}... | collective-permute-start | bytes 393224 | tf_op jit(solution)/shard_map/ppermute | solution.py:201
  47.8 5.1 %collective-permute-start.17 = (f32[64,512]{1,0:T(8,128)S(1)}, f32[64,512]{1,0:T(8,128)S(1)}, u32[]{:S(2)}, u32[]{:S(2)}) collective-permute-start(f32[64,512]{1,0:T(8,128)S(1)} %shard_map.43.c2), channel_id=1, source_target_pairs={{0,3},{4,7},{8,11},{12,15},{16,19},{20,23},{24,27},{28,31},{32,35}... | collective-permute-start | bytes 393224 | tf_op jit(solution)/shard_map/ppermute | solution.py:201
